TPU v7x, 32 devices: a whole 2x2x4 slice. The times are simulated.
32 devices in a mesh: dp: 8 (over z, y), blk: 4 (over x, core).
Axes of the slice: x: 2, y: 2, z: 4, core: 2. Of those that a mesh axis runs over, the one named last changes fastest.
Arguments:
- tokens: bfloat16 [8, 1024, 768], P('dp', 'blk'), may hold values from -6 to 6
- lengths: int32 [8, 5], P('dp'), may hold values from 40 to 197, as said below
- w_qkv: bfloat16 [768, 2304], replicated, may hold values from -0.3125 to 0.3125
- w_out: bfloat16 [768, 768], replicated, may hold values from -0.4375 to 0.4375
- w_up: bfloat16 [768, 3072], replicated, may hold values from -0.21875 to 0.21875
- w_down: bfloat16 [3072, 768], replicated, may hold values from -0.15625 to 0.15625
- vectors: float32 [10752], replicated, may hold values from -0.3 to 2.5
- cotangent: bfloat16 [8, 1024, 768], P('dp', 'blk'), may hold values from -6 to 6
Outputs:
- out: bfloat16 [8, 1024, 768], P('dp', 'blk')
- grad_tokens: bfloat16 [8, 1024, 768], P('dp', 'blk')
- grad_w_qkv: float32 [768, 2304], P('blk', 'dp')
- grad_w_out: float32 [768, 768], P('blk', 'dp')
- grad_w_up: float32 [768, 3072], P('blk', 'dp')
- grad_w_down: float32 [3072, 768], P('blk', 'dp')
- grad_vectors: float32 [10752], P(('dp', 'blk'))
Inputs may be any that keep to these rules, and one draw needn't show every extreme that they name: `lengths`: images fill a set's packing places in order from place 0 and padding fills the rest; in every set one image has exactly 197 visible patches and each other image 40 to 197.
All inputs are finite; a program needn't handle non-finite values.
Results may differ from a plain program's by a relative error of at most 0.022.
Values may be sent and summed in bfloat16 or wider, within the bound.
No kernel may reach another device: no remote copies, remote signals or barrier semaphores. Data moves between devices by JAX's collectives and lax.ppermute only.
A program may use at most 128 MiB of HBM per device.

v0:
```python
import functools
import math

import jax
import jax.numpy as jnp
import numpy as np
from jax import lax
from jax.experimental import pallas as pl
from jax.experimental.pallas import tpu as pltpu
from jax.sharding import PartitionSpec as P

H = 12
HEAD_SIZE = 64
TILE = 64


EPSILON = 1e-06
FLOOR_SCORE = -1e30


def passed_along(array, axis, by):
    length = lax.axis_size(axis)
    return lax.ppermute(array, axis, [(i, (i + by) % length) for i in range(length)])


def norm_rows(values, gain, shift):
    centre = jnp.mean(values, axis=-1, keepdims=True)
    centred = values - centre
    spread = jnp.mean(centred * centred, axis=-1, keepdims=True)
    return centred * lax.rsqrt(spread + EPSILON) * gain + shift


def exact_gelu(values):
    return jax.nn.gelu(values, approximate=False)


def segment_of(rows_index, rows, parts, ends):
    place = rows_index % rows * parts + rows_index // rows
    return jnp.sum((place[:, None] >= ends[None, :]).astype(jnp.int32), axis=1)


def contract_rows(left, right):
    return lax.dot_general(
        left, right, (((0,), (0,)), ((), ())), preferred_element_type=jnp.float32
    )


def contract_cols(left, right):
    return lax.dot_general(
        left, right, (((1,), (1,)), ((), ())), preferred_element_type=jnp.float32
    )


def attend_block(query, query_item, keys, values, key_item, scale, carry):
    best, total, weighted = carry
    count = keys.shape[0]
    heads = query.shape[1]
    key_heads = keys.reshape(count, heads, -1)
    value_heads = values.reshape(count, heads, -1)
    allowed = (query_item[:, None] == key_item[None, :])[None]
    score = jnp.einsum("qhd,khd->hqk", query, key_heads, preferred_element_type=jnp.float32) * scale
    score = jnp.where(allowed, score, FLOOR_SCORE)
    newbest = jnp.maximum(best, jnp.max(score, axis=-1))
    weight = jnp.where(allowed, jnp.exp(score - newbest[..., None]), 0.0)
    factor = jnp.exp(best - newbest)
    total = total * factor + jnp.sum(weight, axis=-1)
    weighted = weighted * factor[..., None] + jnp.einsum(
        "hqk,khd->hqd", weight.astype(jnp.bfloat16), value_heads, preferred_element_type=jnp.float32
    )
    return (newbest, total, weighted)


def grad_block(query, d_out, logsum, delta, query_item, keys, values, key_item, scale):
    count = keys.shape[0]
    heads = query.shape[1]
    key_heads = keys.reshape(count, heads, -1)
    value_heads = values.reshape(count, heads, -1)
    allowed = (query_item[:, None] == key_item[None, :])[None]
    score = jnp.einsum("qhd,khd->hqk", query, key_heads, preferred_element_type=jnp.float32) * scale
    prob = jnp.where(allowed, jnp.exp(score - logsum[..., None]), 0.0)
    d_prob = jnp.einsum("qhd,khd->hqk", d_out, value_heads, preferred_element_type=jnp.float32)
    d_score = (prob * (d_prob - delta[..., None])).astype(jnp.bfloat16)
    d_query = (
        jnp.einsum("hqk,khd->qhd", d_score, key_heads, preferred_element_type=jnp.float32) * scale
    )
    d_keys = jnp.einsum("hqk,qhd->khd", d_score, query, preferred_element_type=jnp.float32) * scale
    d_values = jnp.einsum(
        "hqk,qhd->khd", prob.astype(jnp.bfloat16), d_out, preferred_element_type=jnp.float32
    )
    return (d_query, d_keys.reshape(count, -1), d_values.reshape(count, -1))


def on_device(tokens, lengths, w_qkv, w_out, w_up, w_down, vectors, cotangent):
    inputs = tokens[0].astype(jnp.float32)
    rows, width = inputs.shape
    heads = H
    head_size = width // heads
    scale = head_size ** (-0.5)
    items = lengths.shape[1]
    ends = jnp.cumsum(lengths[0])
    parts = lax.axis_size("blk")
    position = lax.axis_index("blk")
    query_item = segment_of(position * rows + lax.iota(jnp.int32, rows), rows, parts, ends)
    valid = (query_item < items).astype(jnp.float32)[:, None]
    pieces = [vectors[index * width : (index + 1) * width] for index in range(10)]
    (
        gain_one,
        shift_one,
        bias_q,
        bias_v,
        bias_o,
        scale_one,
        gain_two,
        shift_two,
        bias_d,
        scale_two,
    ) = pieces
    bias_up = vectors[10 * width :]
    normed, norm_one_pull = jax.vjp(norm_rows, inputs, gain_one, shift_one)
    normed_low = normed.astype(jnp.bfloat16)
    qkv_bias = jnp.concatenate([bias_q, jnp.zeros_like(bias_q), bias_v])
    projected = (jnp.dot(normed_low, w_qkv, preferred_element_type=jnp.float32) + qkv_bias).astype(
        jnp.bfloat16
    )
    query = projected[:, :width].reshape(rows, heads, head_size)
    keys = projected[:, width : 2 * width]
    values = projected[:, 2 * width :]
    start_state = (
        jnp.full((heads, rows), FLOOR_SCORE, jnp.float32),
        jnp.zeros((heads, rows), jnp.float32),
        jnp.zeros((heads, rows, head_size), jnp.float32),
    )
    carry = start_state
    piece = (
        lax.all_gather(keys, "blk", axis=0, tiled=True),
        lax.all_gather(values, "blk", axis=0, tiled=True),
    )
    count = piece[0].shape[0]
    size = math.gcd(count, 512)
    steps = count // size
    key_blocks = piece[0].reshape(steps, size, width)
    value_blocks = piece[1].reshape(steps, size, width)

    def inner(state, item):
        block_keys, block_values, offset = item
        key_item = segment_of(offset + lax.iota(jnp.int32, size), rows, parts, ends)
        return (
            attend_block(query, query_item, block_keys, block_values, key_item, scale, state),
            None,
        )

    carry, unused = lax.scan(
        inner, carry, (key_blocks, value_blocks, lax.iota(jnp.int32, steps) * size)
    )
    best, total, weighted = carry
    logsum = best + jnp.log(total)
    attended = (weighted / total[..., None]).transpose(1, 0, 2).reshape(rows, width)
    attended_low = attended.astype(jnp.bfloat16)
    branch = jnp.dot(attended_low, w_out, preferred_element_type=jnp.float32) + bias_o
    mid = inputs + scale_one * branch
    normed_two, norm_two_pull = jax.vjp(norm_rows, mid, gain_two, shift_two)
    normed_two_low = normed_two.astype(jnp.bfloat16)
    before = jnp.dot(normed_two_low, w_up, preferred_element_type=jnp.float32) + bias_up
    activated, gelu_pull = jax.vjp(exact_gelu, before)
    activated_low = activated.astype(jnp.bfloat16)
    feed = jnp.dot(activated_low, w_down, preferred_element_type=jnp.float32) + bias_d
    result = mid + scale_two * feed
    out = (result * valid).astype(jnp.bfloat16)
    d_result = cotangent[0].astype(jnp.float32) * valid
    d_feed = (scale_two * d_result).astype(jnp.bfloat16)
    g_scale_two = jnp.sum(d_result * feed, axis=0)
    g_bias_d = jnp.sum(d_feed.astype(jnp.float32), axis=0)
    g_w_down = contract_rows(activated_low, d_feed)
    d_activated = contract_cols(d_feed, w_down)
    d_before = gelu_pull(d_activated)[0].astype(jnp.bfloat16)
    g_bias_up = jnp.sum(d_before.astype(jnp.float32), axis=0)
    g_w_up = contract_rows(normed_two_low, d_before)
    d_normed_two = contract_cols(d_before, w_up)
    d_mid_norm, g_gain_two, g_shift_two = norm_two_pull(d_normed_two)
    d_mid = d_result + d_mid_norm
    d_branch = (scale_one * d_mid).astype(jnp.bfloat16)
    g_scale_one = jnp.sum(d_mid * branch, axis=0)
    g_bias_o = jnp.sum(d_branch.astype(jnp.float32), axis=0)
    g_w_out = contract_rows(attended_low, d_branch)
    d_attended = contract_cols(d_branch, w_out).astype(jnp.bfloat16)
    d_heads = d_attended.reshape(rows, heads, head_size)
    delta = jnp.sum(
        (d_attended.astype(jnp.float32) * attended).reshape(rows, heads, head_size), axis=-1
    ).T
    zero_query = jnp.zeros((rows, heads, head_size), jnp.float32)

    def visit_block(block_keys, block_values, owner):
        key_item = segment_of(owner * rows + lax.iota(jnp.int32, rows), rows, parts, ends)
        return grad_block(
            query, d_heads, logsum, delta, query_item, block_keys, block_values, key_item, scale
        )

    def send_back(d_keys, d_values):
        return (
            passed_along(d_keys.astype(jnp.bfloat16), "blk", 1).astype(d_keys.dtype),
            passed_along(d_values.astype(jnp.bfloat16), "blk", 1).astype(d_values.dtype),
        )

    def accumulate(state, owner):
        d_query, block_keys, block_values, d_keys, d_values = state
        dq_part, dk_part, dv_part = visit_block(block_keys, block_values, owner)
        d_keys, d_values = send_back(d_keys + dk_part, d_values + dv_part)
        return (d_query + dq_part, d_keys, d_values)

    def turn(step, state):
        owner = (position - step) % parts
        d_query, d_keys, d_values = accumulate(state, owner)
        block_keys, block_values = passed_along((state[1], state[2]), "blk", 1)
        return (d_query, block_keys, block_values, d_keys, d_values)

    zero_rows = jnp.zeros((rows, width), jnp.float32)
    state = lax.fori_loop(0, parts - 1, turn, (zero_query, keys, values, zero_rows, zero_rows))
    d_query, d_keys, d_values = accumulate(state, (position + 1) % parts)
    d_projected = jnp.concatenate([d_query.reshape(rows, width), d_keys, d_values], axis=1).astype(
        jnp.bfloat16
    )
    g_bias_q = jnp.sum(d_projected[:, :width].astype(jnp.float32), axis=0)
    g_bias_v = jnp.sum(d_projected[:, 2 * width :].astype(jnp.float32), axis=0)
    g_w_qkv = contract_rows(normed_low, d_projected)
    d_normed = contract_cols(d_projected, w_qkv)
    d_input_norm, g_gain_one, g_shift_one = norm_one_pull(d_normed)
    d_inputs = d_mid + d_input_norm
    g_vectors = jnp.concatenate(
        [
            g_gain_one,
            g_shift_one,
            g_bias_q,
            g_bias_v,
            g_bias_o,
            g_scale_one,
            g_gain_two,
            g_shift_two,
            g_bias_d,
            g_scale_two,
            g_bias_up,
        ]
    )
    column_sums = (
        lax.psum_scatter(
            g_w_qkv.astype(jnp.bfloat16), "dp", scatter_dimension=1, tiled=True
        ).astype(jnp.float32),
        lax.psum_scatter(
            g_w_out.astype(jnp.bfloat16), "dp", scatter_dimension=1, tiled=True
        ).astype(jnp.float32),
        lax.psum_scatter(g_w_up.astype(jnp.bfloat16), "dp", scatter_dimension=1, tiled=True).astype(
            jnp.float32
        ),
        lax.psum_scatter(
            g_w_down.astype(jnp.bfloat16), "dp", scatter_dimension=1, tiled=True
        ).astype(jnp.float32),
        lax.psum_scatter(
            g_vectors.astype(jnp.bfloat16), "dp", scatter_dimension=0, tiled=True
        ).astype(jnp.float32),
    )
    g_w_qkv, g_w_out, g_w_up, g_w_down, g_vectors = (
        lax.psum_scatter(
            column_sums[0].astype(jnp.bfloat16), "blk", scatter_dimension=0, tiled=True
        ).astype(jnp.float32),
        lax.psum_scatter(
            column_sums[1].astype(jnp.bfloat16), "blk", scatter_dimension=0, tiled=True
        ).astype(jnp.float32),
        lax.psum_scatter(
            column_sums[2].astype(jnp.bfloat16), "blk", scatter_dimension=0, tiled=True
        ).astype(jnp.float32),
        lax.psum_scatter(
            column_sums[3].astype(jnp.bfloat16), "blk", scatter_dimension=0, tiled=True
        ).astype(jnp.float32),
        lax.psum_scatter(
            column_sums[4].astype(jnp.bfloat16), "blk", scatter_dimension=0, tiled=True
        ).astype(jnp.float32),
    )
    return (
        out[None],
        d_inputs.astype(jnp.bfloat16)[None],
        g_w_qkv,
        g_w_out,
        g_w_up,
        g_w_down,
        g_vectors,
    )


BF = jnp.bfloat16
F32 = jnp.float32
MASKED = -1e30
GRANT = 60 * 1024 * 1024
STEP_GRANT = 20 * 1024 * 1024
WIDE_CHUNK = 128


def unit_tables():
    lists, places = np.zeros((2, 2, 2, 6), np.int32), np.zeros((2, 2, 4, 3), np.int32)
    units = {core: [unit for unit in range(24) if unit // 4 % 2 == core] for core in range(2)}
    for y in range(2):
        for low_z in range(2):
            first = {}
            for core in range(2):
                own = [unit for unit in units[core] if unit // 3 % 2 == y]
                first[core] = [unit for unit in own if unit // 6 % 2 == low_z]
                rest = [unit for unit in own if unit // 6 % 2 != low_z]
                lists[core, y, low_z] = [units[core].index(unit) for unit in first[core] + rest]
            for core in range(2):
                held = first[core] + first[1 - core]
                for z in (low_z, low_z + 2):
                    places[core, y, z] = [held.index(3 * (2 * z + y) + index) for index in range(3)]
    return np.concatenate([lists.reshape(-1), places.reshape(-1)])


UNIT_TABLE = unit_tables()
UNIT_LIST = 4
ENDS = UNIT_LIST + UNIT_TABLE.size


def dot_nn(left, right):
    return lax.dot_general(left, right, (((1,), (0,)), ((), ())), preferred_element_type=F32)


def dot_nt(left, right):
    return lax.dot_general(left, right, (((1,), (1,)), ((), ())), preferred_element_type=F32)


def dot_tn(left, right):
    return lax.dot_general(left, right, (((0,), (0,)), ((), ())), preferred_element_type=F32)


def standardise(values):
    centred = values - jnp.mean(values, axis=-1, keepdims=True)
    inverse = lax.rsqrt(jnp.mean(centred * centred, axis=-1, keepdims=True) + EPSILON)
    return centred * inverse, inverse


def standardise_grad(grad, xhat, inverse):
    first = jnp.mean(grad, axis=-1, keepdims=True)
    second = jnp.mean(grad * xhat, axis=-1, keepdims=True)
    return (grad - first - xhat * second) * inverse


def column_sum(values):
    return jnp.sum(values, axis=0, keepdims=True)


def item_at(place, where_ref, items):
    found = jnp.zeros_like(place)
    for index in range(items):
        found = found + (place >= where_ref[ENDS + index]).astype(jnp.int32)
    return found


def own_block(where_ref, rel_x, rel_c):
    return 2 * (where_ref[0] ^ rel_x) + (where_ref[1] ^ rel_c)


def low(*shape):
    return jax.ShapeDtypeStruct(shape, BF)


def full(*shape):
    return jax.ShapeDtypeStruct(shape, F32)


def lanes_at(index, size):
    return pl.ds(pl.multiple_of(index * size, size), size)


class Stage:
    def __init__(self, reads, places, writes):
        self.reads, self.places, self.writes = reads, places, writes
        self.started, self.waited, self.begun = set(), set(), []

    def start(self, *indices):
        for index in indices:
            if index not in self.started:
                self.started.add(index)
                for copy in self.reads[index]:
                    copy.start()

    def __getitem__(self, index):
        self.start(index)
        if index not in self.waited:
            self.waited.add(index)
            for copy in self.reads[index]:
                copy.wait()
        return self.places[index]

    def out(self, index):
        return self.writes[index][0]

    def put(self, *indices):
        for index in indices:
            self.writes[index][1].start()
            self.begun.append(index)

    def finish(self):
        for index in range(len(self.reads)):
            self[index]
        self.put(*(index for index in range(len(self.writes)) if index not in self.begun))
        for place, copy in self.writes:
            copy.wait()


class Place:
    def __init__(self, lengths_ref, table_ref):
        position, turn = lax.axis_index("blk"), lax.axis_index("dp")
        self.four = (position // 2, position % 2, turn // 2, turn % 2)
        self.table_ref = table_ref
        self.ends, end = [], jnp.int32(0)
        for index in range(lengths_ref.shape[1]):
            end = end + lengths_ref[0, index]
            self.ends.append(end)

    def __getitem__(self, index):
        if isinstance(index, int) and index < UNIT_LIST:
            return self.four[index]
        if isinstance(index, int) and index >= ENDS:
            return self.ends[index - ENDS]
        return self.table_ref[index - UNIT_LIST]


def unpack_rows(raw_ref, vec_ref):
    count = vec_ref.shape[1] // 128
    for row in range(vec_ref.shape[0]):
        for part in range(count):
            vec_ref[row : row + 1, part * 128 : (part + 1) * 128] = raw_ref[row * count + part : row * count + part + 1]


def staged_call(body, where, operands, out_shape, cuts=None, scratch=(), late=(), pairs=(), tables=False, grant=GRANT):
    cuts = cuts or {}
    count, results = len(operands), len(out_shape)
    shapes, parts = [], []
    for index, operand in enumerate(operands):
        shape, pieces = (operand.shape, 1) if index not in cuts else cuts[index][:2]
        shapes.append(pltpu.VMEM(shape, operand.dtype))
        parts.append(pieces)
    held_shapes, held_at = [], {}
    for index, item in enumerate(out_shape):
        if index - 1 in pairs:
            held_at[index] = (len(held_shapes) - 1, 1)
        elif index in pairs:
            held_at[index] = (len(held_shapes), 0)
            held_shapes.append(pltpu.VMEM((2, *item.shape), item.dtype))
        else:
            held_at[index] = (len(held_shapes), None)
            held_shapes.append(pltpu.VMEM(item.shape, item.dtype))

    def kernel(*refs):
        where_ref = Place(refs[0], refs[1] if tables else None)
        refs = refs[2 if tables else 1 :]
        ins, outs = refs[:count], refs[count : count + results]
        places = refs[count + results : 2 * count + results]
        held = refs[2 * count + results : 2 * count + results + len(held_shapes)]
        read_sem, write_sem, *rest = refs[2 * count + results + len(held_shapes) :]
        reads, used = [], 0
        for index in range(count):
            moves = [(ins[index], places[index])] if index not in cuts else cuts[index][2](where_ref, ins[index], places[index])
            reads.append([])
            for source, target in moves:
                reads[-1].append(pltpu.make_async_copy(source, target, read_sem.at[used]))
                used += 1
        writes = []
        for index in range(results):
            place, entry = held_at[index]
            source = held[place] if entry is None else held[place].at[entry]
            writes.append((held[place], pltpu.make_async_copy(source, outs[index], write_sem.at[index])))
        stage = Stage(reads, places, writes)
        stage.start(*(index for index in range(count) if index not in late))
        body(where_ref, stage, *rest)
        stage.finish()

    return pl.pallas_call(
        kernel,
        in_specs=[pl.BlockSpec(memory_space=pltpu.SMEM)] * (2 if tables else 1)
        + [pl.BlockSpec(memory_space=pl.ANY)] * count,
        out_specs=[pl.BlockSpec(memory_space=pl.ANY)] * results,
        out_shape=out_shape,
        scratch_shapes=shapes
        + held_shapes
        + [pltpu.SemaphoreType.DMA((sum(parts),)), pltpu.SemaphoreType.DMA((results,))]
        + list(scratch),
        compiler_params=pltpu.CompilerParams(vmem_limit_bytes=grant),
    )(where, *((UNIT_TABLE,) if tables else ()), *operands)


def each(count, body):
    def step(index, carry):
        body(index)
        return carry

    lax.fori_loop(0, count, step, 0)


def hidden_unit(where_ref, rel_x, side):
    return 4 * (where_ref[0] ^ rel_x) + 2 * where_ref[1] + side


def lanes_below(shape, count):
    return lax.broadcasted_iota(jnp.int32, shape, 1) < count


def stack_heads(pair):
    first = lanes_below(pair.shape, HEAD_SIZE)
    zero = jnp.zeros_like(pair)
    return jnp.concatenate([jnp.where(first, pair, zero), jnp.where(first, zero, pair)], axis=0)


def turn(source, target):
    each(source.shape[1] // 128, lambda index: target.__setitem__(lanes_at(index, 128), source[:, lanes_at(index, 128)].T))


def valid_at(where_ref, rel_c, first, count, parts, items):
    row = first + lax.broadcasted_iota(jnp.int32, (count, 1), 0)
    item = item_at(row * parts + own_block(where_ref, 0, rel_c), where_ref, items)
    return (item < items).astype(F32)


def normed_rows(xhat, vec_ref, first):
    return (xhat.astype(F32) * vec_ref[first : first + 1] + vec_ref[first + 1 : first + 2]).astype(BF)


def prepare_kernel(parts, items, where_ref, stage, vec_ref, held, normed_ref, row_ref):
    unpack_rows(stage[2], vec_ref)
    own_ref, sib_ref = stage[0], stage[1]
    stage.start(3, 4, 5, 6)
    xhat_ref, qkv_ref, dact_ref, turned_ref, sum_ref = (stage.out(index) for index in range(5))
    rows, width = own_ref.shape
    half = width // 2
    core = where_ref[1]
    for rel_c, ref in enumerate((own_ref, sib_ref)):

        def norm(index, rel_c=rel_c, ref=ref):
            xhat, unused = standardise(ref[lanes_at(index, WIDE_CHUNK)].astype(F32))
            to = lanes_at(index + rel_c * (rows // WIDE_CHUNK), WIDE_CHUNK)
            xhat_ref[to] = xhat.astype(BF)
            normed_ref[to] = (xhat * vec_ref[0:1] + vec_ref[1:2]).astype(BF)

        each(rows // WIDE_CHUNK, norm)
    stage.put(0)
    sum_ref[...] = jnp.zeros_like(sum_ref)
    for rel_c in range(2):

        def grad(index, rel_c=rel_c, ref=stage[4 + rel_c]):
            valid = valid_at(where_ref, rel_c, index * WIDE_CHUNK, WIDE_CHUNK, parts, items)
            part = (vec_ref[9:10] * (ref[lanes_at(index, WIDE_CHUNK)].astype(F32) * valid)).astype(BF)
            held[lanes_at(index + rel_c * (rows // WIDE_CHUNK), WIDE_CHUNK)] = part
            if rel_c == 0:
                sum_ref[...] += column_sum(part.astype(F32))

        each(rows // WIDE_CHUNK, grad)
    turn(held, turned_ref)
    stage.put(3, 4)
    row_ref[0:1, :half] = vec_ref[2:3, lanes_at(core, half)]
    row_ref[0:1, half : 2 * half] = jnp.zeros((1, half), F32)
    row_ref[0:1, 2 * half :] = vec_ref[3:4, lanes_at(core, half)]
    row_ref[1:2, :half] = jnp.full((1, half), HEAD_SIZE ** (-0.5), F32)
    row_ref[1:2, half:] = jnp.ones((1, 2 * half), F32)
    weight_ref = stage[3]

    def project(index):
        lanes = lanes_at(index, half)
        part = dot_nn(normed_ref[...], weight_ref[:, lanes]) + row_ref[0:1, lanes]
        qkv_ref[:, lanes] = (part.astype(BF).astype(F32) * row_ref[1:2, lanes]).astype(BF)

    each(3, project)
    stage.put(1)
    down_ref = stage[6]
    piece = dact_ref.shape[1] // 4

    def back(index):
        dact_ref[:, lanes_at(index, piece)] = dot_nt(held[...], down_ref[lanes_at(index, piece)]).astype(BF)

    each(4, back)


def item_of_place(where_ref, place, items):
    found = jnp.int32(0)
    for index in range(items):
        found = found + (place >= where_ref[ENDS + index]).astype(jnp.int32)
    return found


def tiles_meet(where_ref, one, other, parts, items):
    span = TILE * parts
    first, last = min(one, other), max(one, other)
    return item_of_place(where_ref, first * span + span - 1, items) >= item_of_place(
        where_ref, last * span, items
    )


def near_tiles(tile, tiles):
    return max(0, tile - 1), min(tiles, tile + 2)


def far_pairs(tiles):
    return [(one, other) for one in range(tiles) for other in range(tiles) if abs(one - other) > 1]


def any_far(where_ref, tiles, parts, items):
    found = jnp.bool_(False)
    for one, other in far_pairs(tiles):
        if one < other:
            found = found | tiles_meet(where_ref, one, other, parts, items)
    return found


def attend_kernel(parts, items, where_ref, stage, vec_ref, wide_ref, normed_ref, asks_ref):
    unpack_rows(stage[2], vec_ref)
    xhat_ref, kv_ref, attended_ref, logsum_ref = (stage.out(index) for index in range(4))
    far_a_ref, far_b_ref = stage[0], stage[1]
    stage.start(3, 4)
    rows, width = far_a_ref.shape
    tiles = rows // TILE
    span = parts * TILE
    both = 2 * HEAD_SIZE
    half = width // 2
    core = where_ref[1]
    for rel_c, ref in enumerate((far_a_ref, far_b_ref)):
        xhat, unused = standardise(ref[...].astype(F32))
        xhat_ref[rel_c * rows : (rel_c + 1) * rows] = xhat.astype(BF)
        normed_ref[rel_c * rows : (rel_c + 1) * rows] = normed_rows(xhat, vec_ref, 0)
    stage.put(0)
    row = lax.broadcasted_iota(jnp.int32, (2 * TILE, 2 * TILE), 0)
    block = 2 * where_ref[0] + (where_ref[1] ^ (row // TILE))
    for tile in range(tiles):
        asks_ref[tile] = item_at((tile * TILE + row % TILE) * parts + block, where_ref, items)
    lane = lax.broadcasted_iota(jnp.int32, (1, span), 1)
    slot = lane // TILE
    block = 2 * (where_ref[0] ^ (slot // 2)) + (where_ref[1] ^ (slot % 2))
    key_item = [item_at((tile * TILE + lane % TILE) * parts + block, where_ref, items) for tile in range(tiles)]
    weight_ref = stage[3]
    row_ref = jnp.concatenate([jnp.zeros((1, half), F32), vec_ref[3:4, lanes_at(core, half)]], axis=1)
    far_kv = (dot_nn(normed_ref[...], weight_ref[...]) + row_ref).astype(BF)
    qkv_ref = stage[4]
    for tile in range(tiles):
        for slot in range(2):
            at = slice(slot * rows + tile * TILE, slot * rows + (tile + 1) * TILE)
            kv_ref[tile * span + slot * TILE : tile * span + (slot + 1) * TILE] = qkv_ref[at, half:]
            kv_ref[tile * span + (slot + 2) * TILE : tile * span + (slot + 3) * TILE] = far_kv[at]
    stage.put(1)
    for index in range(half // both):
        wide_ref[:, 2 * index * both : (2 * index + 1) * both] = kv_ref[:, half + index * both : half + (index + 1) * both]
        wide_ref[:, (2 * index + 1) * both : (2 * index + 2) * both] = jnp.ones((tiles * span, both), BF)

    def attend(index, tile, first, last):
        lanes = lanes_at(index, both)
        at = slice(first * span, last * span)
        places = [pl.ds(pl.multiple_of(rel_c * rows + tile * TILE, TILE), TILE) for rel_c in range(2)]
        query = stack_heads(jnp.concatenate([qkv_ref[place, lanes] for place in places], axis=0))
        score = dot_nt(query, kv_ref[at, lanes])
        asked = asks_ref[tile][:, :1]
        allowed = jnp.concatenate([asked == key_item[other] for other in range(first, last)], axis=1)
        score = jnp.where(jnp.concatenate([allowed, allowed], axis=0), score, MASKED)
        best = jnp.max(score, axis=1, keepdims=True)
        weight = jnp.exp(score - best).astype(BF)
        mixed = dot_nn(weight, wide_ref[at, lanes_at(index, 2 * both)])
        total = mixed[:, both:]
        logsum_ref[index, pl.ds(tile, 1)] = (best + jnp.log(total)).T[:1]
        mixed = mixed[:, :both] / total
        attended = jnp.where(lanes_below((both, both), HEAD_SIZE), mixed[:both], mixed[both:]).astype(BF)
        for rel_c, place in enumerate(places):
            attended_ref[place, lanes] = attended[rel_c * TILE : (rel_c + 1) * TILE]

    def pair(index):
        for tile in range(tiles):
            attend(index, tile, *near_tiles(tile, tiles))

    each(half // both, pair)

    @pl.when(any_far(where_ref, tiles, parts, items))
    def far():
        def again(step):
            tile = step % tiles
            found = jnp.bool_(False)
            for one, other in far_pairs(tiles):
                found = found | ((tile == one) & tiles_meet(where_ref, one, other, parts, items))
            pl.when(found)(lambda: attend(step // tiles, tile, 0, tiles))

        each(half // both * tiles, again)


def gelu_with_slope(values):
    bell = jnp.exp(-0.5 * values * values)
    inverse = 1.0 / (1.0 + (0.3275911 * 0.5**0.5) * jnp.abs(values))
    series = 1.061405429
    for coefficient in (-1.453152027, 1.421413741, -0.284496736, 0.254829592):
        series = series * inverse + coefficient
    tail = 0.5 * (series * inverse) * bell
    normal = jnp.where(values >= 0, 1.0 - tail, tail)
    return values * normal, normal + values * bell * ((2.0 * math.pi) ** -0.5)


def set_block(where_ref, rel_y, low_z, high_z):
    return 2 * (where_ref[2] ^ (low_z + 2 * high_z)) + (where_ref[3] ^ rel_y)


def mlp_kernel(where_ref, stage, vec_ref, bias_ref, mid_ref, joined, normed, grad, turned, dbefore_ref):
    py_ref, ux_ref, dz_ref = stage.out(0), stage.out(2), stage.out(4)
    xhat_ref, inverse_ref, mid_own_ref, branch_ref, swap_ref, act_ref, bias_sum_ref = (
        stage.out(index) for index in range(6, 13)
    )
    unpack_rows(stage[4], vec_ref)
    att_own_ref, att_sib_ref, own_ref, sib_ref, raw_ref, out_ref = (stage[index] for index in range(6))
    stage.start(6, 7, 8)
    x, core, z, y = (where_ref[index] for index in range(4))
    rows, width = own_ref.shape
    half = width // 2
    piece = act_ref.shape[1] // 4
    joined[:, :half] = att_own_ref[...]
    joined[:rows, half:] = att_sib_ref[rows:]
    joined[rows:, half:] = att_sib_ref[:rows]

    def project(index):
        lanes = lanes_at(index, 256)
        branch = dot_nn(joined[...], out_ref[:, lanes]) + vec_ref[4:5, lanes]
        branch_ref[:, lanes] = branch[:rows].astype(BF)
        branch = vec_ref[5:6, lanes] * branch
        mid_ref[:rows, lanes] = own_ref[:, lanes].astype(F32) + branch[:rows]
        mid_ref[rows:, lanes] = sib_ref[:, lanes].astype(F32) + branch[rows:]

    each(width // 256, project)

    mid_own_ref[...] = mid_ref[:rows]

    def norm(index):
        at = lanes_at(index, WIDE_CHUNK)
        xhat, inverse = standardise(mid_ref[at])
        normed[at] = (xhat * vec_ref[6:7] + vec_ref[7:8]).astype(BF)
        xhat_ref[at] = xhat.astype(BF)
        inverse_ref[at] = inverse

    each(2 * rows // WIDE_CHUNK, norm)
    stage.put(6, 7, 8, 9)
    count = piece // 128
    for unit in range(8):
        for part in range(count):
            row = 10 * width // 128 + unit * count + part
            bias_ref[unit : unit + 1, part * 128 : (part + 1) * 128] = raw_ref[row : row + 1]
    up_ref, dact_ref, turned_ref = stage[6], stage[7], stage[8]
    size = grad.shape[0] // 8

    def hidden(index):
        rel_x = 1 - index
        for side in range(2):
            at = lanes_at(2 * rel_x + side, piece)
            before = dot_nn(normed[...], up_ref[:, at]) + bias_ref[pl.ds(hidden_unit(where_ref, rel_x, side), 1)]
            act, slope = gelu_with_slope(before)
            act_ref[:, at] = act.astype(BF)
            dbefore = (dact_ref[:, at].astype(F32) * slope).astype(BF)
            dbefore_ref[:, at] = dbefore
            bias_sum_ref[:, at] = column_sum(dbefore.astype(F32))
            grad[:, side * piece : (side + 1) * piece] = dot_nn(turned_ref[...], act_ref[:, at]).astype(BF)

        def lay(index):
            low_z, high_z, rel_y = index // 4, index // 2 % 2, index % 2
            first = set_block(where_ref, rel_y, low_z, high_z) * size
            most = dz_ref.shape[4] - size
            dz_ref[low_z, high_z, rel_x, rel_y, :size] = grad[pl.ds(pl.multiple_of(first, size), size), :piece]
            dz_ref[low_z, high_z, rel_x, rel_y, size:] = grad[pl.ds(pl.multiple_of(first, size), most), piece:]
            py_ref[rel_y, rel_x, lanes_at(2 * low_z + high_z, size - most)] = grad[
                pl.ds(pl.multiple_of(first + most, size - most), size - most), piece:
            ]

        each(8, lay)

    each(2, hidden)
    stage.put(4, 5, 11, 12)
    turn(normed, turned)
    block = 2 * size

    def up(index):
        rel_y, high_z = index // 2, index % 2
        unit = 2 * (x ^ (z // 2) ^ high_z) + (y ^ rel_y)
        grad[:, :piece] = dot_nn(turned[...], dbefore_ref[:, lanes_at(unit, piece)]).astype(BF)
        for rel_x in range(2):
            to = pl.ds(pl.multiple_of(py_ref.shape[2] - 2 * block + high_z * block, 64), block)
            py_ref[rel_y, rel_x, to] = grad[lanes_at(own_block(where_ref, rel_x, 0), block), :piece]
            ux_ref[rel_x, rel_y, high_z] = grad[lanes_at(own_block(where_ref, rel_x, 1), block), :piece]

    each(4, up)
    stage.put(0, 1, 2, 3)

    def back(index):
        lanes = lanes_at(index, 256)
        total = dot_nt(dbefore_ref[...], up_ref[lanes])
        swap_ref[:, lanes] = total.astype(BF)

    each(width // 256, back)


def middle(parts, items, where_ref, stage, vec_ref, sum_ref, datt_ref, held, chosen, packed):
    dmid_ref, a_ref, o_ref = stage.out(0), stage.out(1), stage.out(5)
    keep_ref, got_ref, xhat_ref, inverse_ref, own_ref, sib_ref, raw_ref = (stage[index] for index in range(7))
    stage.start(10, 9, 7, 8, 11, 12, 13)
    unpack_rows(raw_ref, vec_ref)
    rows, width = own_ref.shape
    half = width // 2
    core = where_ref[1]
    left_is_own = lanes_below((rows, half), half // 2) == (core == 0)
    for rel_c, ref in enumerate((own_ref, sib_ref)):
        here = slice(rel_c * rows, (rel_c + 1) * rows)
        there = slice((1 - rel_c) * rows, (2 - rel_c) * rows)
        valid = valid_at(where_ref, rel_c, 0, rows, parts, items)
        dnormed = keep_ref[here].astype(F32) + got_ref[there].astype(F32)
        xhat, inverse = xhat_ref[here].astype(F32), inverse_ref[here]
        dmid = ref[...].astype(F32) * valid + standardise_grad(vec_ref[6:7] * dnormed, xhat, inverse)
        dbranch = (vec_ref[5:6] * dmid).astype(BF)
        held[here] = dbranch
        if rel_c == 0:
            dmid_ref[...] = dmid
            sum_ref[0:1] = column_sum(dbranch.astype(F32))
            sum_ref[1:2] = column_sum(dmid * stage[10][...].astype(F32))
            sum_ref[2:3] = column_sum(dnormed * xhat)
            sum_ref[3:4] = column_sum(dnormed)
    stage.put(0)
    stage.start(14, 15)
    datt_ref[...] = dot_nt(held[...], stage[9][...]).astype(BF)
    att_own_ref, att_sib_ref = stage[7], stage[8]
    for rel_c in range(2):
        here = slice(rel_c * rows, (rel_c + 1) * rows)
        there = slice((1 - rel_c) * rows, (2 - rel_c) * rows)
        other = pltpu.roll(att_sib_ref[there].astype(F32), half // 2, 1)
        chosen[here] = jnp.where(left_is_own, att_own_ref[here].astype(F32), other).astype(BF)
    grad = dot_tn(held[...], chosen[...])
    count, unit_rows = packed.shape[1:3]
    for index in range(count):
        left, right = pack_unit(grad[2 * index * unit_rows : 2 * (index + 1) * unit_rows])
        packed[0, index] = left.astype(BF)
        packed[1, index] = right.astype(BF)

    units = 6 * unit_rows

    def lay(index):
        rel_x, rel_y, block = index // 8, index // 4 % 2, index % 4
        here = packed.at[where_ref[0] ^ rel_x, set_block(where_ref, rel_y, block // 2, block % 2)]
        a_ref[rel_x, rel_y, pl.ds(pl.multiple_of(units + 16 * block, 16), 16)] = here[:16]
        o_ref[rel_y, rel_x, lanes_at(block, unit_rows - 16)] = here[16:]

    each(16, lay)
    stage.put(5, 6)


def pack_unit(unit):
    half = unit.shape[0] // 2
    width = unit.shape[1]
    top, bottom = unit[:half], unit[half:]
    first = lanes_below((half, width), width // 2)
    left = jnp.where(first, top, pltpu.roll(bottom, width // 2, 1))
    right = jnp.where(first, pltpu.roll(top, width // 2, 1), bottom)
    return left, right


def join_heads(stacked_turned):
    stacked = stacked_turned.T
    count = stacked.shape[0] // 2
    return jnp.where(
        lanes_below((count, stacked.shape[1]), HEAD_SIZE), stacked[:count], stacked[count:]
    )


def query_items(where_ref, tile, parts, items):
    lane = lax.broadcasted_iota(jnp.int32, (1, 4 * TILE), 1)
    rel_c = (lane // TILE) % 2
    block = 2 * where_ref[0] + (where_ref[1] ^ rel_c)
    return item_at((tile * TILE + lane % TILE) * parts + block, where_ref, items)


def fill_key_items(where_ref, item_ref, tiles, parts, items):
    row = lax.broadcasted_iota(jnp.int32, (TILE, item_ref.shape[1]), 0)
    for tile in range(tiles):
        for slot in range(parts):
            block = own_block(where_ref, slot // 2, slot % 2)
            at = (tile * parts + slot) * TILE
            item_ref[at : at + TILE] = item_at((tile * TILE + row) * parts + block, where_ref, items)


def both_heads(array):
    return jnp.concatenate([array, array], axis=1)


def attend_grad(
    parts, items, where_ref, stage, datt_ref, dquery_ref, dkeys_ref, dvalues_ref, asks_ref, item_ref, turned_ref, dk, dv, dq
):
    attended_ref, qkv_ref, kv_ref, logsum_ref = stage[7], stage[11], stage[12], stage[13]
    half = datt_ref.shape[1]
    rows = datt_ref.shape[0] // 2
    tiles = rows // TILE
    span = parts * TILE
    scale = HEAD_SIZE ** (-0.5)
    turned_ref[...] = kv_ref[:, :half].T
    fill_key_items(where_ref, item_ref, tiles, parts, items)
    for tile in range(tiles):
        asks_ref[tile : tile + 1] = query_items(where_ref, tile, parts, items)
    some_far = any_far(where_ref, tiles, parts, items)

    def pair(index, carry):
        lanes = lanes_at(index, 2 * HEAD_SIZE)
        value_lanes = pl.ds(pl.multiple_of(half + index * 2 * HEAD_SIZE, 2 * HEAD_SIZE), 2 * HEAD_SIZE)
        dk[...] = jnp.zeros_like(dk)
        dv[...] = jnp.zeros_like(dv)

        def places(tile):
            return [pl.ds(pl.multiple_of(rel_c * rows + tile * TILE, TILE), TILE) for rel_c in range(2)]

        def visit(tile, at):
            query = stack_heads(jnp.concatenate([qkv_ref[place, lanes] for place in places(tile)], axis=0))
            grad = jnp.concatenate([datt_ref[place, lanes] for place in places(tile)], axis=0)
            attended = jnp.concatenate([attended_ref[place, lanes] for place in places(tile)], axis=0)
            product = (grad.astype(F32) * attended.astype(F32)).T
            delta = jnp.concatenate([column_sum(product[:HEAD_SIZE]), column_sum(product[HEAD_SIZE:])], axis=1)
            grad = stack_heads(grad)
            score = dot_nt(kv_ref[at, lanes], query)
            allowed = both_heads(item_ref[at]) == asks_ref[pl.ds(tile, 1)]
            prob = jnp.exp(jnp.where(allowed, score, MASKED) - logsum_ref[index, pl.ds(tile, 1)])
            dprob = dot_nt(kv_ref[at, value_lanes], grad)
            dscore = (prob * (dprob - delta)).astype(BF)
            dv[at] += dot_nn(prob.astype(BF), grad)
            dk[at] += dot_nn(dscore, query)
            return dot_nn(turned_ref[lanes, at], dscore)

        for tile in range(tiles):
            first, last = near_tiles(tile, tiles)
            dq[tile] = visit(tile, slice(first * span, last * span))

        @pl.when(some_far)
        def far():
            def add(step):
                tile, other = step // tiles, step % tiles
                found = jnp.bool_(False)
                for one, two in far_pairs(tiles):
                    found = found | ((step == one * tiles + two) & tiles_meet(where_ref, one, two, parts, items))

                @pl.when(found)
                def meet():
                    at = pl.ds(pl.multiple_of(other * span, span), span)
                    dq[tile] += visit(tile, at)

            each(tiles * tiles, add)

        for tile in range(tiles):
            dquery = (join_heads(dq[tile]) * scale).astype(BF)
            for rel_c, place in enumerate(places(tile)):
                dquery_ref[place, lanes] = dquery[rel_c * TILE : (rel_c + 1) * TILE]
            for slot in range(parts):
                to = slice(slot * rows + tile * TILE, slot * rows + (tile + 1) * TILE)
                at = slice(tile * span + slot * TILE, tile * span + (slot + 1) * TILE)
                dkeys_ref[to, lanes] = dk[at].astype(BF)
                dvalues_ref[to, lanes] = dv[at].astype(BF)
        return carry

    lax.fori_loop(0, half // (2 * HEAD_SIZE), pair, 0)


def twice(half_row, where_ref):
    row = both_heads(half_row)
    return jnp.where(lanes_below(row.shape, half_row.shape[1]) == (where_ref[1] == 0), row, 0.0)


def qkv_grad(where_ref, stage, vec_ref, sum_ref, dquery_ref, dkeys_ref, dvalues_ref, normed_ref, packed):
    a_ref, b_ref = stage.out(1), stage.out(3)
    near_ref, far_ref = stage[14], stage[15]
    rows, width = near_ref.shape
    core, z, y = where_ref[1], where_ref[2], where_ref[3]
    normed_ref[:rows] = normed_rows(near_ref[...], vec_ref, 0)
    normed_ref[rows:] = normed_rows(far_ref[...], vec_ref, 0)
    sum_ref[4:5] = twice(column_sum(dquery_ref[...].astype(F32)), where_ref)
    sum_ref[5:6] = twice(column_sum(dvalues_ref[...].astype(F32)), where_ref)
    for part, ref in enumerate((dquery_ref, dkeys_ref, dvalues_ref)):
        grad = dot_tn(ref[...], normed_ref[: ref.shape[0]])
        size = grad.shape[0] // 4
        for unit in range(4):
            for at_x in range(2):
                left, right = pack_unit(
                    grad[unit * size : (unit + 1) * size, at_x * width // 2 : (at_x + 1) * width // 2]
                )
                packed[2 * at_x, 4 * part + unit] = left.astype(BF)
                packed[2 * at_x + 1, 4 * part + unit] = right.astype(BF)

    def lay(index):
        rel_x, rel_y, at = index // 12, index // 6 % 2, index % 6
        unit = where_ref[UNIT_LIST + 24 * core + 12 * (y ^ rel_y) + 6 * (z % 2) + at]
        a_ref[rel_x, rel_y, lanes_at(at, packed.shape[2])] = packed[own_block(where_ref, rel_x, 0), unit]
        b_ref[rel_y, rel_x, at] = packed[own_block(where_ref, rel_x, 1), unit]

    each(24, lay)
    stage.put(1, 2, 3, 4)


def backward_kernel(
    parts, items, where_ref, stage, vec_ref, datt_ref, held, chosen, gpacked, normed_ref, packed, asks_ref, item_ref,
    turned_ref, dk, dv, dq,
):
    sum_ref, dquery_ref, dkeys_ref, dvalues_ref = (stage.out(index) for index in (10, 7, 8, 9))
    middle(parts, items, where_ref, stage, vec_ref, sum_ref, datt_ref, held, chosen, gpacked)
    attend_grad(
        parts, items, where_ref, stage, datt_ref, dquery_ref, dkeys_ref, dvalues_ref, asks_ref, item_ref, turned_ref,
        dk, dv, dq,
    )
    stage.put(7, 8, 9)
    qkv_grad(where_ref, stage, vec_ref, sum_ref, dquery_ref, dkeys_ref, dvalues_ref, normed_ref, packed)


def tokens_grad_kernel(parts, items, where_ref, stage, vec_ref):
    own_ref, far_ref, send_ref, keep_ref, sum_ref = (stage.out(index) for index in range(5))
    dquery_ref, dkeys_ref, dvalues_ref, weight_ref, near_ref, beyond_ref = (stage[index] for index in range(6))
    rows, width = own_ref.shape
    half = dquery_ref.shape[1]
    gain = jnp.zeros((1, width), F32)
    shift = gain
    for slot in (1, 3, 2, 0):
        at = slice(slot * rows, (slot + 1) * rows)
        part = dot_nt(dkeys_ref[at], weight_ref[:, half : 2 * half]) + dot_nt(dvalues_ref[at], weight_ref[:, 2 * half :])
        if slot < 2:
            part = part + dot_nt(dquery_ref[at], weight_ref[:, :half])
        xhat = (near_ref if slot < 2 else beyond_ref)[(slot % 2) * rows : (slot % 2 + 1) * rows].astype(F32)
        gain = gain + column_sum(part * xhat)
        shift = shift + column_sum(part)
        if slot % 2:
            send_ref[slot // 2 * rows : (slot // 2 + 1) * rows] = part.astype(BF)
        elif slot:
            far_ref[...] = part.astype(BF)
        else:
            own_ref[...] = part.astype(BF)
    stage.put(0, 1)
    unpack_rows(stage[6], vec_ref)
    act_ref, down_ref, cot_ref, cot_sib_ref, back_ref, bias_d_ref, bias_up_ref = (stage[index] for index in range(7, 14))
    feed = dot_nn(act_ref[...], down_ref[...])
    keep_ref[...] = feed[:rows] + vec_ref[8:9]
    send_ref[2 * rows :] = feed[rows:].astype(BF)
    stage.put(2, 3)
    scale = column_sum(cot_ref[...].astype(F32) * valid_at(where_ref, 0, 0, rows, parts, items) * keep_ref[...])
    scale = scale + column_sum(cot_sib_ref[...].astype(F32) * valid_at(where_ref, 1, 0, rows, parts, items) * feed[rows:])
    sum_ref[0:1] = gain
    sum_ref[1:2] = shift
    sum_ref[2:4] = back_ref[4:6]
    sum_ref[4:8] = back_ref[0:4]
    sum_ref[8:9] = bias_d_ref[...]
    sum_ref[9:10] = scale
    for at_x in range(2):
        one = bias_up_ref[:, at_x * width : (at_x + 1) * width]
        two = bias_up_ref[:, (1 - at_x) * width : (2 - at_x) * width]
        here = jnp.where(where_ref[0] == 0, one, two)
        for at_c in range(2):
            at = 10 + 2 * at_x + at_c
            sum_ref[at : at + 1] = jnp.where(where_ref[1] == at_c, here, 0.0)
    sum_ref[14:] = jnp.zeros((2, width), F32)


def unpack_unit(unit, target, first):
    half, lanes = unit.shape
    target[first : first + half] = unit[:, : target.shape[1]]
    target[first + half : first + 2 * half] = pltpu.roll(unit, lanes // 2, 1)[:, : target.shape[1]]


def sum_of(*terms):
    total = terms[0].astype(F32)
    for term in terms[1:]:
        total = total + term.astype(F32)
    return total


def fold_sums(sums):
    lanes = sums.shape[1] // 2
    return jnp.concatenate([sums[:, :lanes], sums[:, lanes:]], axis=0)


def second_step_kernel(where_ref, stage):
    dz_keep, dz_got, py_keep, py_got, a_ref, ux_keep, ux_got, b_got, o_ref = (stage[index] for index in range(9))
    dz_ref, x_ref, y_ref = (stage.out(index) for index in range(3))
    dz_ref[...] = sum_of(dz_keep[...], dz_got[...]).astype(BF)
    stage.put(0)
    count, rows = py_keep.shape[0], a_ref.shape[1]
    x_ref[:count] = sum_of(py_keep[...], py_got[...]).astype(BF)
    for rel_y in range(2):
        x_ref[count + rel_y * rows : count + (rel_y + 1) * rows] = a_ref[rel_y]
    stage.put(1)
    block = ux_keep.shape[1]
    for high_z in range(2):
        y_ref[high_z * block : (high_z + 1) * block] = sum_of(ux_keep[high_z], ux_got[high_z]).astype(BF)
    unit_rows = b_got.shape[2]
    first = 2 * block
    for rel_x in range(2):
        for index in range(6):
            y_ref[first : first + unit_rows] = b_got[rel_x, index]
            first += unit_rows
    rows = o_ref.shape[1]
    for rel_x in range(2):
        y_ref[first : first + rows] = o_ref[rel_x]
        first += rows


def third_step_kernel(where_ref, stage):
    ux_keep, ux_got, y_got, py_keep, py_got, x_got, b_keep, o_keep = (stage[index] for index in range(8))
    sum_refs, a_keep = [stage[index] for index in range(8, 12)], stage[12]
    send_ref, x_ref, a_ref, keep_ref = (stage.out(index) for index in range(4))
    count = py_keep.shape[0]
    block = ux_keep.shape[1]
    lead = send_ref.shape[1] - block
    same = where_ref[2] % 2 == where_ref[1]
    for high_z in range(2):
        at = slice(4 * lead + high_z * block, 4 * lead + (high_z + 1) * block)
        own = sum_of(py_keep[at], py_got[at], x_got[at])
        sib = sum_of(ux_keep[high_z], ux_got[high_z], y_got[high_z * block : (high_z + 1) * block])
        for side, ref in enumerate((keep_ref, send_ref)):
            at = slice((2 * side + high_z) * lead, (2 * side + high_z + 1) * lead)
            ref[high_z, :lead] = sum_of(py_keep[at], py_got[at], x_got[at]).astype(BF)
            here = jnp.where(same, sib, own) if side else jnp.where(same, own, sib)
            ref[high_z, lead:] = here.astype(BF)
    stage.put(0)
    unit_rows, rows = b_keep.shape[1], o_keep.shape[0]
    units = 6 * unit_rows
    first = 2 * block + units
    for index in range(6):
        at = slice(index * unit_rows, (index + 1) * unit_rows)
        x_ref[at] = sum_of(b_keep[index], y_got[first + index * unit_rows : first + (index + 1) * unit_rows]).astype(BF)
    first += units + rows
    x_ref[units : units + rows] = sum_of(o_keep[...], y_got[first : first + rows]).astype(BF)
    x_ref[units + rows :] = fold_sums(sum_of(*(ref[...] for ref in sum_refs))).astype(BF)
    stage.put(1)
    a_ref[...] = sum_of(a_keep[...], x_got[count + a_keep.shape[0] :]).astype(BF)


def fourth_step_kernel(where_ref, stage):
    a_keep, x_got, a_far, b_keep, y_got, b_far, o_keep, y_rest, x_ref, mlp_keep, mlp_got, dz_keep, dz_got, dz_far = (
        stage[index] for index in range(14)
    )
    send_ref, mlp_ref, dz_ref, mlp_kept, kept_ref, dz_kept, dtok_ref = (stage.out(index) for index in range(7))
    unit_rows, rows = b_keep.shape[1], o_keep.shape[0]
    units, most = 6 * unit_rows, rows // 4
    own = sum_of(a_keep[...], x_got[...], a_far[...]).astype(BF)
    rest = sum_of(o_keep[...], y_rest[...], b_far[units : units + rows]).astype(BF)
    sums = sum_of(x_ref[...], b_far[units + rows :]).astype(BF)
    for side, ref in enumerate((kept_ref, send_ref)):
        ref[: units // 2] = own[side * units // 2 : (side + 1) * units // 2]
        for index in range(3):
            unit = 3 * side + index
            at = slice(unit * unit_rows, (unit + 1) * unit_rows)
            to = slice((3 + index) * unit_rows, (4 + index) * unit_rows)
            ref[to] = sum_of(b_keep[unit], y_got[at], b_far[at]).astype(BF)
        for high_z in range(2):
            first, block = units + high_z * unit_rows, 2 * side + high_z
            ref[first : first + 16] = own[units + 16 * block : units + 16 * (block + 1)]
            ref[first + 16 : first + unit_rows] = rest[block * most : (block + 1) * most]
        ref[units + 2 * unit_rows :] = sums
    stage.put(0)
    mlp_ref[...] = sum_of(mlp_keep[1], mlp_got[1]).astype(BF)
    stage.put(1)
    for side, ref in enumerate((dz_kept, dz_ref)):
        ref[...] = sum_of(dz_keep[side], dz_got[side], dz_far[side]).astype(BF)
    stage.put(2)
    dtok_ref[...] = sum_of(stage[14][...], stage[15][...]).astype(BF)
    stage.put(6)
    mlp_kept[...] = sum_of(mlp_keep[0], mlp_got[0]).astype(BF)


def fifth_step_kernel(where_ref, stage, held):
    kept_ref, last_got, dz_kept, dz_got = (stage[index] for index in range(4))
    send_ref, dz_ref, keep_ref, dz_low_ref = (stage.out(index) for index in range(4))
    core, z, y = where_ref[1], where_ref[2], where_ref[3]
    unit_rows = held.shape[1]
    for index in range(6):
        at = slice(index * unit_rows, (index + 1) * unit_rows)
        held[index] = sum_of(kept_ref[at], last_got[at]).astype(BF)
    rest = sum_of(kept_ref[6 * unit_rows :], last_got[6 * unit_rows :]).astype(BF)
    for side, ref, owner_z in ((1, send_ref, z ^ 2), (0, keep_ref, z)):
        for index in range(3):
            at = where_ref[UNIT_LIST + 48 + ((core * 2 + y) * 4 + owner_z) * 3 + index]
            ref[index * unit_rows : (index + 1) * unit_rows] = held[at]
        ref[3 * unit_rows : 4 * unit_rows] = rest[side * unit_rows : (side + 1) * unit_rows]
        ref[4 * unit_rows :] = rest[2 * unit_rows :]
    stage.put(0)
    for side, ref in enumerate((dz_low_ref, dz_ref)):
        ref[...] = sum_of(dz_kept[side], dz_got[side]).astype(BF)


def finish_kernel(where_ref, stage, rows_ref, out_rows_ref, flat):
    mlp_kept, mlp_far, dz_low, dz_far, last_keep, last_far = (stage[index] for index in range(6))
    down_ref, up_ref, out_ref, vec_ref, qkv_ref = (stage.out(index) for index in range(5))
    size, block = down_ref.shape[0], up_ref.shape[0]
    lanes = up_ref.shape[1]
    mlp, dz = sum_of(mlp_kept[...], mlp_far[...]), sum_of(dz_low[...], dz_far[...])
    lead = mlp.shape[0] - block
    most = size - lead
    up_ref[...] = mlp[lead:]
    down_ref[:, :lanes] = dz[:size]
    down_ref[:most, lanes:] = dz[size : size + most]
    down_ref[most:, lanes:] = mlp[:lead]
    stage.put(0, 1)
    out_rows_ref[...] = jnp.zeros_like(out_rows_ref)
    last = sum_of(last_keep[...], last_far[...])
    half = size // 2
    unpack_unit(last[3 * half : 4 * half], out_rows_ref, 0)
    out_ref[...] = out_rows_ref[...].T[: out_ref.shape[0], : out_ref.shape[1]]
    sums = last[4 * half :]
    count = sums.shape[0] // 2
    for row in range(count):
        flat[:, 2 * row * lanes : (2 * row + 1) * lanes] = sums[row : row + 1]
        flat[:, (2 * row + 1) * lanes : (2 * row + 2) * lanes] = sums[count + row : count + row + 1]
    share = vec_ref.shape[1]
    start = (4 * set_block(where_ref, 0, 0, 0) + own_block(where_ref, 0, 0)) * share
    window = flat[:, pl.ds(pl.multiple_of(start // 128 * 128, 128), 512)]
    window = pltpu.roll(jnp.broadcast_to(window, (8, 512)), (512 - start % 128) % 512, 1)
    vec_ref[...] = window[:1, :share]
    stage.put(2, 3)
    rows_ref[...] = jnp.zeros_like(rows_ref)
    for unit in range(3):
        unpack_unit(last[unit * half : (unit + 1) * half], rows_ref, 2 * unit * half)
    qkv_ref[...] = rows_ref[...].T[: qkv_ref.shape[0], : qkv_ref.shape[1]]


def rows_kernel(parts, items, where_ref, stage, vec_ref):
    keep_ref, late_ref, far_ref, own_ref, dmid_ref, raw_ref, feed_ref, mid_ref = (stage[index] for index in range(8))
    unpack_rows(raw_ref, vec_ref)
    rows = own_ref.shape[0]
    dnormed = sum_of(keep_ref[...], late_ref[:rows], far_ref[...])
    xhat, inverse = standardise(own_ref[...].astype(F32))
    stage.out(0)[...] = (dmid_ref[...] + standardise_grad(vec_ref[0:1] * dnormed, xhat, inverse)).astype(BF)
    stage.put(0)
    valid = valid_at(where_ref, 0, 0, rows, parts, items)
    feed = sum_of(feed_ref[...], late_ref[rows:])
    stage.out(1)[...] = (valid * (mid_ref[...] + vec_ref[9:10] * feed)).astype(BF)


def swapped(array, axis, bit):
    length = lax.axis_size(axis)
    return lax.ppermute(array, axis, [(i, i ^ bit) for i in range(length)])


def to_core(array):
    return swapped(array, "blk", 1)


def to_x(array):
    return swapped(array, "blk", 2)


def to_y(array):
    return swapped(array, "dp", 1)


def to_z(array):
    return swapped(array, "dp", 2)


def to_zz(array):
    return swapped(array, "dp", 4)


def after(done, *arrays):
    return lax.optimization_barrier((done, *arrays))[1:]


def first_rows(count):
    def cut(where_ref, source, target):
        return [(source.at[:count], target)]

    return cut


def entry(array, index):
    def cut(where_ref, source, target):
        return [(source.at[index], target)]

    return (array.shape[1:], 1, cut)


def first_and_last_rows(count):
    def cut(where_ref, source, target):
        return [(source.at[:count], target.at[:count]), (source.at[2 * count :], target.at[count:])]

    return cut


def some_rows(array, first, last):
    def cut(where_ref, source, target):
        return [(source.at[first:last], target)]

    return ((last - first, *array.shape[1:]), 1, cut)


def own_columns(first):
    def cut(where_ref, source, target):
        half = source.shape[0] // 2
        return [
            (source.at[:, lanes_at(where_ref[1] + 2 * part, half)], target.at[:, (part - first) * half : (part - first + 1) * half])
            for part in range(first, 3)
        ]

    return cut


def own_hidden(axis):
    def cut(where_ref, source, target):
        pairs = []
        piece = target.shape[axis] // 4
        for rel_x in range(2):
            for side in range(2):
                at = lanes_at(hidden_unit(where_ref, rel_x, side), piece)
                to = slice((2 * rel_x + side) * piece, (2 * rel_x + side + 1) * piece)
                pairs.append((source.at[at], target.at[to]) if axis == 0 else (source.at[:, at], target.at[:, to]))
        return pairs

    return cut


def both_head_rows(where_ref, source, target):
    half = target.shape[0] // 2
    return [
        (source.at[lanes_at(where_ref[1], half), :], target.at[:half]),
        (source.at[lanes_at(1 - where_ref[1], half), :], target.at[half:]),
    ]


def own_head_rows(where_ref, source, target):
    return [(source.at[lanes_at(where_ref[1], target.shape[0]), :], target)]


def on_device_aligned(tokens, lengths, w_qkv, w_out, w_up, w_down, vectors, cotangent):
    tokens, cotangent = tokens[0], cotangent[0]
    rows, width = tokens.shape
    hidden = w_up.shape[1]
    items = lengths.shape[1]
    parts = lax.axis_size("blk")
    sets = lax.axis_size("dp")
    position, turn = lax.axis_index("blk"), lax.axis_index("dp")
    x, core, z, y = position // 2, position % 2, turn // 2, turn % 2
    where = lengths
    half = width // 2
    inner = hidden // 2
    piece = hidden // sets
    both = 2 * rows
    total_rows = parts * rows
    block = width // parts
    share = width // sets
    names = (parts, items)
    zs = sets // 2
    all_columns = ((width, 3 * half), 3, own_columns(0))
    kv_columns = ((width, 2 * half), 2, own_columns(1))
    up_columns = ((width, inner), 4, own_hidden(1))
    down_rows = ((inner, width), 4, own_hidden(0))
    head_rows = ((half, width), 1, own_head_rows)
    out_rows = ((width, width), 2, both_head_rows)

    far_a = to_x(tokens)
    sib = to_core(tokens)
    cot_sib = to_core(cotangent)

    vec = vectors.reshape(-1, 128)
    rows_of_vec = pltpu.VMEM((10, width), F32)

    xhat_near, qkv_near, dact, dfeed_turned, bias_d_sum = staged_call(
        functools.partial(prepare_kernel, *names),
        where,
        (tokens, sib, vec, w_qkv, cotangent, cot_sib, w_down),
        [low(both, width), low(both, 3 * half), low(both, inner), low(width, both), full(1, width)],
        cuts={3: all_columns, 6: down_rows},
        scratch=[rows_of_vec, pltpu.VMEM((both, width), BF), pltpu.VMEM((both, width), BF), pltpu.VMEM((2, 3 * half), F32)],
    )

    far_a, qkv_near, dact = lax.optimization_barrier((far_a, qkv_near, dact))
    far_b = to_core(far_a)

    xhat_far, kv, attended, logsum = staged_call(
        functools.partial(attend_kernel, *names),
        where,
        (far_a, far_b, vec, w_qkv, qkv_near),
        [low(both, width), low(total_rows, width), low(both, half), full(half // (2 * HEAD_SIZE), rows // TILE, 4 * TILE)],
        cuts={3: kv_columns},
        scratch=[
            rows_of_vec,
            pltpu.VMEM((total_rows, 2 * half), BF),
            pltpu.VMEM((both, width), BF),
            pltpu.VMEM((rows // TILE, 2 * TILE, 2 * TILE), jnp.int32),
        ],
    )
    attended_sib = to_core(attended)

    unit_rows = share // 2
    lead = 32
    py, us, dz = low(2, 4 * lead + 2 * block, piece), low(2, 2, block, piece), low(2, 2, 2, 2 * share - lead, piece)
    (py_keep, py_send, ux_keep, ux_send, dz_keep, dz_send, xhat_two, inverse_two, mid, branch, swap, act,
     bias_up_sum) = staged_call(
        mlp_kernel,
        where,
        (attended, attended_sib, tokens, sib, vec, w_out, w_up, dact, dfeed_turned),
        [py, py, us, us, dz, dz, low(both, width), full(both, 1), full(rows, width), low(rows, width), low(both, width),
         low(both, inner), full(1, inner)],
        cuts={5: out_rows, 6: up_columns},
        late=(6, 7, 8),
        pairs=(0, 2, 4),
        scratch=[rows_of_vec, pltpu.VMEM((sets, piece), F32), pltpu.VMEM((both, width), F32),
                 pltpu.VMEM((both, width), BF), pltpu.VMEM((both, width), BF), pltpu.VMEM((width, 2 * piece), BF),
                 pltpu.VMEM((width, both), BF), pltpu.VMEM((both, inner), BF)],
    )
    swap_got = to_core(swap)
    ux_send, ux_keep = to_core(ux_send), to_core(ux_keep)
    py_got = to_y(py_send)
    ux_got = to_x(ux_send)
    dz_got = to_z(dz_send)

    dmid, a_keep, a_send, b_keep, b_send, o_keep, o_send, dquery, dkeys, dvalues, back_sums = staged_call(
        functools.partial(backward_kernel, *names),
        where,
        (swap, swap_got, xhat_two, inverse_two, cotangent, cot_sib, vec, attended, attended_sib, w_out, branch,
         qkv_near, kv, logsum, xhat_near, xhat_far),
        [full(rows, width)] + [low(2, 6 * unit_rows + 64, half)] * 2 + [low(2, 6, unit_rows, half)] * 2
        + [low(2, 4 * unit_rows - 64, half)] * 2
        + [low(both, half), low(total_rows, half), low(total_rows, half), full(8, width)],
        cuts={9: head_rows},
        late=tuple(range(7, 16)),
        pairs=(1, 3, 5),
        tables=True,
        scratch=[rows_of_vec, pltpu.VMEM((both, half), BF), pltpu.VMEM((both, width), BF),
                 pltpu.VMEM((both, half), BF), pltpu.VMEM((2, sets, unit_rows, half), BF),
                 pltpu.VMEM((total_rows, width), BF), pltpu.VMEM((4, 12, unit_rows, half), BF),
                 pltpu.VMEM((rows // TILE, 4 * TILE), jnp.int32), pltpu.VMEM((total_rows, 2 * TILE), jnp.int32),
                 pltpu.VMEM((half, total_rows), BF), pltpu.VMEM((total_rows, 2 * HEAD_SIZE), F32),
                 pltpu.VMEM((total_rows, 2 * HEAD_SIZE), F32),
                 pltpu.VMEM((rows // TILE, 2 * HEAD_SIZE, 4 * TILE), F32)],
    )
    six, top = 6 * unit_rows, 2 * share - lead
    step = functools.partial(staged_call, grant=STEP_GRANT)
    b_send, b_keep = to_core(b_send), to_core(b_keep)
    py_got, ux_got, dz_got, b_send, b_keep = after(back_sums, py_got, ux_got, dz_got, b_send, b_keep)
    count = py_keep.shape[1]
    dz_step, x_step, y_step = staged_call(
        second_step_kernel,
        where,
        (dz_keep, dz_got, py_keep, py_got, a_send, ux_keep, ux_got, b_send, o_send),
        [low(*dz_keep.shape[1:]), low(count + 2 * six + 128, half), low(2 * block + 2 * six + 8 * unit_rows - 128, half)],
        cuts={index: entry(array, 1)
              for index, array in ((0, dz_keep), (1, dz_got), (2, py_keep), (3, py_got), (5, ux_keep), (6, ux_got))},
    )
    dz_far, x_got, y_got = to_zz(dz_step), to_x(x_step), to_y(y_step)
    (back_sums,) = after(y_step, back_sums)
    dtok_own, dtok_far, late_send, feed_keep, sums = staged_call(
        functools.partial(tokens_grad_kernel, *names),
        where,
        (dquery, dkeys, dvalues, w_qkv, xhat_near, xhat_far, vec, act, w_down, cotangent, cot_sib, back_sums,
         bias_d_sum, bias_up_sum),
        [low(rows, width), low(rows, width), low(3 * rows, width), full(rows, width), full(16, width)],
        cuts={3: all_columns, 8: down_rows},
        scratch=[rows_of_vec],
    )
    sums_core, sums_y = to_core(sums), to_y(sums)
    sums_far = to_core(sums_y)
    dz_far, x_got, y_got, sums_core, sums_y, sums_far = lax.optimization_barrier(
        (dz_far, x_got, y_got, sums_core, sums_y, sums_far)
    )

    rest = 4 * unit_rows - 64
    mlp_send, b_step, a_step, mlp_keep = staged_call(
        third_step_kernel,
        where,
        (ux_keep, ux_got, y_got, py_keep, py_got, x_got, b_keep, o_keep, sums, sums_core, sums_y, sums_far, a_keep),
        [low(2, lead + block, piece), low(six + rest + 32, half), low(six + 64, half), low(2, lead + block, piece)],
        cuts={index: entry(array, 0) for index, array in ((0, ux_keep), (1, ux_got), (3, py_keep), (4, py_got))}
        | {index: entry(array, 1) for index, array in ((6, b_keep), (7, o_keep), (12, a_keep))},
    )
    mlp_got, b_far, a_far = to_z(mlp_send), to_x(b_step), to_y(a_step)
    (late_send,) = after(mlp_keep, late_send)
    late_got = to_core(late_send)
    mlp_got, b_far, a_far, late_got = lax.optimization_barrier((mlp_got, b_far, a_far, late_got))

    first = 2 * block + 2 * six
    last_send, mlp_step, dz_step, mlp_kept, last_keep, dz_kept, dtok_step = staged_call(
        fourth_step_kernel,
        where,
        (a_keep, x_got, a_far, b_keep, y_got, b_far, o_keep, y_got, b_step, mlp_keep, mlp_got, dz_keep, dz_got, dz_far,
         dtok_far, late_got),
        [low(six + 2 * unit_rows + 32, half), low(lead + block, piece), low(2, top, piece), low(lead + block, piece),
         low(six + 2 * unit_rows + 32, half), low(2, top, piece), low(rows, width)],
        cuts={0: entry(a_keep, 0), 1: some_rows(x_got, count, count + six + 64), 3: entry(b_keep, 0),
              4: some_rows(y_got, 2 * block, 2 * block + six), 6: entry(o_keep, 0), 7: some_rows(y_got, first, first + rest),
              8: some_rows(b_step, six + rest, six + rest + 32), 11: entry(dz_keep, 0), 12: entry(dz_got, 0),
              15: some_rows(late_got, rows, both)},
    )
    last_got, mlp_far, dz_x, dtok_x = to_z(last_send), to_zz(mlp_step), to_x(dz_step), to_x(dtok_step)
    last_send, dz_y, last_kept, dz_low = step(
        fifth_step_kernel,
        where,
        (last_keep, last_got, dz_kept, dz_x),
        [low(4 * unit_rows + 32, half), low(top, piece), low(4 * unit_rows + 32, half), low(top, piece)],
        scratch=[pltpu.VMEM((6, unit_rows, half), BF)],
        tables=True,
    )
    last_far, dz_y = to_zz(last_send), to_y(dz_y)

    (dtok_x,) = after(dz_low, dtok_x)
    grad_tokens, out = staged_call(
        functools.partial(rows_kernel, *names),
        where,
        (dtok_own, late_got, dtok_x, tokens, dmid, vec, feed_keep, mid),
        [low(rows, width), low(rows, width)],
        cuts={1: ((both, width), 2, first_and_last_rows(rows))},
        scratch=[rows_of_vec],
    )

    mlp_far, dz_y, last_far = after(grad_tokens, mlp_far, dz_y, last_far)
    g_w_down, g_w_up, g_w_out, g_vec, g_w_qkv = step(
        finish_kernel,
        where,
        (mlp_kept, mlp_far, dz_low, dz_y, last_kept, last_far),
        [full(share, 2 * piece), full(block, piece), full(block, share), full(1, vectors.shape[0] // (sets * parts)),
         full(block, 3 * share)],
        scratch=[pltpu.VMEM((384, 256), F32), pltpu.VMEM((128, 256), F32), pltpu.VMEM((1, 16 * width + 512), F32)],
    )
    return (out[None], grad_tokens[None], g_w_qkv, g_w_out, g_w_up, g_w_down.T, g_vec.reshape(-1))


def is_aligned(mesh, tokens, w_up):
    parts, sets = mesh.shape["blk"], mesh.shape["dp"]
    width, hidden = w_up.shape
    rows = tokens.shape[1] // parts
    return (
        parts == 4
        and sets == 2 * parts
        and rows == 4 * TILE
        and (hidden // sets) % 128 == 0
        and (width // 2) % 128 == 0
        and (width // sets) % 32 == 0
        and width == H * HEAD_SIZE
    )


def solution(mesh):
    def run(tokens, lengths, w_qkv, w_out, w_up, w_down, vectors, cotangent):
        body = on_device_aligned if is_aligned(mesh, tokens, w_up) else on_device
        return jax.shard_map(
            body,
            mesh=mesh,
            in_specs=(
                P("dp", "blk", None),
                P("dp", None),
                P(),
                P(),
                P(),
                P(),
                P(),
                P("dp", "blk", None),
            ),
            out_specs=(
                P("dp", "blk", None),
                P("dp", "blk", None),
                P("blk", "dp"),
                P("blk", "dp"),
                P("blk", "dp"),
                P("blk", "dp"),
                P(("dp", "blk")),
            ),
            check_vma=False,
        )(tokens, lengths, w_qkv, w_out, w_up, w_down, vectors, cotangent)

    return run
```

profile of v0, /device:TPU:0, one launch (start us, length us, event | category | flops | bytes accessed | tf_op | source)
XLA Modules:
  0.0 157.3 jit_solution(7844096720945826967)
XLA Ops:
  1.2 2.9 %collective-permute-start = (bf16[256,768]{1,0:T(8,128)(2,1)}, bf16[256,768]{1,0:T(8,128)(2,1)S(1)}, u32[]{:S(2)}, u32[]{:S(2)}) collective-permute-start(bf16[256,768]{1,0:T(8,128)(2,1)} %bitcast.11), channel_id=1, source_target_pairs={{0,2},{1,3},{2,0},{3,1},{4,6},{5,7},{6,4},{7,5},{8,10},{9,11},{10,... | collective-permute-start | bytes 1179656 | tf_op jit(solution)/shard_map/ppermute | solution.py:1228
  4.2 0.7 copy-done.16
  5.0 9.2 %shard_map.144 = (bf16[512,768]{1,0:T(8,128)(2,1)}, bf16[512,1152]{1,0:T(8,128)(2,1)}, bf16[512,1536]{1,0:T(8,128)(2,1)}, bf16[768,512]{1,0:T(8,128)(2,1)}, f32[1,768]{1,0:T(1,128)}) custom-call(s32[1,5]{1,0:T(1,128)} %refs_0_.21, bf16[256,768]{1,0:T(8,128)(2,1)} %bitcast.12, bf16[256,768]{1,0:T(8,128)(2,1)} %copy-done.16, f32[84,128]{1,0:T(8,128)} %bitcast.15, ...), custom_call_target="tpu_custom_call" | custom-call | tf_op jit(solution)/shard_map/pallas_call | solution.py:474
  14.3 1.7 %collective-permute-done.3.refs_2_ = bf16[256,768]{1,0:T(8,128)(2,1)S(1)} collective-permute-done((bf16[256,768]{1,0:T(8,128)(2,1)S(1)}, bf16[256,768]{1,0:T(8,128)(2,1)S(1)}, u32[]{:S(2)}, u32[]{:S(2)}) %collective-permute-start.3) | collective-permute-done | bytes 393248 | tf_op jit(solution)/shard_map/ppermute | solution.py:1228
  16.0 0.7 copy-done.22
  16.8 8.7 %shard_map.145 = (bf16[512,768]{1,0:T(8,128)(2,1)}, bf16[1024,768]{1,0:T(8,128)(2,1)}, bf16[512,384]{1,0:T(8,128)(2,1)}, f32[3,4,256]{2,1,0:T(4,128)}) custom-call(s32[1,5]{1,0:T(1,128)} %refs_0_.21, bf16[256,768]{1,0:T(8,128)(2,1)} %copy-done.21, bf16[256,768]{1,0:T(8,128)(2,1)} %copy-done.22, f32[84,128]{1,0:T(8,128)} %bitcast.16, ...), custom_call_target="tpu_custom_call" | custom-call | tf_op jit(solution)/shard_map/pallas_call | solution.py:474
  25.7 1.8 %collective-permute-done.4.refs_2_.refs_10_ = bf16[512,384]{1,0:T(8,128)(2,1)S(1)} collective-permute-done((bf16[512,384]{1,0:T(8,128)(2,1)}, bf16[512,384]{1,0:T(8,128)(2,1)S(1)}, u32[]{:S(2)}, u32[]{:S(2)}) %collective-permute-start.4) | collective-permute-done | bytes 393248 | tf_op jit(solution)/shard_map/ppermute | solution.py:1228
  27.5 0.7 copy-done.15
  28.2 17.9 %shard_map.146 = (bf16[2,512,384]{2,1,0:T(8,128)(2,1)}, bf16[2,512,384]{2,1,0:T(8,128)(2,1)}, bf16[2,2,192,384]{3,2,1,0:T(8,128)(2,1)}, bf16[2,2,192,384]{3,2,1,...) custom-call(s32[1,5]{1,0:T(1,128)} %refs_0_.21, ...), custom_call_target="tpu_custom_call" | custom-call | tf_op jit(solution)/shard_map/pallas_call | solution.py:474
  46.3 1.9 %collective-permute-start.6 = (bf16[2,512,384]{2,1,0:T(8,128)(2,1)}, bf16[2,512,384]{2,1,0:T(8,128)(2,1)S(1)}, u32[]{:S(2)}, u32[]{:S(2)}) collective-permute-start(bf16[2,512,384]{2,1,0:T(8,128)(2,1)} %get-tuple-element.115), channel_id=1, source_target_pairs={{0,4},{4,0},{8,12},{12,8},{16,20},{20,16},{24,28},{28,24},{1,5},{5... | collective-permute-start | bytes 2359304 | tf_op jit(solution)/shard_map/ppermute | solution.py:1228
  48.3 1.6 %collective-permute-start.9 = (bf16[2,2,2,160,384]{4,3,2,1,0:T(8,128)(2,1)}, bf16[2,2,2,160,384]{4,3,2,1,0:T(8,128)(2,1)S(1)}, u32[]{:S(2)}, u32[]{:S(2)}) collective-permute-start(bf16[2,2,2,160,384]{4,3,2,1,0:T(8,128)(2,1)} %get-tuple-element.117), channel_id=1, source_target_pairs={{0,8},{4,12},{8,0},{12,4},{16,24},{20,28},{24,16},{28,20},{1,9},{5... | collective-permute-start | bytes 2949128 | tf_op jit(solution)/shard_map/ppermute | solution.py:1228
  49.9 0.7 collective-permute-done.7
  50.6 1.5 collective-permute-start.8
  52.1 0.9 copy-done.17
  52.9 17.1 %shard_map.147 = (f32[256,768]{1,0:T(8,128)}, bf16[2,352,384]{2,1,0:T(8,128)(2,1)}, bf16[2,352,384]{2,1,0:T(8,128)(2,1)}, bf16[2,6,48,384]{3,2,1,0:T(8,128)(2,1)...) custom-call(s32[1,5]{1,0:T(1,128)} %refs_0_.21, ...), custom_call_target="tpu_custom_call" | custom-call | tf_op jit(solution)/shard_map/pallas_call | solution.py:474
  70.7 1.9 %collective-permute-done.9.refs_2_.refs_13_ = bf16[2,2,2,160,384]{4,3,2,1,0:T(8,128)(2,1)S(1)} collective-permute-done((bf16[2,2,2,160,384]{4,3,2,1,0:T(8,128)(2,1)}, bf16[2,2,2,160,384]{4,3,2,1,0:T(8,128)(2,1)S(1)}, u32[]{:S(2)}, u32[]{:S(2)}) %collective-permute-start.9) | collective-permute-done | bytes 983072 | tf_op jit(solution)/shard_map/ppermute | solution.py:1228
  72.9 0.7 copy-done.8
  74.1 4.2 %shard_map.148 = (bf16[2,2,160,384]{3,2,1,0:T(8,128)(2,1)}, bf16[1216,384]{1,0:T(8,128)(2,1)}, bf16[1216,384]{1,0:T(8,128)(2,1)}) custom-call(s32[1,5]{1,0:T(1,128)} %refs_0_.21, bf16[2,2,2,160,384]{4,3,2,1,0:T(8,128)(2,1)} %get-tuple-element.113.refs_1_.refs_12_, bf16[2,2,2,160,384]{4,3,2,1,0:T(8,128)(2,1)} %copy-done.8, ...), custom_call_target="tpu_custom_call" | custom-call | tf_op jit(solution)/shard_map/pallas_call | solution.py:474
  78.3 1.5 collective-permute-start.14
  80.4 2.6 %collective-permute-start.13 = (bf16[2,2,160,384]{3,2,1,0:T(8,128)(2,1)}, bf16[2,2,160,384]{3,2,1,0:T(8,128)(2,1)S(1)}, u32[]{:S(2)}, u32[]{:S(2)}) collective-permute-start(bf16[2,2,160,384]{3,2,1,0:T(8,128)(2,1)} %get-tuple-element.133), channel_id=1, source_target_pairs={{0,16},{4,20},{8,24},{12,28},{16,0},{20,4},{24,8},{28,12},{1,17},{... | collective-permute-start | bytes 1474568 | tf_op jit(solution)/shard_map/ppermute | solution.py:1228
  83.0 9.2 %shard_map.149 = (bf16[256,768]{1,0:T(8,128)(2,1)}, bf16[256,768]{1,0:T(8,128)(2,1)}, bf16[768,768]{1,0:T(8,128)(2,1)}, f32[256,768]{1,0:T(8,128)}, f32[16,768]{1,0:T(8,128)}) custom-call(s32[1,5]{1,0:T(1,128)} %refs_0_.21, bf16[512,384]{1,0:T(8,128)(2,1)} %get-tuple-element.109.refs_1_, bf16[1024,384]{1,0:T(8,128)(2,1)} %get-tuple-element.110.refs_2_, ...), custom_call_target="tpu_custom_call" | custom-call | tf_op jit(solution)/shard_map/pallas_call | solution.py:474
  92.2 1.6 %collective-permute-start.17 = (f32[16,768]{1,0:T(8,128)}, f32[16,768]{1,0:T(8,128)S(1)}, u32[]{:S(2)}, u32[]{:S(2)}) collective-permute-start(f32[16,768]{1,0:T(8,128)} %get-tuple-element.135.refs_9_), channel_id=1, source_target_pairs={{0,4},{4,0},{8,12},{12,8},{16,20},{20,16},{24,28},{28,24},{1,5},{5... | collective-permute-start | bytes 147464 | tf_op jit(solution)/shard_map/ppermute | solution.py:1228
  93.8 9.3 %collective-permute-done.17.refs_11_ = f32[16,768]{1,0:T(8,128)S(1)} collective-permute-done((f32[16,768]{1,0:T(8,128)}, f32[16,768]{1,0:T(8,128)S(1)}, u32[]{:S(2)}, u32[]{:S(2)}) %collective-permute-start.17) | collective-permute-done | bytes 49184 | tf_op jit(solution)/shard_map/ppermute | solution.py:1228
  103.1 1.2 collective-permute-done.18.refs_12_
  104.4 0.6 copy-done.28
  105.6 4.3 %shard_map.150 = (bf16[2,224,384]{2,1,0:T(8,128)(2,1)}, bf16[448,384]{1,0:T(8,128)(2,1)}, bf16[352,384]{1,0:T(8,128)(2,1)}, bf16[2,224,384]{2,1,0:T(8,128)(2,1)}) custom-call(s32[1,5]{1,0:T(1,128)} %refs_0_.21, bf16[2,2,192,384]{3,2,1,0:T(8,128)(2,1)} %copy-done.13, bf16[2,2,192,384]{3,2,1,0:T(8,128)(2,1)} %copy-done.12, bf16[1216,384]{1,0:T(8,128)(2,1)} %copy-done.6, ...), custom_call_target="tpu_custom_call" | custom-call | tf_op jit(solution)/shard_map/pallas_call | solution.py:474
  110.2 1.6 %collective-permute-start.19 = (bf16[2,224,384]{2,1,0:T(8,128)(2,1)}, bf16[2,224,384]{2,1,0:T(8,128)(2,1)S(1)}, u32[]{:S(2)}, u32[]{:S(2)}) collective-permute-start(bf16[2,224,384]{2,1,0:T(8,128)(2,1)} %get-tuple-element.144), channel_id=1, source_target_pairs={{0,8},{4,12},{8,0},{12,4},{16,24},{20,28},{24,16},{28,20},{1,9},{5... | collective-permute-start | bytes 1032200 | tf_op jit(solution)/shard_map/ppermute | solution.py:1228
  111.8 0.9 collective-permute-start.20
  112.7 1.0 collective-permute-start.21
  113.7 7.4 %collective-permute-done.21.refs_3_ = bf16[352,384]{1,0:T(8,128)(2,1)S(1)} collective-permute-done((bf16[352,384]{1,0:T(8,128)(2,1)}, bf16[352,384]{1,0:T(8,128)(2,1)S(1)}, u32[]{:S(2)}, u32[]{:S(2)}) %collective-permute-start.21) | collective-permute-done | bytes 270368 | tf_op jit(solution)/shard_map/ppermute | solution.py:1228
  121.1 0.9 collective-permute-done.20.refs_6_
  122.0 0.7 copy-done.24
  123.2 4.6 %shard_map.151 = (bf16[416,384]{1,0:T(8,128)(2,1)}, bf16[224,384]{1,0:T(8,128)(2,1)}, bf16[2,160,384]{2,1,0:T(8,128)(2,1)}, bf16[224,384]{1,0:T(8,128)(2,1)}, bf...) custom-call(s32[1,5]{1,0:T(1,128)} %refs_0_.21, ...), custom_call_target="tpu_custom_call" | custom-call | tf_op jit(solution)/shard_map/pallas_call | solution.py:474
  128.3 1.3 collective-permute-start.24
  129.6 0.7 collective-permute-start.25
  130.3 2.6 %collective-permute-start.26 = (bf16[224,384]{1,0:T(8,128)(2,1)}, bf16[224,384]{1,0:T(8,128)(2,1)S(1)}, u32[]{:S(2)}, u32[]{:S(2)}) collective-permute-start(bf16[224,384]{1,0:T(8,128)(2,1)} %get-tuple-element.169), channel_id=1, source_target_pairs={{0,16},{4,20},{8,24},{12,28},{16,0},{20,4},{24,8},{28,12},{1,17},{... | collective-permute-start | bytes 516104 | tf_op jit(solution)/shard_map/ppermute | solution.py:1228
  133.0 4.4 %collective-permute-done.24.refs_5_ = bf16[2,160,384]{2,1,0:T(8,128)(2,1)S(1)} collective-permute-done((bf16[2,160,384]{2,1,0:T(8,128)(2,1)}, bf16[2,160,384]{2,1,0:T(8,128)(2,1)S(1)}, u32[]{:S(2)}, u32[]{:S(2)}) %collective-permute-start.24) | collective-permute-done | bytes 245792 | tf_op jit(solution)/shard_map/ppermute | solution.py:1228
  137.4 3.0 %collective-permute-done.23.refs_3_ = bf16[416,384]{1,0:T(8,128)(2,1)S(1)} collective-permute-done((bf16[416,384]{1,0:T(8,128)(2,1)}, bf16[416,384]{1,0:T(8,128)(2,1)S(1)}, u32[]{:S(2)}, u32[]{:S(2)}) %collective-permute-start.23) | collective-permute-done | bytes 319520 | tf_op jit(solution)/shard_map/ppermute | solution.py:1228
  140.5 1.0 copy-done
  141.4 0.9 copy-done.1
  142.4 2.4 %shard_map.152 = (bf16[224,384]{1,0:T(8,128)(2,1)S(1)}, bf16[160,384]{1,0:T(8,128)(2,1)S(1)}, bf16[224,384]{1,0:T(8,128)(2,1)S(1)}, bf16[160,384]{1,0:T(8,128)(2,1)S(1)}) custom-call(s32[1,5]{1,0:T(1,128)S(1)} %copy-done.3, s32[96]{0:T(128)S(1)} %copy-done.5, bf16[416,384]{1,0:T(8,128)(2,1)S(1)} %copy-done, ...), custom_call_target="tpu_custom_call" | custom-call | tf_op jit(solution)/shard_map/pallas_call | solution.py:474
  144.8 0.8 collective-permute-start.28
  145.5 1.3 collective-permute-start.27
  146.9 0.8 copy-done.20
  147.6 4.8 %shard_map.153 = (bf16[256,768]{1,0:T(8,128)(2,1)}, bf16[256,768]{1,0:T(8,128)(2,1)}) custom-call(s32[1,5]{1,0:T(1,128)} %refs_0_.21, bf16[256,768]{1,0:T(8,128)(2,1)} %get-tuple-element.132.refs_1_, bf16[768,768]{1,0:T(8,128)(2,1)} %copy-done.7, bf16[256,768]{1,0:T(8,128)(2,1)} %copy-done.20, bf16[256,768]{1,0:T(8,128)(2,1)} %bitcast.14, ...), custom_call_target="tpu_custom_call" | custom-call | tf_op jit(solution)/shard_map/pallas_call | solution.py:474
  152.5 1.1 collective-permute-done.28.refs_6_
  153.6 3.0 %shard_map.154 = (f32[96,768]{1,0:T(8,128)}, f32[192,384]{1,0:T(8,128)}, f32[192,96]{1,0:T(8,128)}, f32[1,336]{1,0:T(1,128)S(1)}, f32[192,288]{1,0:T(8,128)}) custom-call(s32[1,5]{1,0:T(1,128)S(1)} %copy-done.4, bf16[224,384]{1,0:T(8,128)(2,1)S(1)} %copy-done.2, bf16[224,384]{1,0:T(8,128)(2,1)S(1)} %collective-permute-done.26.refs_2_, ...), custom_call_target="tpu_custom_call" | custom-call | tf_op jit(solution)/shard_map/pallas_call | solution.py:474
  156.7 0.6 reduce
  (82 shorter events, 5.2 us)
Async XLA Ops:
  0.6 3.5 %collective-permute-start.1 = (bf16[256,768]{1,0:T(8,128)(2,1)}, bf16[256,768]{1,0:T(8,128)(2,1)S(1)}, u32[]{:S(2)}, u32[]{:S(2)}) collective-permute-start(bf16[256,768]{1,0:T(8,128)(2,1)} %bitcast.10), channel_id=1, source_target_pairs={{0,1},{1,0},{2,3},{3,2},{4,5},{5,4},{6,7},{7,6},{8,9},{9,8},{10,11... | collective-permute-start | bytes 1179656 | tf_op jit(solution)/shard_map/ppermute | solution.py:1228
  1.1 3.0 %collective-permute-start.2 = (bf16[256,768]{1,0:T(8,128)(2,1)}, bf16[256,768]{1,0:T(8,128)(2,1)S(1)}, u32[]{:S(2)}, u32[]{:S(2)}) collective-permute-start(bf16[256,768]{1,0:T(8,128)(2,1)} %bitcast.6), channel_id=1, source_target_pairs={{0,1},{1,0},{2,3},{3,2},{4,5},{5,4},{6,7},{7,6},{8,9},{9,8},{10,11... | collective-permute-start | bytes 1179656 | tf_op jit(solution)/shard_map/ppermute | solution.py:1228
  1.2 13.0 %collective-permute-start = (bf16[256,768]{1,0:T(8,128)(2,1)}, bf16[256,768]{1,0:T(8,128)(2,1)S(1)}, u32[]{:S(2)}, u32[]{:S(2)}) collective-permute-start(bf16[256,768]{1,0:T(8,128)(2,1)} %bitcast.11), channel_id=1, source_target_pairs={{0,2},{1,3},{2,0},{3,1},{4,6},{5,7},{6,4},{7,5},{8,10},{9,11},{10,... | collective-permute-start | bytes 1179656 | tf_op jit(solution)/shard_map/ppermute | solution.py:1228
  14.2 1.8 %copy-start.21 = (bf16[256,768]{1,0:T(8,128)(2,1)}, bf16[256,768]{1,0:T(8,128)(2,1)S(1)}, u32[]{:S(2)}) copy-start(bf16[256,768]{1,0:T(8,128)(2,1)S(1)} %collective-permute-done.refs_1_) | copy-start | bytes 1179652
  14.2 1.8 %collective-permute-start.3 = (bf16[256,768]{1,0:T(8,128)(2,1)S(1)}, bf16[256,768]{1,0:T(8,128)(2,1)S(1)}, u32[]{:S(2)}, u32[]{:S(2)}) collective-permute-start(bf16[256,768]{1,0:T(8,128)(2,1)S(1)} %collective-permute-done.refs_1_), channel_id=1, source_target_pairs={{0,1},{1,0},{2,3},{3,2},{4,5},{5,4},{6,7},{7,6},{8,9},{9,8},{10,11... | collective-permute-start | bytes 1179656 | tf_op jit(solution)/shard_map/ppermute | solution.py:1228
  25.5 2.0 %collective-permute-start.4 = (bf16[512,384]{1,0:T(8,128)(2,1)}, bf16[512,384]{1,0:T(8,128)(2,1)S(1)}, u32[]{:S(2)}, u32[]{:S(2)}) collective-permute-start(bf16[512,384]{1,0:T(8,128)(2,1)} %get-tuple-element.98.refs_1_.refs_9_), channel_id=1, source_target_pairs={{0,1},{1,0},{2,3},{3,2},{4,5},{5,4},{6,7},{7,6},{8,9},{9,8},{10,11... | collective-permute-start | bytes 1179656 | tf_op jit(solution)/shard_map/ppermute | solution.py:1228
  46.1 5.9 %collective-permute-start.5 = (bf16[512,768]{1,0:T(8,128)(2,1)}, bf16[512,768]{1,0:T(8,128)(2,1)S(1)}, u32[]{:S(2)}, u32[]{:S(2)}) collective-permute-start(bf16[512,768]{1,0:T(8,128)(2,1)} %get-tuple-element.101.refs_2_), channel_id=1, source_target_pairs={{0,1},{1,0},{2,3},{3,2},{4,5},{5,4},{6,7},{7,6},{8,9},{9,8},{10,11... | collective-permute-start | bytes 2359304 | tf_op jit(solution)/shard_map/ppermute | solution.py:1228
  46.3 24.3 %collective-permute-start.6 = (bf16[2,512,384]{2,1,0:T(8,128)(2,1)}, bf16[2,512,384]{2,1,0:T(8,128)(2,1)S(1)}, u32[]{:S(2)}, u32[]{:S(2)}) collective-permute-start(bf16[2,512,384]{2,1,0:T(8,128)(2,1)} %get-tuple-element.115), channel_id=1, source_target_pairs={{0,4},{4,0},{8,12},{12,8},{16,20},{20,16},{24,28},{28,24},{1,5},{5... | collective-permute-start | bytes 2359304 | tf_op jit(solution)/shard_map/ppermute | solution.py:1228
  48.2 2.3 %collective-permute-start.7 = (bf16[2,2,192,384]{3,2,1,0:T(8,128)(2,1)}, bf16[2,2,192,384]{3,2,1,0:T(8,128)(2,1)}, u32[]{:S(2)}, u32[]{:S(2)}) collective-permute-start(bf16[2,2,192,384]{3,2,1,0:T(8,128)(2,1)} %get-tuple-element.116), channel_id=1, source_target_pairs={{0,1},{1,0},{2,3},{3,2},{4,5},{5,4},{6,7},{7,6},{8,9},{9,8},{10,11... | collective-permute-start | bytes 1769480 | tf_op jit(solution)/shard_map/ppermute | solution.py:1228
  48.3 24.3 %collective-permute-start.9 = (bf16[2,2,2,160,384]{4,3,2,1,0:T(8,128)(2,1)}, bf16[2,2,2,160,384]{4,3,2,1,0:T(8,128)(2,1)S(1)}, u32[]{:S(2)}, u32[]{:S(2)}) collective-permute-start(bf16[2,2,2,160,384]{4,3,2,1,0:T(8,128)(2,1)} %get-tuple-element.117), channel_id=1, source_target_pairs={{0,8},{4,12},{8,0},{12,4},{16,24},{20,28},{24,16},{28,20},{1,9},{5... | collective-permute-start | bytes 2949128 | tf_op jit(solution)/shard_map/ppermute | solution.py:1228
  50.6 22.1 %collective-permute-start.8 = (bf16[2,2,192,384]{3,2,1,0:T(8,128)(2,1)}, bf16[2,2,192,384]{3,2,1,0:T(8,128)(2,1)S(1)}, u32[]{:S(2)}, u32[]{:S(2)}) collective-permute-start(bf16[2,2,192,384]{3,2,1,0:T(8,128)(2,1)} %collective-permute-done.7), channel_id=1, source_target_pairs={{0,2},{1,3},{2,0},{3,1},{4,6},{5,7},{6,4},{7,5},{8,10},{9,11},{10,... | collective-permute-start | bytes 1769480 | tf_op jit(solution)/shard_map/ppermute | solution.py:1228
  52.0 20.8 %collective-permute-start.12 = (bf16[2,2,192,384]{3,2,1,0:T(8,128)(2,1)}, bf16[2,2,192,384]{3,2,1,0:T(8,128)(2,1)S(1)}, u32[]{:S(2)}, u32[]{:S(2)}) collective-permute-start(bf16[2,2,192,384]{3,2,1,0:T(8,128)(2,1)} %get-tuple-element.124), channel_id=1, source_target_pairs={{0,1},{1,0},{2,3},{3,2},{4,5},{5,4},{6,7},{7,6},{8,9},{9,8},{10,11... | collective-permute-start | bytes 1769480 | tf_op jit(solution)/shard_map/ppermute | solution.py:1228
  70.0 2.6 %collective-permute-start.10 = (bf16[2,6,48,384]{3,2,1,0:T(8,128)(2,1)}, bf16[2,6,48,384]{3,2,1,0:T(8,128)(2,1)S(1)}, u32[]{:S(2)}, u32[]{:S(2)}) collective-permute-start(bf16[2,6,48,384]{3,2,1,0:T(8,128)(2,1)} %get-tuple-element.118), channel_id=1, source_target_pairs={{0,1},{1,0},{2,3},{3,2},{4,5},{5,4},{6,7},{7,6},{8,9},{9,8},{10,11... | collective-permute-start | bytes 1327112 | tf_op jit(solution)/shard_map/ppermute | solution.py:1228
  70.6 2.3 %copy-start.11 = (bf16[2,512,384]{2,1,0:T(8,128)(2,1)}, bf16[2,512,384]{2,1,0:T(8,128)(2,1)S(1)}, u32[]{:S(2)}) copy-start(bf16[2,512,384]{2,1,0:T(8,128)(2,1)S(1)} %collective-permute-done.6.refs_4_.refs_5_) | copy-start | bytes 2359300
  70.6 2.3 %collective-permute-start.11 = (bf16[2,6,48,384]{3,2,1,0:T(8,128)(2,1)}, bf16[2,6,48,384]{3,2,1,0:T(8,128)(2,1)S(1)}, u32[]{:S(2)}, u32[]{:S(2)}) collective-permute-start(bf16[2,6,48,384]{3,2,1,0:T(8,128)(2,1)} %get-tuple-element.119), channel_id=1, source_target_pairs={{0,1},{1,0},{2,3},{3,2},{4,5},{5,4},{6,7},{7,6},{8,9},{9,8},{10,11... | collective-permute-start | bytes 1327112 | tf_op jit(solution)/shard_map/ppermute | solution.py:1228
  72.6 1.4 copy-start.12
  72.6 1.5 copy-start.19
  72.9 19.3 %copy-start.14 = (bf16[2,6,48,384]{3,2,1,0:T(8,128)(2,1)}, bf16[2,6,48,384]{3,2,1,0:T(8,128)(2,1)S(1)}, u32[]{:S(2)}) copy-start(bf16[2,6,48,384]{3,2,1,0:T(8,128)(2,1)S(1)} %collective-permute-done.11.refs_7_.refs_4_) | copy-start | bytes 1327108
  72.9 1.2 copy-start.13
  78.3 26.0 %collective-permute-start.14 = (bf16[1216,384]{1,0:T(8,128)(2,1)}, bf16[1216,384]{1,0:T(8,128)(2,1)S(1)}, u32[]{:S(2)}, u32[]{:S(2)}) collective-permute-start(bf16[1216,384]{1,0:T(8,128)(2,1)} %get-tuple-element.134), channel_id=1, source_target_pairs={{0,2},{1,3},{2,0},{3,1},{4,6},{5,7},{6,4},{7,5},{8,10},{9,11},{10,... | collective-permute-start | bytes 2801672 | tf_op jit(solution)/shard_map/ppermute | solution.py:1228
  79.8 24.5 %collective-permute-start.15 = (bf16[1216,384]{1,0:T(8,128)(2,1)}, bf16[1216,384]{1,0:T(8,128)(2,1)S(1)}, u32[]{:S(2)}, u32[]{:S(2)}) collective-permute-start(bf16[1216,384]{1,0:T(8,128)(2,1)} %get-tuple-element.128), channel_id=1, source_target_pairs={{0,4},{4,0},{8,12},{12,8},{16,20},{20,16},{24,28},{28,24},{1,5},{5... | collective-permute-start | bytes 2801672 | tf_op jit(solution)/shard_map/ppermute | solution.py:1228
  80.4 24.0 %collective-permute-start.13 = (bf16[2,2,160,384]{3,2,1,0:T(8,128)(2,1)}, bf16[2,2,160,384]{3,2,1,0:T(8,128)(2,1)S(1)}, u32[]{:S(2)}, u32[]{:S(2)}) collective-permute-start(bf16[2,2,160,384]{3,2,1,0:T(8,128)(2,1)} %get-tuple-element.133), channel_id=1, source_target_pairs={{0,16},{4,20},{8,24},{12,28},{16,0},{20,4},{24,8},{28,12},{1,17},{... | collective-permute-start | bytes 1474568 | tf_op jit(solution)/shard_map/ppermute | solution.py:1228
  92.2 10.9 %collective-permute-start.17 = (f32[16,768]{1,0:T(8,128)}, f32[16,768]{1,0:T(8,128)S(1)}, u32[]{:S(2)}, u32[]{:S(2)}) collective-permute-start(f32[16,768]{1,0:T(8,128)} %get-tuple-element.135.refs_9_), channel_id=1, source_target_pairs={{0,4},{4,0},{8,12},{12,8},{16,20},{20,16},{24,28},{28,24},{1,5},{5... | collective-permute-start | bytes 147464 | tf_op jit(solution)/shard_map/ppermute | solution.py:1228
  93.8 9.4 %collective-permute-start.16 = (f32[16,768]{1,0:T(8,128)}, f32[16,768]{1,0:T(8,128)S(1)}, u32[]{:S(2)}, u32[]{:S(2)}) collective-permute-start(f32[16,768]{1,0:T(8,128)} %get-tuple-element.135.refs_9_), channel_id=1, source_target_pairs={{0,1},{1,0},{2,3},{3,2},{4,5},{5,4},{6,7},{7,6},{8,9},{9,8},{10,11... | collective-permute-start | bytes 147464 | tf_op jit(solution)/shard_map/ppermute | solution.py:1228
  103.1 1.3 copy-start.26
  103.1 1.2 collective-permute-start.18
  103.1 1.3 copy-start.27
  104.3 17.7 %copy-start.18 = (bf16[2,2,160,384]{3,2,1,0:T(8,128)(2,1)}, bf16[2,2,160,384]{3,2,1,0:T(8,128)(2,1)S(1)}, u32[]{:S(2)}) copy-start(bf16[2,2,160,384]{3,2,1,0:T(8,128)(2,1)S(1)} %collective-permute-done.13.refs_14_) | copy-start | bytes 1474564
  104.3 1.1 copy-start.9
  104.4 1.3 copy-start.6
  105.6 4.3 %copy-start.29 = (bf16[768,768]{1,0:T(8,128)(2,1)S(1)}, bf16[768,768]{1,0:T(8,128)(2,1)}, u32[]{:S(2)}) copy-start(bf16[768,768]{1,0:T(8,128)(2,1)} %get-tuple-element.149) | copy-start | bytes 3538948
  110.0 12.1 %collective-permute-start.22 = (bf16[768,768]{1,0:T(8,128)(2,1)S(1)}, bf16[768,768]{1,0:T(8,128)(2,1)S(1)}, u32[]{:S(2)}, u32[]{:S(2)}) collective-permute-start(bf16[768,768]{1,0:T(8,128)(2,1)S(1)} %copy-done.29), channel_id=1, source_target_pairs={{0,1},{1,0},{2,3},{3,2},{4,5},{5,4},{6,7},{7,6},{8,9},{9,8},{10,11... | collective-permute-start | bytes 3538952 | tf_op jit(solution)/shard_map/ppermute | solution.py:1228
  110.2 10.9 %collective-permute-start.19 = (bf16[2,224,384]{2,1,0:T(8,128)(2,1)}, bf16[2,224,384]{2,1,0:T(8,128)(2,1)S(1)}, u32[]{:S(2)}, u32[]{:S(2)}) collective-permute-start(bf16[2,224,384]{2,1,0:T(8,128)(2,1)} %get-tuple-element.144), channel_id=1, source_target_pairs={{0,8},{4,12},{8,0},{12,4},{16,24},{20,28},{24,16},{28,20},{1,9},{5... | collective-permute-start | bytes 1032200 | tf_op jit(solution)/shard_map/ppermute | solution.py:1228
  111.8 10.2 %collective-permute-start.20 = (bf16[448,384]{1,0:T(8,128)(2,1)}, bf16[448,384]{1,0:T(8,128)(2,1)S(1)}, u32[]{:S(2)}, u32[]{:S(2)}) collective-permute-start(bf16[448,384]{1,0:T(8,128)(2,1)} %get-tuple-element.145.refs_9_), channel_id=1, source_target_pairs={{0,2},{1,3},{2,0},{3,1},{4,6},{5,7},{6,4},{7,5},{8,10},{9,11},{10,... | collective-permute-start | bytes 1032200 | tf_op jit(solution)/shard_map/ppermute | solution.py:1228
  112.7 8.4 %collective-permute-start.21 = (bf16[352,384]{1,0:T(8,128)(2,1)}, bf16[352,384]{1,0:T(8,128)(2,1)S(1)}, u32[]{:S(2)}, u32[]{:S(2)}) collective-permute-start(bf16[352,384]{1,0:T(8,128)(2,1)} %get-tuple-element.146), channel_id=1, source_target_pairs={{0,4},{4,0},{8,12},{12,8},{16,20},{20,16},{24,28},{28,24},{1,5},{5... | collective-permute-start | bytes 811016 | tf_op jit(solution)/shard_map/ppermute | solution.py:1228
  121.1 1.0 copy-start.23
  122.0 1.2 copy-start.7
  123.2 17.3 %copy-start.3 = (s32[1,5]{1,0:T(1,128)S(1)}, s32[1,5]{1,0:T(1,128)}, u32[]{:S(2)}) copy-start(s32[1,5]{1,0:T(1,128)} %refs_0_.21) | copy-start | bytes 64
  123.2 17.3 %copy-start.5 = (s32[96]{0:T(128)S(1)}, s32[96]{0:T(128)}, u32[]{:S(2)}) copy-start(s32[96]{0:T(128)} %constant.2.clone.refs_1_) | copy-start | bytes 1156
  127.8 12.6 %collective-permute-start.23 = (bf16[416,384]{1,0:T(8,128)(2,1)}, bf16[416,384]{1,0:T(8,128)(2,1)S(1)}, u32[]{:S(2)}, u32[]{:S(2)}) collective-permute-start(bf16[416,384]{1,0:T(8,128)(2,1)} %get-tuple-element.157), channel_id=1, source_target_pairs={{0,8},{4,12},{8,0},{12,4},{16,24},{20,28},{24,16},{28,20},{1,9},{5... | collective-permute-start | bytes 958472 | tf_op jit(solution)/shard_map/ppermute | solution.py:1228
  128.3 9.1 %collective-permute-start.24 = (bf16[2,160,384]{2,1,0:T(8,128)(2,1)}, bf16[2,160,384]{2,1,0:T(8,128)(2,1)S(1)}, u32[]{:S(2)}, u32[]{:S(2)}) collective-permute-start(bf16[2,160,384]{2,1,0:T(8,128)(2,1)} %get-tuple-element.159), channel_id=1, source_target_pairs={{0,2},{1,3},{2,0},{3,1},{4,6},{5,7},{6,4},{7,5},{8,10},{9,11},{10,... | collective-permute-start | bytes 737288 | tf_op jit(solution)/shard_map/ppermute | solution.py:1228
  129.6 17.3 %collective-permute-start.25 = (bf16[256,768]{1,0:T(8,128)(2,1)}, bf16[256,768]{1,0:T(8,128)(2,1)S(1)}, u32[]{:S(2)}, u32[]{:S(2)}) collective-permute-start(bf16[256,768]{1,0:T(8,128)(2,1)} %get-tuple-element.161), channel_id=1, source_target_pairs={{0,2},{1,3},{2,0},{3,1},{4,6},{5,7},{6,4},{7,5},{8,10},{9,11},{10,... | collective-permute-start | bytes 1179656 | tf_op jit(solution)/shard_map/ppermute | solution.py:1228
  130.3 22.1 %collective-permute-start.26 = (bf16[224,384]{1,0:T(8,128)(2,1)}, bf16[224,384]{1,0:T(8,128)(2,1)S(1)}, u32[]{:S(2)}, u32[]{:S(2)}) collective-permute-start(bf16[224,384]{1,0:T(8,128)(2,1)} %get-tuple-element.169), channel_id=1, source_target_pairs={{0,16},{4,20},{8,24},{12,28},{16,0},{20,4},{24,8},{28,12},{1,17},{... | collective-permute-start | bytes 516104 | tf_op jit(solution)/shard_map/ppermute | solution.py:1228
  140.5 1.0 copy-start
  144.8 8.8 %collective-permute-start.28 = (bf16[224,384]{1,0:T(8,128)(2,1)S(1)}, bf16[224,384]{1,0:T(8,128)(2,1)S(1)}, u32[]{:S(2)}, u32[]{:S(2)}) collective-permute-start(bf16[224,384]{1,0:T(8,128)(2,1)S(1)} %get-tuple-element.171), channel_id=1, source_target_pairs={{0,16},{4,20},{8,24},{12,28},{16,0},{20,4},{24,8},{28,12},{1,17},{... | collective-permute-start | bytes 516104 | tf_op jit(solution)/shard_map/ppermute | solution.py:1228
  145.5 6.9 %collective-permute-start.27 = (bf16[160,384]{1,0:T(8,128)(2,1)S(1)}, bf16[160,384]{1,0:T(8,128)(2,1)S(1)}, u32[]{:S(2)}, u32[]{:S(2)}) collective-permute-start(bf16[160,384]{1,0:T(8,128)(2,1)S(1)} %get-tuple-element.170), channel_id=1, source_target_pairs={{0,4},{4,0},{8,12},{12,8},{16,20},{20,16},{24,28},{28,24},{1,5},{5... | collective-permute-start | bytes 368648 | tf_op jit(solution)/shard_map/ppermute | solution.py:1228
  147.6 6.0 %copy-start.2 = (bf16[224,384]{1,0:T(8,128)(2,1)S(1)}, bf16[224,384]{1,0:T(8,128)(2,1)}, u32[]{:S(2)}) copy-start(bf16[224,384]{1,0:T(8,128)(2,1)} %get-tuple-element.168.refs_1_) | copy-start | bytes 516100
  147.6 6.0 %copy-start.4 = (s32[1,5]{1,0:T(1,128)S(1)}, s32[1,5]{1,0:T(1,128)}, u32[]{:S(2)}) copy-start(s32[1,5]{1,0:T(1,128)} %refs_0_.21) | copy-start | bytes 64
  (11 other events, 9.0 us)
where the time goes:
time: 158 us; the launch traced here: 157 us
  Pallas kernels  85.4 us (54%)
  waiting for transfers between devices  33.9 us (21%)
  starting transfers between devices  26.8 us (17%)
  local copies, waits for them, and re-layouts  9.57 us (6%)
    pallas_call x11, Pallas kernels, staged_call(): pl.pallas_call(kernel, in_specs=[pl.BlockSpec(memory_space=pltpu.SMEM)] *...  85.4 us
    ppermute x29, waiting for transfers between devices, swapped(): return lax.ppermute(array, axis, [(i, i ^ bit) for i in range(length)])  33.9 us
    ppermute x29, starting transfers between devices, swapped(): return lax.ppermute(array, axis, [(i, i ^ bit) for i in range(length)])  26.8 us
    unnamed x60, local copies, waits for them, and re-layouts  9.57 us
  transfers between devices with their start and end apart: 29, of which 12 were waited for; matrix products, arithmetic and copies ran while one was open for 0% of the time, Pallas kernels for 27%

commit v1 on v0

--- a/solution.py
+++ b/solution.py
@@ -290,6 +290,7 @@
 MASKED = -1e30
 GRANT = 60 * 1024 * 1024
 STEP_GRANT = 20 * 1024 * 1024
+LATE_GRANT = 32 * 1024 * 1024
 WIDE_CHUNK = 128
 
 
@@ -743,14 +744,19 @@
 
     def hidden(index):
         rel_x = 1 - index
+        count = normed.shape[0] // 2
         for side in range(2):
             at = lanes_at(2 * rel_x + side, piece)
-            before = dot_nn(normed[...], up_ref[:, at]) + bias_ref[pl.ds(hidden_unit(where_ref, rel_x, side), 1)]
-            act, slope = gelu_with_slope(before)
-            act_ref[:, at] = act.astype(BF)
-            dbefore = (dact_ref[:, at].astype(F32) * slope).astype(BF)
-            dbefore_ref[:, at] = dbefore
-            bias_sum_ref[:, at] = column_sum(dbefore.astype(F32))
+            bias = bias_ref[pl.ds(hidden_unit(where_ref, rel_x, side), 1)]
+            total = jnp.zeros((1, piece), F32)
+            for part in range(2):
+                here = slice(part * count, (part + 1) * count)
+                act, slope = gelu_with_slope(dot_nn(normed[here], up_ref[:, at]) + bias)
+                act_ref[here, at] = act.astype(BF)
+                dbefore = (dact_ref[here, at].astype(F32) * slope).astype(BF)
+                dbefore_ref[here, at] = dbefore
+                total = total + column_sum(dbefore.astype(F32))
+            bias_sum_ref[:, at] = total
             grad[:, side * piece : (side + 1) * piece] = dot_nn(turned_ref[...], act_ref[:, at]).astype(BF)
 
         def lay(index):
@@ -779,7 +785,8 @@
             py_ref[rel_y, rel_x, to] = grad[lanes_at(own_block(where_ref, rel_x, 0), block), :piece]
             ux_ref[rel_x, rel_y, high_z] = grad[lanes_at(own_block(where_ref, rel_x, 1), block), :piece]
 
-    each(4, up)
+    for index in range(4):
+        up(index)
     stage.put(0, 1, 2, 3)
 
     def back(index):
@@ -950,7 +957,8 @@
                 dvalues_ref[to, lanes] = dv[at].astype(BF)
         return carry
 
-    lax.fori_loop(0, half // (2 * HEAD_SIZE), pair, 0)
+    for index in range(half // (2 * HEAD_SIZE)):
+        pair(index, 0)
 
 
 def twice(half_row, where_ref):
@@ -1443,6 +1451,7 @@
         [low(rows, width), low(rows, width), low(3 * rows, width), full(rows, width), full(16, width)],
         cuts={3: all_columns, 8: down_rows},
         scratch=[rows_of_vec],
+        grant=LATE_GRANT,
     )
     sums_core, sums_y = to_core(sums), to_y(sums)
     sums_far = to_core(sums_y)
@@ -1451,7 +1460,7 @@
     )
 
     rest = 4 * unit_rows - 64
-    mlp_send, b_step, a_step, mlp_keep = staged_call(
+    mlp_send, b_step, a_step, mlp_keep = step(
         third_step_kernel,
         where,
         (ux_keep, ux_got, y_got, py_keep, py_got, x_got, b_keep, o_keep, sums, sums_core, sums_y, sums_far, a_keep),
@@ -1465,7 +1474,7 @@
     mlp_got, b_far, a_far, late_got = lax.optimization_barrier((mlp_got, b_far, a_far, late_got))
 
     first = 2 * block + 2 * six
-    last_send, mlp_step, dz_step, mlp_kept, last_keep, dz_kept, dtok_step = staged_call(
+    last_send, mlp_step, dz_step, mlp_kept, last_keep, dz_kept, dtok_step = step(
         fourth_step_kernel,
         where,
         (a_keep, x_got, a_far, b_keep, y_got, b_far, o_keep, y_got, b_step, mlp_keep, mlp_got, dz_keep, dz_got, dz_far,
@@ -1496,6 +1505,7 @@
         [low(rows, width), low(rows, width)],
         cuts={1: ((both, width), 2, first_and_last_rows(rows))},
         scratch=[rows_of_vec],
+        grant=STEP_GRANT,
     )
 
     mlp_far, dz_y, last_far = after(grad_tokens, mlp_far, dz_y, last_far)

time: 158 us -> 155 us (0.981)
  local copies, waits for them, and re-layouts: 9.57 us -> 15.4 us
  waiting for transfers between devices: 33.9 us -> 30.1 us
  Pallas kernels: 85.4 us -> 82.6 us
  starting transfers between devices: 26.8 us -> 24.3 us
    unnamed x60 -> x80, local copies, waits for them, and re-layouts: 9.57 us -> 15.4 us
    ppermute x29, waiting for transfers between devices: 33.9 us -> 30.1 us  [swapped(): return lax.ppermute(array, axis, [(i, i ^ bit) for i in range(length)])]
    pallas_call x11, Pallas kernels: 85.4 us -> 82.6 us  [staged_call(): pl.pallas_call(kernel, in_specs=[pl.BlockSpec(memory_space=pltpu.SMEM)] *...]
    ppermute x29, starting transfers between devices: 26.8 us -> 24.3 us  [swapped(): return lax.ppermute(array, axis, [(i, i ^ bit) for i in range(length)])]
  transfers between devices with their start and end apart: 29 -> 29, of which waited for: 12 -> 11; matrix products, arithmetic and copies ran while one was open for 0% -> 0% of each run, Pallas kernels for 27% -> 26%
where the time goes in v1:
time: 155 us; the launch traced here: 154 us
  Pallas kernels  82.6 us (53%)
  waiting for transfers between devices  30.1 us (19%)
  starting transfers between devices  24.3 us (16%)
  local copies, waits for them, and re-layouts  15.4 us (10%)
    pallas_call x11, Pallas kernels, staged_call(): pl.pallas_call(kernel, in_specs=[pl.BlockSpec(memory_space=pltpu.SMEM)] *...  82.6 us
    ppermute x29, waiting for transfers between devices, swapped(): return lax.ppermute(array, axis, [(i, i ^ bit) for i in range(length)])  30.1 us
    ppermute x29, starting transfers between devices, swapped(): return lax.ppermute(array, axis, [(i, i ^ bit) for i in range(length)])  24.3 us
    unnamed x80, local copies, waits for them, and re-layouts  15.4 us
  transfers between devices with their start and end apart: 29, of which 11 were waited for; matrix products, arithmetic and copies ran while one was open for 0% of the time, Pallas kernels for 26%

profile of v1, /device:TPU:0, one launch (start us, length us, event | category | flops | bytes accessed | tf_op | source)
XLA Modules:
  0.0 154.1 jit_solution(2662241545115896421)
XLA Ops:
  1.2 2.9 %collective-permute-start = (bf16[256,768]{1,0:T(8,128)(2,1)}, bf16[256,768]{1,0:T(8,128)(2,1)S(1)}, u32[]{:S(2)}, u32[]{:S(2)}) collective-permute-start(bf16[256,768]{1,0:T(8,128)(2,1)} %bitcast.11), channel_id=1, source_target_pairs={{0,2},{1,3},{2,0},{3,1},{4,6},{5,7},{6,4},{7,5},{8,10},{9,11},{10,... | collective-permute-start | bytes 1179656 | tf_op jit(solution)/shard_map/ppermute | solution.py:1236
  4.2 0.8 copy-done.35
  5.1 9.2 %shard_map.144 = (bf16[512,768]{1,0:T(8,128)(2,1)}, bf16[512,1152]{1,0:T(8,128)(2,1)}, bf16[512,1536]{1,0:T(8,128)(2,1)}, bf16[768,512]{1,0:T(8,128)(2,1)}, f32[1,768]{1,0:T(1,128)}) custom-call(s32[1,5]{1,0:T(1,128)} %refs_0_.21, bf16[256,768]{1,0:T(8,128)(2,1)} %bitcast.12, bf16[256,768]{1,0:T(8,128)(2,1)} %copy-done.35, f32[84,128]{1,0:T(8,128)} %bitcast.15, ...), custom_call_target="tpu_custom_call" | custom-call | tf_op jit(solution)/shard_map/pallas_call | solution.py:475
  14.3 1.7 %collective-permute-done.3.refs_2_ = bf16[256,768]{1,0:T(8,128)(2,1)S(1)} collective-permute-done((bf16[256,768]{1,0:T(8,128)(2,1)S(1)}, bf16[256,768]{1,0:T(8,128)(2,1)S(1)}, u32[]{:S(2)}, u32[]{:S(2)}) %collective-permute-start.3) | collective-permute-done | bytes 393248 | tf_op jit(solution)/shard_map/ppermute | solution.py:1236
  16.0 0.7 copy-done.39
  16.8 8.9 %shard_map.145 = (bf16[512,768]{1,0:T(8,128)(2,1)}, bf16[1024,768]{1,0:T(8,128)(2,1)}, bf16[512,384]{1,0:T(8,128)(2,1)}, f32[3,4,256]{2,1,0:T(4,128)}) custom-call(s32[1,5]{1,0:T(1,128)} %refs_0_.21, bf16[256,768]{1,0:T(8,128)(2,1)} %copy-done.38, bf16[256,768]{1,0:T(8,128)(2,1)} %copy-done.39, f32[84,128]{1,0:T(8,128)} %bitcast.16, ...), custom_call_target="tpu_custom_call" | custom-call | tf_op jit(solution)/shard_map/pallas_call | solution.py:475
  25.9 1.8 %collective-permute-done.4.refs_2_.refs_10_ = bf16[512,384]{1,0:T(8,128)(2,1)S(1)} collective-permute-done((bf16[512,384]{1,0:T(8,128)(2,1)}, bf16[512,384]{1,0:T(8,128)(2,1)S(1)}, u32[]{:S(2)}, u32[]{:S(2)}) %collective-permute-start.4) | collective-permute-done | bytes 393248 | tf_op jit(solution)/shard_map/ppermute | solution.py:1236
  27.7 0.7 copy-done.34
  28.4 16.9 %shard_map.146 = (bf16[2,512,384]{2,1,0:T(8,128)(2,1)}, bf16[2,512,384]{2,1,0:T(8,128)(2,1)}, bf16[2,2,192,384]{3,2,1,0:T(8,128)(2,1)}, bf16[2,2,192,384]{3,2,1,...) custom-call(s32[1,5]{1,0:T(1,128)} %refs_0_.21, ...), custom_call_target="tpu_custom_call" | custom-call | tf_op jit(solution)/shard_map/pallas_call | solution.py:475
  45.5 1.9 %collective-permute-start.6 = (bf16[2,512,384]{2,1,0:T(8,128)(2,1)}, bf16[2,512,384]{2,1,0:T(8,128)(2,1)S(1)}, u32[]{:S(2)}, u32[]{:S(2)}) collective-permute-start(bf16[2,512,384]{2,1,0:T(8,128)(2,1)} %get-tuple-element.115), channel_id=1, source_target_pairs={{0,4},{4,0},{8,12},{12,8},{16,20},{20,16},{24,28},{28,24},{1,5},{5... | collective-permute-start | bytes 2359304 | tf_op jit(solution)/shard_map/ppermute | solution.py:1236
  47.4 1.6 %collective-permute-start.9 = (bf16[2,2,2,160,384]{4,3,2,1,0:T(8,128)(2,1)}, bf16[2,2,2,160,384]{4,3,2,1,0:T(8,128)(2,1)S(1)}, u32[]{:S(2)}, u32[]{:S(2)}) collective-permute-start(bf16[2,2,2,160,384]{4,3,2,1,0:T(8,128)(2,1)} %get-tuple-element.117), channel_id=1, source_target_pairs={{0,8},{4,12},{8,0},{12,4},{16,24},{20,28},{24,16},{28,20},{1,9},{5... | collective-permute-start | bytes 2949128 | tf_op jit(solution)/shard_map/ppermute | solution.py:1236
  49.0 0.7 collective-permute-done.7
  49.7 1.5 collective-permute-start.8
  51.2 0.9 copy-done.36
  52.1 16.8 %shard_map.147 = (f32[256,768]{1,0:T(8,128)}, bf16[2,352,384]{2,1,0:T(8,128)(2,1)}, bf16[2,352,384]{2,1,0:T(8,128)(2,1)}, bf16[2,6,48,384]{3,2,1,0:T(8,128)(2,1)...) custom-call(s32[1,5]{1,0:T(1,128)} %refs_0_.21, ...), custom_call_target="tpu_custom_call" | custom-call | tf_op jit(solution)/shard_map/pallas_call | solution.py:475
  69.6 2.2 %collective-permute-done.9.refs_2_.refs_13_ = bf16[2,2,2,160,384]{4,3,2,1,0:T(8,128)(2,1)S(1)} collective-permute-done((bf16[2,2,2,160,384]{4,3,2,1,0:T(8,128)(2,1)}, bf16[2,2,2,160,384]{4,3,2,1,0:T(8,128)(2,1)S(1)}, u32[]{:S(2)}, u32[]{:S(2)}) %collective-permute-start.9) | collective-permute-done | bytes 983072 | tf_op jit(solution)/shard_map/ppermute | solution.py:1236
  71.8 0.8 copy-done.19
  73.6 4.7 %shard_map.148 = (bf16[2,2,160,384]{3,2,1,0:T(8,128)(2,1)}, bf16[1216,384]{1,0:T(8,128)(2,1)}, bf16[1216,384]{1,0:T(8,128)(2,1)}) custom-call(s32[1,5]{1,0:T(1,128)} %refs_0_.21, bf16[2,2,2,160,384]{4,3,2,1,0:T(8,128)(2,1)} %get-tuple-element.113.refs_1_.refs_12_, bf16[2,2,2,160,384]{4,3,2,1,0:T(8,128)(2,1)} %copy-done.3, ...), custom_call_target="tpu_custom_call" | custom-call | tf_op jit(solution)/shard_map/pallas_call | solution.py:475
  78.3 1.6 %collective-permute-start.14 = (bf16[1216,384]{1,0:T(8,128)(2,1)}, bf16[1216,384]{1,0:T(8,128)(2,1)S(1)}, u32[]{:S(2)}, u32[]{:S(2)}) collective-permute-start(bf16[1216,384]{1,0:T(8,128)(2,1)} %get-tuple-element.134), channel_id=1, source_target_pairs={{0,2},{1,3},{2,0},{3,1},{4,6},{5,7},{6,4},{7,5},{8,10},{9,11},{10,... | collective-permute-start | bytes 2801672 | tf_op jit(solution)/shard_map/ppermute | solution.py:1236
  80.4 2.6 %collective-permute-start.13 = (bf16[2,2,160,384]{3,2,1,0:T(8,128)(2,1)}, bf16[2,2,160,384]{3,2,1,0:T(8,128)(2,1)S(1)}, u32[]{:S(2)}, u32[]{:S(2)}) collective-permute-start(bf16[2,2,160,384]{3,2,1,0:T(8,128)(2,1)} %get-tuple-element.133), channel_id=1, source_target_pairs={{0,16},{4,20},{8,24},{12,28},{16,0},{20,4},{24,8},{28,12},{1,17},{... | collective-permute-start | bytes 1474568 | tf_op jit(solution)/shard_map/ppermute | solution.py:1236
  83.0 2.3 %copy-done.1 = bf16[3072,768]{1,0:T(8,128)(2,1)S(1)} copy-done((bf16[3072,768]{1,0:T(8,128)(2,1)S(1)}, bf16[3072,768]{1,0:T(8,128)(2,1)}, u32[]{:S(2)}) %copy-start.1) | copy-done | bytes 4718616
  85.4 1.0 copy-done.7
  86.4 1.1 copy-done.10
  87.5 1.1 copy-done.13
  88.6 1.4 copy-done.22
  90.0 1.1 copy-done.23
  91.2 1.1 copy-done.24
  92.3 1.0 copy-done.28
  93.3 8.3 %shard_map.149 = (bf16[256,768]{1,0:T(8,128)(2,1)S(1)}, bf16[256,768]{1,0:T(8,128)(2,1)S(1)}, bf16[768,768]{1,0:T(8,128)(2,1)S(1)}, f32[256,768]{1,0:T(8,128)S(1)}, f32[16,768]{1,0:T(8,128)S(1)}) custom-call(s32[1,5]{1,0:T(1,128)S(1)} %copy-done.29, bf16[512,384]{1,0:T(8,128)(2,1)S(1)} %copy-done.28, bf16[1024,384]{1,0:T(8,128)(2,1)S(1)} %copy-done.23, ...), custom_call_target="tpu_custom_call" | custom-call | tf_op jit(solution)/shard_map/pallas_call | solution.py:475
  101.7 1.6 %collective-permute-start.17 = (f32[16,768]{1,0:T(8,128)S(1)}, f32[16,768]{1,0:T(8,128)S(1)}, u32[]{:S(2)}, u32[]{:S(2)}) collective-permute-start(f32[16,768]{1,0:T(8,128)S(1)} %get-tuple-element.135.refs_9_), channel_id=1, source_target_pairs={{0,4},{4,0},{8,12},{12,8},{16,20},{20,16},{24,28},{28,24},{1,5},{5... | collective-permute-start | bytes 147464 | tf_op jit(solution)/shard_map/ppermute | solution.py:1236
  103.3 2.6 %collective-permute-done.17.refs_11_ = f32[16,768]{1,0:T(8,128)S(1)} collective-permute-done((f32[16,768]{1,0:T(8,128)S(1)}, f32[16,768]{1,0:T(8,128)S(1)}, u32[]{:S(2)}, u32[]{:S(2)}) %collective-permute-start.17) | collective-permute-done | bytes 49184 | tf_op jit(solution)/shard_map/ppermute | solution.py:1236
  105.8 1.2 collective-permute-done.18.refs_12_
  107.2 3.3 %shard_map.150 = (bf16[2,224,384]{2,1,0:T(8,128)(2,1)S(1)}, bf16[448,384]{1,0:T(8,128)(2,1)S(1)}, bf16[352,384]{1,0:T(8,128)(2,1)S(1)}, bf16[2,224,384]{2,1,0:T(8,128)(2,1)S(1)}) custom-call(s32[1,5]{1,0:T(1,128)S(1)} %copy-done.29, bf16[2,2,192,384]{3,2,1,0:T(8,128)(2,1)S(1)} %copy-done.17, bf16[2,2,192,384]{3,2,1,0:T(8,128)(2,1)S(1)} %copy-done.15, ...), custom_call_target="tpu_custom_call" | custom-call | tf_op jit(solution)/shard_map/pallas_call | solution.py:475
  110.7 1.6 %collective-permute-start.19 = (bf16[2,224,384]{2,1,0:T(8,128)(2,1)S(1)}, bf16[2,224,384]{2,1,0:T(8,128)(2,1)S(1)}, u32[]{:S(2)}, u32[]{:S(2)}) collective-permute-start(bf16[2,224,384]{2,1,0:T(8,128)(2,1)S(1)} %get-tuple-element.144), channel_id=1, source_target_pairs={{0,8},{4,12},{8,0},{12,4},{16,24},{20,28},{24,16},{28,20},{1,9},{5... | collective-permute-start | bytes 1032200 | tf_op jit(solution)/shard_map/ppermute | solution.py:1236
  112.2 1.1 collective-permute-start.20
  113.4 0.9 collective-permute-start.21
  114.3 7.3 %collective-permute-done.21.refs_3_ = bf16[352,384]{1,0:T(8,128)(2,1)S(1)} collective-permute-done((bf16[352,384]{1,0:T(8,128)(2,1)S(1)}, bf16[352,384]{1,0:T(8,128)(2,1)S(1)}, u32[]{:S(2)}, u32[]{:S(2)}) %collective-permute-start.21) | collective-permute-done | bytes 270368 | tf_op jit(solution)/shard_map/ppermute | solution.py:1236
  121.6 0.7 collective-permute-done.20.refs_6_
  122.3 5.7 %shard_map.151 = (bf16[416,384]{1,0:T(8,128)(2,1)S(1)}, bf16[224,384]{1,0:T(8,128)(2,1)S(1)}, bf16[2,160,384]{2,1,0:T(8,128)(2,1)S(1)}, bf16[224,384]{1,0:T(8,12...) custom-call(s32[1,5]{1,0:T(1,128)S(1)} %copy-done.29, ...), custom_call_target="tpu_custom_call" | custom-call | tf_op jit(solution)/shard_map/pallas_call | solution.py:475
  128.6 1.1 collective-permute-start.24
  129.7 0.9 collective-permute-start.25
  130.9 6.5 %collective-permute-done.24.refs_5_ = bf16[2,160,384]{2,1,0:T(8,128)(2,1)S(1)} collective-permute-done((bf16[2,160,384]{2,1,0:T(8,128)(2,1)S(1)}, bf16[2,160,384]{2,1,0:T(8,128)(2,1)S(1)}, u32[]{:S(2)}, u32[]{:S(2)}) %collective-permute-start.24) | collective-permute-done | bytes 245792 | tf_op jit(solution)/shard_map/ppermute | solution.py:1236
  137.5 2.9 %collective-permute-done.23.refs_3_ = bf16[416,384]{1,0:T(8,128)(2,1)S(1)} collective-permute-done((bf16[416,384]{1,0:T(8,128)(2,1)S(1)}, bf16[416,384]{1,0:T(8,128)(2,1)S(1)}, u32[]{:S(2)}, u32[]{:S(2)}) %collective-permute-start.23) | collective-permute-done | bytes 319520 | tf_op jit(solution)/shard_map/ppermute | solution.py:1236
  140.4 2.4 %shard_map.152 = (bf16[224,384]{1,0:T(8,128)(2,1)S(1)}, bf16[160,384]{1,0:T(8,128)(2,1)S(1)}, bf16[224,384]{1,0:T(8,128)(2,1)S(1)}, bf16[160,384]{1,0:T(8,128)(2,1)S(1)}) custom-call(s32[1,5]{1,0:T(1,128)S(1)} %copy-done.29, s32[96]{0:T(128)S(1)} %copy-done.33, bf16[416,384]{1,0:T(8,128)(2,1)S(1)} %get-tuple-element.156.refs_2_, ...), custom_call_target="tpu_custom_call" | custom-call | tf_op jit(solution)/shard_map/pallas_call | solution.py:475
  142.9 1.6 %collective-permute-start.27 = (bf16[160,384]{1,0:T(8,128)(2,1)S(1)}, bf16[160,384]{1,0:T(8,128)(2,1)S(1)}, u32[]{:S(2)}, u32[]{:S(2)}) collective-permute-start(bf16[160,384]{1,0:T(8,128)(2,1)S(1)} %get-tuple-element.170), channel_id=1, source_target_pairs={{0,4},{4,0},{8,12},{12,8},{16,20},{20,16},{24,28},{28,24},{1,5},{5... | collective-permute-start | bytes 368648 | tf_op jit(solution)/shard_map/ppermute | solution.py:1236
  144.5 3.5 %shard_map.153 = (bf16[256,768]{1,0:T(8,128)(2,1)}, bf16[256,768]{1,0:T(8,128)(2,1)}) custom-call(s32[1,5]{1,0:T(1,128)S(1)} %copy-done.29, bf16[256,768]{1,0:T(8,128)(2,1)S(1)} %get-tuple-element.132.refs_1_, bf16[768,768]{1,0:T(8,128)(2,1)S(1)} %collective-permute-done.22.refs_16_.refs_2_, bf16[256,768]{1,0:T(8,128)(2,1)S(1)} %collective-permute-done.25.refs_3_, ...), custom_call_target="tpu_custom_call" | custom-call | tf_op jit(solution)/shard_map/pallas_call | solution.py:475
  148.0 2.5 %collective-permute-done.28.refs_6_ = bf16[224,384]{1,0:T(8,128)(2,1)S(1)} collective-permute-done((bf16[224,384]{1,0:T(8,128)(2,1)S(1)}, bf16[224,384]{1,0:T(8,128)(2,1)S(1)}, u32[]{:S(2)}, u32[]{:S(2)}) %collective-permute-start.28) | collective-permute-done | bytes 172064 | tf_op jit(solution)/shard_map/ppermute | solution.py:1236
  150.5 3.0 %shard_map.154 = (f32[96,768]{1,0:T(8,128)}, f32[192,384]{1,0:T(8,128)}, f32[192,96]{1,0:T(8,128)}, f32[1,336]{1,0:T(1,128)S(1)}, f32[192,288]{1,0:T(8,128)}) custom-call(s32[1,5]{1,0:T(1,128)S(1)} %copy-done.29, bf16[224,384]{1,0:T(8,128)(2,1)S(1)} %get-tuple-element.168.refs_1_, bf16[224,384]{1,0:T(8,128)(2,1)S(1)} %collective-permute-done.26.refs_2_, ...), custom_call_target="tpu_custom_call" | custom-call | tf_op jit(solution)/shard_map/pallas_call | solution.py:475
  (102 shorter events, 5.3 us)
Async XLA Ops:
  0.6 3.5 %collective-permute-start.1 = (bf16[256,768]{1,0:T(8,128)(2,1)}, bf16[256,768]{1,0:T(8,128)(2,1)S(1)}, u32[]{:S(2)}, u32[]{:S(2)}) collective-permute-start(bf16[256,768]{1,0:T(8,128)(2,1)} %bitcast.10), channel_id=1, source_target_pairs={{0,1},{1,0},{2,3},{3,2},{4,5},{5,4},{6,7},{7,6},{8,9},{9,8},{10,11... | collective-permute-start | bytes 1179656 | tf_op jit(solution)/shard_map/ppermute | solution.py:1236
  1.1 3.0 %collective-permute-start.2 = (bf16[256,768]{1,0:T(8,128)(2,1)}, bf16[256,768]{1,0:T(8,128)(2,1)S(1)}, u32[]{:S(2)}, u32[]{:S(2)}) collective-permute-start(bf16[256,768]{1,0:T(8,128)(2,1)} %bitcast.6), channel_id=1, source_target_pairs={{0,1},{1,0},{2,3},{3,2},{4,5},{5,4},{6,7},{7,6},{8,9},{9,8},{10,11... | collective-permute-start | bytes 1179656 | tf_op jit(solution)/shard_map/ppermute | solution.py:1236
  1.2 13.0 %collective-permute-start = (bf16[256,768]{1,0:T(8,128)(2,1)}, bf16[256,768]{1,0:T(8,128)(2,1)S(1)}, u32[]{:S(2)}, u32[]{:S(2)}) collective-permute-start(bf16[256,768]{1,0:T(8,128)(2,1)} %bitcast.11), channel_id=1, source_target_pairs={{0,2},{1,3},{2,0},{3,1},{4,6},{5,7},{6,4},{7,5},{8,10},{9,11},{10,... | collective-permute-start | bytes 1179656 | tf_op jit(solution)/shard_map/ppermute | solution.py:1236
  14.2 1.8 %collective-permute-start.3 = (bf16[256,768]{1,0:T(8,128)(2,1)S(1)}, bf16[256,768]{1,0:T(8,128)(2,1)S(1)}, u32[]{:S(2)}, u32[]{:S(2)}) collective-permute-start(bf16[256,768]{1,0:T(8,128)(2,1)S(1)} %collective-permute-done.refs_1_), channel_id=1, source_target_pairs={{0,1},{1,0},{2,3},{3,2},{4,5},{5,4},{6,7},{7,6},{8,9},{9,8},{10,11... | collective-permute-start | bytes 1179656 | tf_op jit(solution)/shard_map/ppermute | solution.py:1236
  25.7 2.0 %collective-permute-start.4 = (bf16[512,384]{1,0:T(8,128)(2,1)}, bf16[512,384]{1,0:T(8,128)(2,1)S(1)}, u32[]{:S(2)}, u32[]{:S(2)}) collective-permute-start(bf16[512,384]{1,0:T(8,128)(2,1)} %get-tuple-element.98.refs_1_.refs_9_), channel_id=1, source_target_pairs={{0,1},{1,0},{2,3},{3,2},{4,5},{5,4},{6,7},{7,6},{8,9},{9,8},{10,11... | collective-permute-start | bytes 1179656 | tf_op jit(solution)/shard_map/ppermute | solution.py:1236
  45.3 5.9 %collective-permute-start.5 = (bf16[512,768]{1,0:T(8,128)(2,1)}, bf16[512,768]{1,0:T(8,128)(2,1)S(1)}, u32[]{:S(2)}, u32[]{:S(2)}) collective-permute-start(bf16[512,768]{1,0:T(8,128)(2,1)} %get-tuple-element.101.refs_2_), channel_id=1, source_target_pairs={{0,1},{1,0},{2,3},{3,2},{4,5},{5,4},{6,7},{7,6},{8,9},{9,8},{10,11... | collective-permute-start | bytes 2359304 | tf_op jit(solution)/shard_map/ppermute | solution.py:1236
  45.5 24.0 %collective-permute-start.6 = (bf16[2,512,384]{2,1,0:T(8,128)(2,1)}, bf16[2,512,384]{2,1,0:T(8,128)(2,1)S(1)}, u32[]{:S(2)}, u32[]{:S(2)}) collective-permute-start(bf16[2,512,384]{2,1,0:T(8,128)(2,1)} %get-tuple-element.115), channel_id=1, source_target_pairs={{0,4},{4,0},{8,12},{12,8},{16,20},{20,16},{24,28},{28,24},{1,5},{5... | collective-permute-start | bytes 2359304 | tf_op jit(solution)/shard_map/ppermute | solution.py:1236
  47.4 2.3 %collective-permute-start.7 = (bf16[2,2,192,384]{3,2,1,0:T(8,128)(2,1)}, bf16[2,2,192,384]{3,2,1,0:T(8,128)(2,1)}, u32[]{:S(2)}, u32[]{:S(2)}) collective-permute-start(bf16[2,2,192,384]{3,2,1,0:T(8,128)(2,1)} %get-tuple-element.116), channel_id=1, source_target_pairs={{0,1},{1,0},{2,3},{3,2},{4,5},{5,4},{6,7},{7,6},{8,9},{9,8},{10,11... | collective-permute-start | bytes 1769480 | tf_op jit(solution)/shard_map/ppermute | solution.py:1236
  47.4 24.3 %collective-permute-start.9 = (bf16[2,2,2,160,384]{4,3,2,1,0:T(8,128)(2,1)}, bf16[2,2,2,160,384]{4,3,2,1,0:T(8,128)(2,1)S(1)}, u32[]{:S(2)}, u32[]{:S(2)}) collective-permute-start(bf16[2,2,2,160,384]{4,3,2,1,0:T(8,128)(2,1)} %get-tuple-element.117), channel_id=1, source_target_pairs={{0,8},{4,12},{8,0},{12,4},{16,24},{20,28},{24,16},{28,20},{1,9},{5... | collective-permute-start | bytes 2949128 | tf_op jit(solution)/shard_map/ppermute | solution.py:1236
  49.7 22.1 %collective-permute-start.8 = (bf16[2,2,192,384]{3,2,1,0:T(8,128)(2,1)}, bf16[2,2,192,384]{3,2,1,0:T(8,128)(2,1)S(1)}, u32[]{:S(2)}, u32[]{:S(2)}) collective-permute-start(bf16[2,2,192,384]{3,2,1,0:T(8,128)(2,1)} %collective-permute-done.7), channel_id=1, source_target_pairs={{0,2},{1,3},{2,0},{3,1},{4,6},{5,7},{6,4},{7,5},{8,10},{9,11},{10,... | collective-permute-start | bytes 1769480 | tf_op jit(solution)/shard_map/ppermute | solution.py:1236
  51.2 21.4 %collective-permute-start.12 = (bf16[2,2,192,384]{3,2,1,0:T(8,128)(2,1)}, bf16[2,2,192,384]{3,2,1,0:T(8,128)(2,1)S(1)}, u32[]{:S(2)}, u32[]{:S(2)}) collective-permute-start(bf16[2,2,192,384]{3,2,1,0:T(8,128)(2,1)} %get-tuple-element.124), channel_id=1, source_target_pairs={{0,1},{1,0},{2,3},{3,2},{4,5},{5,4},{6,7},{7,6},{8,9},{9,8},{10,11... | collective-permute-start | bytes 1769480 | tf_op jit(solution)/shard_map/ppermute | solution.py:1236
  68.9 2.9 %collective-permute-start.10 = (bf16[2,6,48,384]{3,2,1,0:T(8,128)(2,1)}, bf16[2,6,48,384]{3,2,1,0:T(8,128)(2,1)S(1)}, u32[]{:S(2)}, u32[]{:S(2)}) collective-permute-start(bf16[2,6,48,384]{3,2,1,0:T(8,128)(2,1)} %get-tuple-element.118), channel_id=1, source_target_pairs={{0,1},{1,0},{2,3},{3,2},{4,5},{5,4},{6,7},{7,6},{8,9},{9,8},{10,11... | collective-permute-start | bytes 1327112 | tf_op jit(solution)/shard_map/ppermute | solution.py:1236
  69.5 2.3 %collective-permute-start.11 = (bf16[2,6,48,384]{3,2,1,0:T(8,128)(2,1)}, bf16[2,6,48,384]{3,2,1,0:T(8,128)(2,1)S(1)}, u32[]{:S(2)}, u32[]{:S(2)}) collective-permute-start(bf16[2,6,48,384]{3,2,1,0:T(8,128)(2,1)} %get-tuple-element.119), channel_id=1, source_target_pairs={{0,1},{1,0},{2,3},{3,2},{4,5},{5,4},{6,7},{7,6},{8,9},{9,8},{10,11... | collective-permute-start | bytes 1327112 | tf_op jit(solution)/shard_map/ppermute | solution.py:1236
  73.5 9.5 %copy-start = (bf16[768,2304]{1,0:T(8,128)(2,1)S(1)}, bf16[768,2304]{1,0:T(8,128)(2,1)}, u32[]{:S(2)}) copy-start(bf16[768,2304]{1,0:T(8,128)(2,1)} %refs_4_.5) | copy-start | bytes 10616836
  73.5 9.5 %copy-start.5 = (bf16[1,256,768]{2,1,0:T(8,128)(2,1)S(1)}, bf16[1,256,768]{2,1,0:T(8,128)(2,1)}, u32[]{:S(2)}) copy-start(bf16[1,256,768]{2,1,0:T(8,128)(2,1)} %param.16) | copy-start | bytes 1179652
  73.5 9.5 %copy-start.21 = (f32[10752]{0:T(1024)S(1)}, f32[10752]{0:T(1024)}, u32[]{:S(2)}) copy-start(f32[10752]{0:T(1024)} %param.15) | copy-start | bytes 129028
  73.5 9.5 %copy-start.29 = (s32[1,5]{1,0:T(1,128)S(1)}, s32[1,5]{1,0:T(1,128)}, u32[]{:S(2)}) copy-start(s32[1,5]{1,0:T(1,128)} %refs_0_.21) | copy-start | bytes 64
  73.5 9.5 %copy-start.30 = (f32[8,768]{1,0:T(8,128)S(1)}, f32[8,768]{1,0:T(8,128)}, u32[]{:S(2)}) copy-start(f32[8,768]{1,0:T(8,128)} %get-tuple-element.129.refs_12_) | copy-start | bytes 73732
  73.6 9.5 %copy-start.31 = (f32[1,1536]{1,0:T(1,128)S(1)}, f32[1,1536]{1,0:T(1,128)}, u32[]{:S(2)}) copy-start(f32[1,1536]{1,0:T(1,128)} %get-tuple-element.131.refs_14_) | copy-start | bytes 18436
  78.3 28.7 %collective-permute-start.14 = (bf16[1216,384]{1,0:T(8,128)(2,1)}, bf16[1216,384]{1,0:T(8,128)(2,1)S(1)}, u32[]{:S(2)}, u32[]{:S(2)}) collective-permute-start(bf16[1216,384]{1,0:T(8,128)(2,1)} %get-tuple-element.134), channel_id=1, source_target_pairs={{0,2},{1,3},{2,0},{3,1},{4,6},{5,7},{6,4},{7,5},{8,10},{9,11},{10,... | collective-permute-start | bytes 2801672 | tf_op jit(solution)/shard_map/ppermute | solution.py:1236
  79.9 27.2 %collective-permute-start.15 = (bf16[1216,384]{1,0:T(8,128)(2,1)}, bf16[1216,384]{1,0:T(8,128)(2,1)S(1)}, u32[]{:S(2)}, u32[]{:S(2)}) collective-permute-start(bf16[1216,384]{1,0:T(8,128)(2,1)} %get-tuple-element.128), channel_id=1, source_target_pairs={{0,4},{4,0},{8,12},{12,8},{16,20},{20,16},{24,28},{28,24},{1,5},{5... | collective-permute-start | bytes 2801672 | tf_op jit(solution)/shard_map/ppermute | solution.py:1236
  80.4 26.7 %collective-permute-start.13 = (bf16[2,2,160,384]{3,2,1,0:T(8,128)(2,1)}, bf16[2,2,160,384]{3,2,1,0:T(8,128)(2,1)S(1)}, u32[]{:S(2)}, u32[]{:S(2)}) collective-permute-start(bf16[2,2,160,384]{3,2,1,0:T(8,128)(2,1)} %get-tuple-element.133), channel_id=1, source_target_pairs={{0,16},{4,20},{8,24},{12,28},{16,0},{20,4},{24,8},{28,12},{1,17},{... | collective-permute-start | bytes 1474568 | tf_op jit(solution)/shard_map/ppermute | solution.py:1236
  93.3 13.8 %copy-start.9 = (bf16[2,512,384]{2,1,0:T(8,128)(2,1)S(1)}, bf16[2,512,384]{2,1,0:T(8,128)(2,1)}, u32[]{:S(2)}) copy-start(bf16[2,512,384]{2,1,0:T(8,128)(2,1)} %get-tuple-element.121.refs_3_.refs_4_) | copy-start | bytes 2359300
  93.3 13.8 %copy-start.12 = (bf16[2,512,384]{2,1,0:T(8,128)(2,1)S(1)}, bf16[2,512,384]{2,1,0:T(8,128)(2,1)}, u32[]{:S(2)}) copy-start(bf16[2,512,384]{2,1,0:T(8,128)(2,1)} %copy-done.11) | copy-start | bytes 2359300
  93.3 13.8 %copy-start.15 = (bf16[2,2,192,384]{3,2,1,0:T(8,128)(2,1)S(1)}, bf16[2,2,192,384]{3,2,1,0:T(8,128)(2,1)}, u32[]{:S(2)}) copy-start(bf16[2,2,192,384]{3,2,1,0:T(8,128)(2,1)} %copy-done.14) | copy-start | bytes 1769476
  93.3 13.8 %copy-start.17 = (bf16[2,2,192,384]{3,2,1,0:T(8,128)(2,1)S(1)}, bf16[2,2,192,384]{3,2,1,0:T(8,128)(2,1)}, u32[]{:S(2)}) copy-start(bf16[2,2,192,384]{3,2,1,0:T(8,128)(2,1)} %copy-done.16) | copy-start | bytes 1769476
  93.3 13.8 %copy-start.18 = (bf16[2,352,384]{2,1,0:T(8,128)(2,1)S(1)}, bf16[2,352,384]{2,1,0:T(8,128)(2,1)}, u32[]{:S(2)}) copy-start(bf16[2,352,384]{2,1,0:T(8,128)(2,1)} %get-tuple-element.143.refs_13_.refs_1_) | copy-start | bytes 1622020
  93.3 13.8 %copy-start.20 = (bf16[2,6,48,384]{3,2,1,0:T(8,128)(2,1)S(1)}, bf16[2,6,48,384]{3,2,1,0:T(8,128)(2,1)}, u32[]{:S(2)}) copy-start(bf16[2,6,48,384]{3,2,1,0:T(8,128)(2,1)} %copy-done.19) | copy-start | bytes 1327108
  93.3 13.8 %copy-start.25 = (bf16[2,128,384]{2,1,0:T(8,128)(2,1)S(1)}, bf16[2,128,384]{2,1,0:T(8,128)(2,1)}, u32[]{:S(2)}) copy-start(bf16[2,128,384]{2,1,0:T(8,128)(2,1)} %get-tuple-element.139.refs_8_.refs_7_) | copy-start | bytes 589828
  101.7 4.2 %collective-permute-start.17 = (f32[16,768]{1,0:T(8,128)S(1)}, f32[16,768]{1,0:T(8,128)S(1)}, u32[]{:S(2)}, u32[]{:S(2)}) collective-permute-start(f32[16,768]{1,0:T(8,128)S(1)} %get-tuple-element.135.refs_9_), channel_id=1, source_target_pairs={{0,4},{4,0},{8,12},{12,8},{16,20},{20,16},{24,28},{28,24},{1,5},{5... | collective-permute-start | bytes 147464 | tf_op jit(solution)/shard_map/ppermute | solution.py:1236
  103.2 2.6 %collective-permute-start.16 = (f32[16,768]{1,0:T(8,128)S(1)}, f32[16,768]{1,0:T(8,128)S(1)}, u32[]{:S(2)}, u32[]{:S(2)}) collective-permute-start(f32[16,768]{1,0:T(8,128)S(1)} %get-tuple-element.135.refs_9_), channel_id=1, source_target_pairs={{0,1},{1,0},{2,3},{3,2},{4,5},{5,4},{6,7},{7,6},{8,9},{9,8},{10,11... | collective-permute-start | bytes 147464 | tf_op jit(solution)/shard_map/ppermute | solution.py:1236
  105.8 1.2 collective-permute-start.18
  107.1 15.2 %copy-start.2 = (bf16[2,2,2,160,384]{4,3,2,1,0:T(8,128)(2,1)S(1)}, bf16[2,2,2,160,384]{4,3,2,1,0:T(8,128)(2,1)}, u32[]{:S(2)}) copy-start(bf16[2,2,2,160,384]{4,3,2,1,0:T(8,128)(2,1)} %get-tuple-element.113.refs_1_.refs_12_) | copy-start | bytes 2949124
  107.1 15.2 %copy-start.4 = (bf16[2,2,2,160,384]{4,3,2,1,0:T(8,128)(2,1)S(1)}, bf16[2,2,2,160,384]{4,3,2,1,0:T(8,128)(2,1)}, u32[]{:S(2)}) copy-start(bf16[2,2,2,160,384]{4,3,2,1,0:T(8,128)(2,1)} %copy-done.3) | copy-start | bytes 2949124
  110.5 11.8 %collective-permute-start.22 = (bf16[768,768]{1,0:T(8,128)(2,1)S(1)}, bf16[768,768]{1,0:T(8,128)(2,1)S(1)}, u32[]{:S(2)}, u32[]{:S(2)}) collective-permute-start(bf16[768,768]{1,0:T(8,128)(2,1)S(1)} %get-tuple-element.149), channel_id=1, source_target_pairs={{0,1},{1,0},{2,3},{3,2},{4,5},{5,4},{6,7},{7,6},{8,9},{9,8},{10,11... | collective-permute-start | bytes 3538952 | tf_op jit(solution)/shard_map/ppermute | solution.py:1236
  110.7 10.9 %collective-permute-start.19 = (bf16[2,224,384]{2,1,0:T(8,128)(2,1)S(1)}, bf16[2,224,384]{2,1,0:T(8,128)(2,1)S(1)}, u32[]{:S(2)}, u32[]{:S(2)}) collective-permute-start(bf16[2,224,384]{2,1,0:T(8,128)(2,1)S(1)} %get-tuple-element.144), channel_id=1, source_target_pairs={{0,8},{4,12},{8,0},{12,4},{16,24},{20,28},{24,16},{28,20},{1,9},{5... | collective-permute-start | bytes 1032200 | tf_op jit(solution)/shard_map/ppermute | solution.py:1236
  112.2 10.0 %collective-permute-start.20 = (bf16[448,384]{1,0:T(8,128)(2,1)S(1)}, bf16[448,384]{1,0:T(8,128)(2,1)S(1)}, u32[]{:S(2)}, u32[]{:S(2)}) collective-permute-start(bf16[448,384]{1,0:T(8,128)(2,1)S(1)} %get-tuple-element.145.refs_9_), channel_id=1, source_target_pairs={{0,2},{1,3},{2,0},{3,1},{4,6},{5,7},{6,4},{7,5},{8,10},{9,11},{10,... | collective-permute-start | bytes 1032200 | tf_op jit(solution)/shard_map/ppermute | solution.py:1236
  113.4 8.2 %collective-permute-start.21 = (bf16[352,384]{1,0:T(8,128)(2,1)S(1)}, bf16[352,384]{1,0:T(8,128)(2,1)S(1)}, u32[]{:S(2)}, u32[]{:S(2)}) collective-permute-start(bf16[352,384]{1,0:T(8,128)(2,1)S(1)} %get-tuple-element.146), channel_id=1, source_target_pairs={{0,4},{4,0},{8,12},{12,8},{16,20},{20,16},{24,28},{28,24},{1,5},{5... | collective-permute-start | bytes 811016 | tf_op jit(solution)/shard_map/ppermute | solution.py:1236
  122.3 18.1 %copy-start.33 = (s32[96]{0:T(128)S(1)}, s32[96]{0:T(128)}, u32[]{:S(2)}) copy-start(s32[96]{0:T(128)} %constant.2.clone.refs_1_) | copy-start | bytes 1156
  122.3 22.2 %copy-start.8 = (bf16[1,256,768]{2,1,0:T(8,128)(2,1)S(1)}, bf16[1,256,768]{2,1,0:T(8,128)(2,1)}, u32[]{:S(2)}) copy-start(bf16[1,256,768]{2,1,0:T(8,128)(2,1)} %param.9) | copy-start | bytes 1179652
  122.3 22.1 %copy-start.27 = (f32[256,768]{1,0:T(8,128)S(1)}, f32[256,768]{1,0:T(8,128)}, u32[]{:S(2)}) copy-start(f32[256,768]{1,0:T(8,128)} %get-tuple-element.163.refs_5_) | copy-start | bytes 2359300
  128.1 16.4 %copy-start.26 = (f32[256,768]{1,0:T(8,128)S(1)}, f32[256,768]{1,0:T(8,128)}, u32[]{:S(2)}) copy-start(f32[256,768]{1,0:T(8,128)} %get-tuple-element.165.refs_8_) | copy-start | bytes 2359300
  128.1 12.3 %collective-permute-start.23 = (bf16[416,384]{1,0:T(8,128)(2,1)S(1)}, bf16[416,384]{1,0:T(8,128)(2,1)S(1)}, u32[]{:S(2)}, u32[]{:S(2)}) collective-permute-start(bf16[416,384]{1,0:T(8,128)(2,1)S(1)} %get-tuple-element.157), channel_id=1, source_target_pairs={{0,8},{4,12},{8,0},{12,4},{16,24},{20,28},{24,16},{28,20},{1,9},{5... | collective-permute-start | bytes 958472 | tf_op jit(solution)/shard_map/ppermute | solution.py:1236
  128.6 8.9 %collective-permute-start.24 = (bf16[2,160,384]{2,1,0:T(8,128)(2,1)S(1)}, bf16[2,160,384]{2,1,0:T(8,128)(2,1)S(1)}, u32[]{:S(2)}, u32[]{:S(2)}) collective-permute-start(bf16[2,160,384]{2,1,0:T(8,128)(2,1)S(1)} %get-tuple-element.159), channel_id=1, source_target_pairs={{0,2},{1,3},{2,0},{3,1},{4,6},{5,7},{6,4},{7,5},{8,10},{9,11},{10,... | collective-permute-start | bytes 737288 | tf_op jit(solution)/shard_map/ppermute | solution.py:1236
  129.7 14.7 %collective-permute-start.25 = (bf16[256,768]{1,0:T(8,128)(2,1)S(1)}, bf16[256,768]{1,0:T(8,128)(2,1)S(1)}, u32[]{:S(2)}, u32[]{:S(2)}) collective-permute-start(bf16[256,768]{1,0:T(8,128)(2,1)S(1)} %get-tuple-element.161), channel_id=1, source_target_pairs={{0,2},{1,3},{2,0},{3,1},{4,6},{5,7},{6,4},{7,5},{8,10},{9,11},{10,... | collective-permute-start | bytes 1179656 | tf_op jit(solution)/shard_map/ppermute | solution.py:1236
  130.6 17.4 %collective-permute-start.26 = (bf16[224,384]{1,0:T(8,128)(2,1)S(1)}, bf16[224,384]{1,0:T(8,128)(2,1)S(1)}, u32[]{:S(2)}, u32[]{:S(2)}) collective-permute-start(bf16[224,384]{1,0:T(8,128)(2,1)S(1)} %get-tuple-element.169), channel_id=1, source_target_pairs={{0,16},{4,20},{8,24},{12,28},{16,0},{20,4},{24,8},{28,12},{1,17},{... | collective-permute-start | bytes 516104 | tf_op jit(solution)/shard_map/ppermute | solution.py:1236
  142.8 7.7 %collective-permute-start.28 = (bf16[224,384]{1,0:T(8,128)(2,1)S(1)}, bf16[224,384]{1,0:T(8,128)(2,1)S(1)}, u32[]{:S(2)}, u32[]{:S(2)}) collective-permute-start(bf16[224,384]{1,0:T(8,128)(2,1)S(1)} %get-tuple-element.171), channel_id=1, source_target_pairs={{0,16},{4,20},{8,24},{12,28},{16,0},{20,4},{24,8},{28,12},{1,17},{... | collective-permute-start | bytes 516104 | tf_op jit(solution)/shard_map/ppermute | solution.py:1236
  142.9 5.2 %collective-permute-start.27 = (bf16[160,384]{1,0:T(8,128)(2,1)S(1)}, bf16[160,384]{1,0:T(8,128)(2,1)S(1)}, u32[]{:S(2)}, u32[]{:S(2)}) collective-permute-start(bf16[160,384]{1,0:T(8,128)(2,1)S(1)} %get-tuple-element.170), channel_id=1, source_target_pairs={{0,4},{4,0},{8,12},{12,8},{16,20},{20,16},{24,28},{28,24},{1,5},{5... | collective-permute-start | bytes 368648 | tf_op jit(solution)/shard_map/ppermute | solution.py:1236
  (21 other events, 34.5 us)

commit v2 on v1

--- a/solution.py
+++ b/solution.py
@@ -290,7 +290,7 @@
 MASKED = -1e30
 GRANT = 60 * 1024 * 1024
 STEP_GRANT = 20 * 1024 * 1024
-LATE_GRANT = 32 * 1024 * 1024
+LATE_GRANT = 48 * 1024 * 1024
 WIDE_CHUNK = 128
 
 
@@ -1130,37 +1130,46 @@
     a_ref[...] = sum_of(a_keep[...], x_got[count + a_keep.shape[0] :]).astype(BF)
 
 
+def last_rows(side, a_keep, a_got, a_far, b_keep, y_got, b_far, o_keep, y_rest, x_ref, ref):
+    unit_rows, rows = b_keep.shape[1], o_keep.shape[0]
+    units, most = 6 * unit_rows, rows // 2
+    half = units // 2
+    at = slice(side * half, (side + 1) * half)
+    ref[:half] = sum_of(a_keep[at], a_got[at], a_far[at]).astype(BF)
+    for index in range(3):
+        at = slice(index * unit_rows, (index + 1) * unit_rows)
+        far = slice(side * half + index * unit_rows, side * half + (index + 1) * unit_rows)
+        ref[half + index * unit_rows : half + (index + 1) * unit_rows] = sum_of(
+            b_keep[index], y_got[at], b_far[far]
+        ).astype(BF)
+    for high_z in range(2):
+        first, block = units + high_z * unit_rows, 2 * side + high_z
+        at = slice(units + 16 * block, units + 16 * (block + 1))
+        ref[first : first + 16] = sum_of(a_keep[at], a_got[at], a_far[at]).astype(BF)
+        at = slice(high_z * most, (high_z + 1) * most)
+        far = units + side * rows + high_z * most
+        ref[first + 16 : first + unit_rows] = sum_of(o_keep[at], y_rest[at], b_far[far : far + most]).astype(BF)
+    ref[units + 2 * unit_rows :] = sum_of(x_ref[...], b_far[units + 2 * rows :]).astype(BF)
+
+
 def fourth_step_kernel(where_ref, stage):
-    a_keep, x_got, a_far, b_keep, y_got, b_far, o_keep, y_rest, x_ref, mlp_keep, mlp_got, dz_keep, dz_got, dz_far = (
-        stage[index] for index in range(14)
-    )
-    send_ref, mlp_ref, dz_ref, mlp_kept, kept_ref, dz_kept, dtok_ref = (stage.out(index) for index in range(7))
-    unit_rows, rows = b_keep.shape[1], o_keep.shape[0]
-    units, most = 6 * unit_rows, rows // 4
-    own = sum_of(a_keep[...], x_got[...], a_far[...]).astype(BF)
-    rest = sum_of(o_keep[...], y_rest[...], b_far[units : units + rows]).astype(BF)
-    sums = sum_of(x_ref[...], b_far[units + rows :]).astype(BF)
-    for side, ref in enumerate((kept_ref, send_ref)):
-        ref[: units // 2] = own[side * units // 2 : (side + 1) * units // 2]
-        for index in range(3):
-            unit = 3 * side + index
-            at = slice(unit * unit_rows, (unit + 1) * unit_rows)
-            to = slice((3 + index) * unit_rows, (4 + index) * unit_rows)
-            ref[to] = sum_of(b_keep[unit], y_got[at], b_far[at]).astype(BF)
-        for high_z in range(2):
-            first, block = units + high_z * unit_rows, 2 * side + high_z
-            ref[first : first + 16] = own[units + 16 * block : units + 16 * (block + 1)]
-            ref[first + 16 : first + unit_rows] = rest[block * most : (block + 1) * most]
-        ref[units + 2 * unit_rows :] = sums
+    send_ref, mlp_ref, dz_ref, dtok_ref = (stage.out(index) for index in range(4))
+    last_rows(1, *(stage[index] for index in range(9)), send_ref)
     stage.put(0)
-    mlp_ref[...] = sum_of(mlp_keep[1], mlp_got[1]).astype(BF)
-    stage.put(1)
-    for side, ref in enumerate((dz_kept, dz_ref)):
-        ref[...] = sum_of(dz_keep[side], dz_got[side], dz_far[side]).astype(BF)
+    dz_ref[...] = sum_of(stage[11][...], stage[12][...], stage[13][...]).astype(BF)
     stage.put(2)
     dtok_ref[...] = sum_of(stage[14][...], stage[15][...]).astype(BF)
-    stage.put(6)
-    mlp_kept[...] = sum_of(mlp_keep[0], mlp_got[0]).astype(BF)
+    stage.put(3)
+    mlp_ref[...] = sum_of(stage[9][...], stage[10][...]).astype(BF)
+
+
+def kept_kernel(where_ref, stage):
+    mlp_ref, kept_ref, dz_ref = (stage.out(index) for index in range(3))
+    last_rows(0, *(stage[index] for index in range(9)), kept_ref)
+    stage.put(1)
+    dz_ref[...] = sum_of(stage[11][...], stage[12][...], stage[13][...]).astype(BF)
+    stage.put(2)
+    mlp_ref[...] = sum_of(stage[9][...], stage[10][...]).astype(BF)
 
 
 def fifth_step_kernel(where_ref, stage, held):
@@ -1180,7 +1189,7 @@
         ref[4 * unit_rows :] = rest[2 * unit_rows :]
     stage.put(0)
     for side, ref in enumerate((dz_low_ref, dz_ref)):
-        ref[...] = sum_of(dz_kept[side], dz_got[side]).astype(BF)
+        ref[...] = sum_of(dz_kept[0, side], dz_got[0, side]).astype(BF)
 
 
 def finish_kernel(where_ref, stage, rows_ref, out_rows_ref, flat):
@@ -1281,6 +1290,13 @@
     return cut
 
 
+def rows_of_entry(array, index, first, last):
+    def cut(where_ref, source, target):
+        return [(source.at[index, first:last], target)]
+
+    return ((last - first, *array.shape[2:]), 1, cut)
+
+
 def some_rows(array, first, last):
     def cut(where_ref, source, target):
         return [(source.at[first:last], target)]
@@ -1473,20 +1489,39 @@
     late_got = to_core(late_send)
     mlp_got, b_far, a_far, late_got = lax.optimization_barrier((mlp_got, b_far, a_far, late_got))
 
-    first = 2 * block + 2 * six
-    last_send, mlp_step, dz_step, mlp_kept, last_keep, dz_kept, dtok_step = step(
+    first, part = 2 * block + 2 * six, rest // 2
+
+    def side_cuts(side):
+        start = 2 * block + side * six // 2
+        return {
+            0: entry(a_keep, 0), 1: some_rows(x_got, count, count + six + 64),
+            3: rows_of_entry(b_keep, 0, 3 * side, 3 * side + 3),
+            4: some_rows(y_got, start, start + six // 2),
+            6: rows_of_entry(o_keep, 0, side * part, (side + 1) * part),
+            7: some_rows(y_got, first + side * part, first + (side + 1) * part),
+            8: some_rows(b_step, six + rest, six + rest + 32),
+            9: entry(mlp_keep, side), 10: entry(mlp_got, side),
+            11: rows_of_entry(dz_keep, 0, side, side + 1), 12: rows_of_entry(dz_got, 0, side, side + 1),
+            13: some_rows(dz_far, side, side + 1),
+        }
+
+    operands = (a_keep, x_got, a_far, b_keep, y_got, b_far, o_keep, y_got, b_step, mlp_keep, mlp_got, dz_keep, dz_got, dz_far)
+    last = low(six + 2 * unit_rows + 32, half)
+    last_send, mlp_step, dz_step, dtok_step = step(
         fourth_step_kernel,
         where,
-        (a_keep, x_got, a_far, b_keep, y_got, b_far, o_keep, y_got, b_step, mlp_keep, mlp_got, dz_keep, dz_got, dz_far,
-         dtok_far, late_got),
-        [low(six + 2 * unit_rows + 32, half), low(lead + block, piece), low(2, top, piece), low(lead + block, piece),
-         low(six + 2 * unit_rows + 32, half), low(2, top, piece), low(rows, width)],
-        cuts={0: entry(a_keep, 0), 1: some_rows(x_got, count, count + six + 64), 3: entry(b_keep, 0),
-              4: some_rows(y_got, 2 * block, 2 * block + six), 6: entry(o_keep, 0), 7: some_rows(y_got, first, first + rest),
-              8: some_rows(b_step, six + rest, six + rest + 32), 11: entry(dz_keep, 0), 12: entry(dz_got, 0),
-              15: some_rows(late_got, rows, both)},
+        (*operands, dtok_far, late_got),
+        [last, low(lead + block, piece), low(1, 2, top, piece), low(rows, width)],
+        cuts=side_cuts(1) | {15: some_rows(late_got, rows, both)},
     )
     last_got, mlp_far, dz_x, dtok_x = to_z(last_send), to_zz(mlp_step), to_x(dz_step), to_x(dtok_step)
+    mlp_kept, last_keep, dz_kept = step(
+        kept_kernel,
+        where,
+        after(last_send, *operands),
+        [low(lead + block, piece), last, low(1, 2, top, piece)],
+        cuts=side_cuts(0),
+    )
     last_send, dz_y, last_kept, dz_low = step(
         fifth_step_kernel,
         where,

time: 155 us -> 151 us (0.974)
  local copies, waits for them, and re-layouts: 15.4 us -> 8.4 us
  Pallas kernels: 82.6 us -> 84.9 us
  starting transfers between devices: 24.3 us -> 25.9 us
    unnamed x80 -> x70, local copies, waits for them, and re-layouts: 15.4 us -> 8.4 us
    pallas_call x11 -> x12, Pallas kernels: 82.6 us -> 84.9 us  [staged_call(): pl.pallas_call(kernel, in_specs=[pl.BlockSpec(memory_space=pltpu.SMEM)] *...]
    ppermute x29, starting transfers between devices: 24.3 us -> 25.9 us  [swapped(): return lax.ppermute(array, axis, [(i, i ^ bit) for i in range(length)])]
  transfers between devices with their start and end apart: 29 -> 29, of which waited for: 11 -> 11; matrix products, arithmetic and copies ran while one was open for 0% -> 0% of each run, Pallas kernels for 26% -> 29%
where the time goes in v2:
time: 151 us; the launch traced here: 150 us
  Pallas kernels  84.9 us (56%)
  waiting for transfers between devices  29.5 us (20%)
  starting transfers between devices  25.9 us (17%)
  local copies, waits for them, and re-layouts  8.4 us (6%)
    pallas_call x12, Pallas kernels, staged_call(): pl.pallas_call(kernel, in_specs=[pl.BlockSpec(memory_space=pltpu.SMEM)] *...  84.9 us
    ppermute x29, waiting for transfers between devices, swapped(): return lax.ppermute(array, axis, [(i, i ^ bit) for i in range(length)])  29.5 us
    ppermute x29, starting transfers between devices, swapped(): return lax.ppermute(array, axis, [(i, i ^ bit) for i in range(length)])  25.9 us
    unnamed x70, local copies, waits for them, and re-layouts  8.4 us
  transfers between devices with their start and end apart: 29, of which 11 were waited for; matrix products, arithmetic and copies ran while one was open for 0% of the time, Pallas kernels for 29%

profile of v2, /device:TPU:0, one launch (start us, length us, event | category | flops | bytes accessed | tf_op | source)
XLA Modules:
  0.0 150.4 jit_solution(9575799488653310545)
XLA Ops:
  0.6 0.5 collective-permute-start.1
  1.2 2.9 %collective-permute-start = (bf16[256,768]{1,0:T(8,128)(2,1)}, bf16[256,768]{1,0:T(8,128)(2,1)S(1)}, u32[]{:S(2)}, u32[]{:S(2)}) collective-permute-start(bf16[256,768]{1,0:T(8,128)(2,1)} %bitcast.11), channel_id=1, source_target_pairs={{0,2},{1,3},{2,0},{3,1},{4,6},{5,7},{6,4},{7,5},{8,10},{9,11},{10,... | collective-permute-start | bytes 1179656 | tf_op jit(solution)/shard_map/ppermute | solution.py:1245
  4.2 0.8 copy-done.30
  5.1 9.2 %shard_map.144 = (bf16[512,768]{1,0:T(8,128)(2,1)}, bf16[512,1152]{1,0:T(8,128)(2,1)}, bf16[512,1536]{1,0:T(8,128)(2,1)}, bf16[768,512]{1,0:T(8,128)(2,1)}, f32[1,768]{1,0:T(1,128)}) custom-call(s32[1,5]{1,0:T(1,128)} %refs_0_.23, bf16[256,768]{1,0:T(8,128)(2,1)} %bitcast.12, bf16[256,768]{1,0:T(8,128)(2,1)} %copy-done.30, f32[84,128]{1,0:T(8,128)} %bitcast.15, ...), custom_call_target="tpu_custom_call" | custom-call | tf_op jit(solution)/shard_map/pallas_call | solution.py:475
  14.4 1.7 %collective-permute-done.3.refs_2_ = bf16[256,768]{1,0:T(8,128)(2,1)S(1)} collective-permute-done((bf16[256,768]{1,0:T(8,128)(2,1)S(1)}, bf16[256,768]{1,0:T(8,128)(2,1)S(1)}, u32[]{:S(2)}, u32[]{:S(2)}) %collective-permute-start.3) | collective-permute-done | bytes 393248 | tf_op jit(solution)/shard_map/ppermute | solution.py:1245
  16.1 0.7 copy-done.33
  16.8 8.9 %shard_map.145 = (bf16[512,768]{1,0:T(8,128)(2,1)}, bf16[1024,768]{1,0:T(8,128)(2,1)}, bf16[512,384]{1,0:T(8,128)(2,1)}, f32[3,4,256]{2,1,0:T(4,128)}) custom-call(s32[1,5]{1,0:T(1,128)} %refs_0_.23, bf16[256,768]{1,0:T(8,128)(2,1)} %copy-done.32, bf16[256,768]{1,0:T(8,128)(2,1)} %copy-done.33, f32[84,128]{1,0:T(8,128)} %bitcast.16, ...), custom_call_target="tpu_custom_call" | custom-call | tf_op jit(solution)/shard_map/pallas_call | solution.py:475
  25.9 1.8 %collective-permute-done.4.refs_2_.refs_10_ = bf16[512,384]{1,0:T(8,128)(2,1)S(1)} collective-permute-done((bf16[512,384]{1,0:T(8,128)(2,1)}, bf16[512,384]{1,0:T(8,128)(2,1)S(1)}, u32[]{:S(2)}, u32[]{:S(2)}) %collective-permute-start.4) | collective-permute-done | bytes 393248 | tf_op jit(solution)/shard_map/ppermute | solution.py:1245
  27.7 0.7 copy-done.29
  28.4 16.8 %shard_map.146 = (bf16[2,512,384]{2,1,0:T(8,128)(2,1)}, bf16[2,512,384]{2,1,0:T(8,128)(2,1)}, bf16[2,2,192,384]{3,2,1,0:T(8,128)(2,1)}, bf16[2,2,192,384]{3,2,1,...) custom-call(s32[1,5]{1,0:T(1,128)} %refs_0_.23, ...), custom_call_target="tpu_custom_call" | custom-call | tf_op jit(solution)/shard_map/pallas_call | solution.py:475
  45.5 1.9 %collective-permute-start.6 = (bf16[2,512,384]{2,1,0:T(8,128)(2,1)}, bf16[2,512,384]{2,1,0:T(8,128)(2,1)S(1)}, u32[]{:S(2)}, u32[]{:S(2)}) collective-permute-start(bf16[2,512,384]{2,1,0:T(8,128)(2,1)} %get-tuple-element.129), channel_id=1, source_target_pairs={{0,4},{4,0},{8,12},{12,8},{16,20},{20,16},{24,28},{28,24},{1,5},{5... | collective-permute-start | bytes 2359304 | tf_op jit(solution)/shard_map/ppermute | solution.py:1245
  47.4 1.6 %collective-permute-start.9 = (bf16[2,2,2,160,384]{4,3,2,1,0:T(8,128)(2,1)}, bf16[2,2,2,160,384]{4,3,2,1,0:T(8,128)(2,1)S(1)}, u32[]{:S(2)}, u32[]{:S(2)}) collective-permute-start(bf16[2,2,2,160,384]{4,3,2,1,0:T(8,128)(2,1)} %get-tuple-element.131), channel_id=1, source_target_pairs={{0,8},{4,12},{8,0},{12,4},{16,24},{20,28},{24,16},{28,20},{1,9},{5... | collective-permute-start | bytes 2949128 | tf_op jit(solution)/shard_map/ppermute | solution.py:1245
  49.0 0.6 collective-permute-done.7
  49.6 1.5 %collective-permute-start.8 = (bf16[2,2,192,384]{3,2,1,0:T(8,128)(2,1)S(1)}, bf16[2,2,192,384]{3,2,1,0:T(8,128)(2,1)S(1)}, u32[]{:S(2)}, u32[]{:S(2)}) collective-permute-start(bf16[2,2,192,384]{3,2,1,0:T(8,128)(2,1)S(1)} %collective-permute-done.7), channel_id=1, source_target_pairs={{0,2},{1,3},{2,0},{3,1},{4,6},{5,7},{6,4},{7,5},{8,10},{9,11},{10,... | collective-permute-start | bytes 1769480 | tf_op jit(solution)/shard_map/ppermute | solution.py:1245
  51.1 16.8 %shard_map.147 = (f32[256,768]{1,0:T(8,128)}, bf16[2,352,384]{2,1,0:T(8,128)(2,1)}, bf16[2,352,384]{2,1,0:T(8,128)(2,1)}, bf16[2,6,48,384]{3,2,1,0:T(8,128)(2,1)...) custom-call(s32[1,5]{1,0:T(1,128)} %refs_0_.23, ...), custom_call_target="tpu_custom_call" | custom-call | tf_op jit(solution)/shard_map/pallas_call | solution.py:475
  67.9 0.6 collective-permute-start.10
  68.5 3.2 %collective-permute-done.9.refs_2_.refs_13_ = bf16[2,2,2,160,384]{4,3,2,1,0:T(8,128)(2,1)S(1)} collective-permute-done((bf16[2,2,2,160,384]{4,3,2,1,0:T(8,128)(2,1)}, bf16[2,2,2,160,384]{4,3,2,1,0:T(8,128)(2,1)S(1)}, u32[]{:S(2)}, u32[]{:S(2)}) %collective-permute-start.9) | collective-permute-done | bytes 983072 | tf_op jit(solution)/shard_map/ppermute | solution.py:1245
  71.8 0.9 copy-done.13
  73.3 4.3 %shard_map.148 = (bf16[2,2,160,384]{3,2,1,0:T(8,128)(2,1)}, bf16[1216,384]{1,0:T(8,128)(2,1)}, bf16[1216,384]{1,0:T(8,128)(2,1)}) custom-call(s32[1,5]{1,0:T(1,128)} %refs_0_.23, bf16[2,2,2,160,384]{4,3,2,1,0:T(8,128)(2,1)} %get-tuple-element.182.refs_1_.refs_12_, bf16[2,2,2,160,384]{4,3,2,1,0:T(8,128)(2,1)} %copy-done.1, ...), custom_call_target="tpu_custom_call" | custom-call | tf_op jit(solution)/shard_map/pallas_call | solution.py:475
  77.7 1.6 %collective-permute-start.14 = (bf16[1216,384]{1,0:T(8,128)(2,1)}, bf16[1216,384]{1,0:T(8,128)(2,1)S(1)}, u32[]{:S(2)}, u32[]{:S(2)}) collective-permute-start(bf16[1216,384]{1,0:T(8,128)(2,1)} %get-tuple-element.148), channel_id=1, source_target_pairs={{0,2},{1,3},{2,0},{3,1},{4,6},{5,7},{6,4},{7,5},{8,10},{9,11},{10,... | collective-permute-start | bytes 2801672 | tf_op jit(solution)/shard_map/ppermute | solution.py:1245
  79.7 2.6 %collective-permute-start.13 = (bf16[2,2,160,384]{3,2,1,0:T(8,128)(2,1)}, bf16[2,2,160,384]{3,2,1,0:T(8,128)(2,1)S(1)}, u32[]{:S(2)}, u32[]{:S(2)}) collective-permute-start(bf16[2,2,160,384]{3,2,1,0:T(8,128)(2,1)} %get-tuple-element.147), channel_id=1, source_target_pairs={{0,16},{4,20},{8,24},{12,28},{16,0},{20,4},{24,8},{28,12},{1,17},{... | collective-permute-start | bytes 1474568 | tf_op jit(solution)/shard_map/ppermute | solution.py:1245
  82.4 1.1 copy-done.12
  83.5 1.1 copy-done.19
  84.7 1.1 copy-done.20
  85.8 1.0 copy-done.23
  86.8 8.6 %shard_map.149 = (bf16[256,768]{1,0:T(8,128)(2,1)S(1)}, bf16[256,768]{1,0:T(8,128)(2,1)S(1)}, bf16[768,768]{1,0:T(8,128)(2,1)}, f32[256,768]{1,0:T(8,128)S(1)}, f32[16,768]{1,0:T(8,128)S(1)}) custom-call(s32[1,5]{1,0:T(1,128)S(1)} %copy-done.24, bf16[512,384]{1,0:T(8,128)(2,1)S(1)} %copy-done.23, bf16[1024,384]{1,0:T(8,128)(2,1)S(1)} %copy-done.19, ...), custom_call_target="tpu_custom_call" | custom-call | tf_op jit(solution)/shard_map/pallas_call | solution.py:475
  95.4 1.6 %collective-permute-start.17 = (f32[16,768]{1,0:T(8,128)S(1)}, f32[16,768]{1,0:T(8,128)S(1)}, u32[]{:S(2)}, u32[]{:S(2)}) collective-permute-start(f32[16,768]{1,0:T(8,128)S(1)} %get-tuple-element.149.refs_9_), channel_id=1, source_target_pairs={{0,4},{4,0},{8,12},{12,8},{16,20},{20,16},{24,28},{28,24},{1,5},{5... | collective-permute-start | bytes 147464 | tf_op jit(solution)/shard_map/ppermute | solution.py:1245
  97.0 5.5 %collective-permute-done.17.refs_11_ = f32[16,768]{1,0:T(8,128)S(1)} collective-permute-done((f32[16,768]{1,0:T(8,128)S(1)}, f32[16,768]{1,0:T(8,128)S(1)}, u32[]{:S(2)}, u32[]{:S(2)}) %collective-permute-start.17) | collective-permute-done | bytes 49184 | tf_op jit(solution)/shard_map/ppermute | solution.py:1245
  102.5 1.2 collective-permute-done.18.refs_12_
  103.8 3.3 %shard_map.150 = (bf16[2,224,384]{2,1,0:T(8,128)(2,1)S(1)}, bf16[448,384]{1,0:T(8,128)(2,1)S(1)}, bf16[352,384]{1,0:T(8,128)(2,1)S(1)}, bf16[2,224,384]{2,1,0:T(8,128)(2,1)S(1)}) custom-call(s32[1,5]{1,0:T(1,128)S(1)} %copy-done.24, bf16[2,2,192,384]{3,2,1,0:T(8,128)(2,1)S(1)} %copy-done.16, bf16[2,2,192,384]{3,2,1,0:T(8,128)(2,1)S(1)} %copy-done.14, ...), custom_call_target="tpu_custom_call" | custom-call | tf_op jit(solution)/shard_map/pallas_call | solution.py:475
  107.4 1.6 %collective-permute-start.19 = (bf16[2,224,384]{2,1,0:T(8,128)(2,1)S(1)}, bf16[2,224,384]{2,1,0:T(8,128)(2,1)S(1)}, u32[]{:S(2)}, u32[]{:S(2)}) collective-permute-start(bf16[2,224,384]{2,1,0:T(8,128)(2,1)S(1)} %get-tuple-element.158), channel_id=1, source_target_pairs={{0,8},{4,12},{8,0},{12,4},{16,24},{20,28},{24,16},{28,20},{1,9},{5... | collective-permute-start | bytes 1032200 | tf_op jit(solution)/shard_map/ppermute | solution.py:1245
  109.5 0.5 collective-permute-start.21
  110.0 7.6 %collective-permute-done.21.refs_3_ = bf16[352,384]{1,0:T(8,128)(2,1)S(1)} collective-permute-done((bf16[352,384]{1,0:T(8,128)(2,1)S(1)}, bf16[352,384]{1,0:T(8,128)(2,1)S(1)}, u32[]{:S(2)}, u32[]{:S(2)}) %collective-permute-start.21) | collective-permute-done | bytes 270368 | tf_op jit(solution)/shard_map/ppermute | solution.py:1245
  117.7 1.3 collective-permute-done.20.refs_6_
  119.0 4.5 %shard_map.151 = (bf16[416,384]{1,0:T(8,128)(2,1)S(1)}, bf16[224,384]{1,0:T(8,128)(2,1)S(1)}, bf16[1,2,160,384]{3,2,1,0:T(8,128)(2,1)S(1)}, bf16[256,768]{1,0:T(8,128)(2,1)S(1)}) custom-call(s32[1,5]{1,0:T(1,128)S(1)} %copy-done.24, bf16[2,352,384]{2,1,0:T(8,128)(2,1)S(1)} %copy-done.3, bf16[1216,384]{1,0:T(8,128)(2,1)S(1)} %collective-permute-done.14.refs_6_.refs_2_, ...), custom_call_target="tpu_custom_call" | custom-call | tf_op jit(solution)/shard_map/pallas_call | solution.py:475
  124.0 0.5 collective-permute-start.24
  124.5 1.5 %collective-permute-start.25 = (bf16[256,768]{1,0:T(8,128)(2,1)S(1)}, bf16[256,768]{1,0:T(8,128)(2,1)S(1)}, u32[]{:S(2)}, u32[]{:S(2)}) collective-permute-start(bf16[256,768]{1,0:T(8,128)(2,1)S(1)} %get-tuple-element.189), channel_id=1, source_target_pairs={{0,2},{1,3},{2,0},{3,1},{4,6},{5,7},{6,4},{7,5},{8,10},{9,11},{10,... | collective-permute-start | bytes 1179656 | tf_op jit(solution)/shard_map/ppermute | solution.py:1245
  126.1 2.6 %collective-permute-start.26 = (bf16[224,384]{1,0:T(8,128)(2,1)S(1)}, bf16[224,384]{1,0:T(8,128)(2,1)S(1)}, u32[]{:S(2)}, u32[]{:S(2)}) collective-permute-start(bf16[224,384]{1,0:T(8,128)(2,1)S(1)} %get-tuple-element.197), channel_id=1, source_target_pairs={{0,16},{4,20},{8,24},{12,28},{16,0},{20,4},{24,8},{28,12},{1,17},{... | collective-permute-start | bytes 516104 | tf_op jit(solution)/shard_map/ppermute | solution.py:1245
  128.6 3.7 %shard_map.152 = (bf16[224,384]{1,0:T(8,128)(2,1)S(1)}, bf16[416,384]{1,0:T(8,128)(2,1)S(1)}, bf16[1,2,160,384]{3,2,1,0:T(8,128)(2,1)S(1)}) custom-call(s32[1,5]{1,0:T(1,128)S(1)} %copy-done.24, bf16[2,352,384]{2,1,0:T(8,128)(2,1)S(1)} %copy-done.3, bf16[1216,384]{1,0:T(8,128)(2,1)S(1)} %collective-permute-done.14.refs_6_.refs_2_, ...), custom_call_target="tpu_custom_call" | custom-call | tf_op jit(solution)/shard_map/pallas_call | solution.py:475
  132.3 0.6 collective-permute-done.24.refs_5_
  132.9 3.0 %collective-permute-done.23.refs_3_ = bf16[416,384]{1,0:T(8,128)(2,1)S(1)} collective-permute-done((bf16[416,384]{1,0:T(8,128)(2,1)S(1)}, bf16[416,384]{1,0:T(8,128)(2,1)S(1)}, u32[]{:S(2)}, u32[]{:S(2)}) %collective-permute-start.23) | collective-permute-done | bytes 319520 | tf_op jit(solution)/shard_map/ppermute | solution.py:1245
  135.9 2.4 %shard_map.153 = (bf16[224,384]{1,0:T(8,128)(2,1)S(1)}, bf16[160,384]{1,0:T(8,128)(2,1)S(1)}, bf16[224,384]{1,0:T(8,128)(2,1)S(1)}, bf16[160,384]{1,0:T(8,128)(2,1)S(1)}) custom-call(s32[1,5]{1,0:T(1,128)S(1)} %copy-done.24, s32[96]{0:T(128)S(1)} %copy-done.28, bf16[416,384]{1,0:T(8,128)(2,1)S(1)} %get-tuple-element.185.refs_2_, ...), custom_call_target="tpu_custom_call" | custom-call | tf_op jit(solution)/shard_map/pallas_call | solution.py:475
  138.3 0.8 collective-permute-start.28
  139.1 1.3 collective-permute-start.27
  140.4 3.5 %shard_map.154 = (bf16[256,768]{1,0:T(8,128)(2,1)}, bf16[256,768]{1,0:T(8,128)(2,1)}) custom-call(s32[1,5]{1,0:T(1,128)S(1)} %copy-done.24, bf16[256,768]{1,0:T(8,128)(2,1)S(1)} %get-tuple-element.146.refs_1_, bf16[768,768]{1,0:T(8,128)(2,1)S(1)} %collective-permute-done.22.refs_16_.refs_2_, bf16[256,768]{1,0:T(8,128)(2,1)S(1)} %collective-permute-done.25.refs_3_, ...), custom_call_target="tpu_custom_call" | custom-call | tf_op jit(solution)/shard_map/pallas_call | solution.py:475
  144.0 2.8 %collective-permute-done.28.refs_6_ = bf16[224,384]{1,0:T(8,128)(2,1)S(1)} collective-permute-done((bf16[224,384]{1,0:T(8,128)(2,1)S(1)}, bf16[224,384]{1,0:T(8,128)(2,1)S(1)}, u32[]{:S(2)}, u32[]{:S(2)}) %collective-permute-start.28) | collective-permute-done | bytes 172064 | tf_op jit(solution)/shard_map/ppermute | solution.py:1245
  146.8 3.0 %shard_map.155 = (f32[96,768]{1,0:T(8,128)}, f32[192,384]{1,0:T(8,128)}, f32[192,96]{1,0:T(8,128)}, f32[1,336]{1,0:T(1,128)S(1)}, f32[192,288]{1,0:T(8,128)}) custom-call(s32[1,5]{1,0:T(1,128)S(1)} %copy-done.24, bf16[224,384]{1,0:T(8,128)(2,1)S(1)} %get-tuple-element.196.refs_1_, bf16[224,384]{1,0:T(8,128)(2,1)S(1)} %collective-permute-done.26.refs_2_, ...), custom_call_target="tpu_custom_call" | custom-call | tf_op jit(solution)/shard_map/pallas_call | solution.py:475
  149.8 0.6 reduce
  (93 shorter events, 3.5 us)
Async XLA Ops:
  0.6 3.5 %collective-permute-start.1 = (bf16[256,768]{1,0:T(8,128)(2,1)}, bf16[256,768]{1,0:T(8,128)(2,1)S(1)}, u32[]{:S(2)}, u32[]{:S(2)}) collective-permute-start(bf16[256,768]{1,0:T(8,128)(2,1)} %bitcast.10), channel_id=1, source_target_pairs={{0,1},{1,0},{2,3},{3,2},{4,5},{5,4},{6,7},{7,6},{8,9},{9,8},{10,11... | collective-permute-start | bytes 1179656 | tf_op jit(solution)/shard_map/ppermute | solution.py:1245
  1.1 3.0 %collective-permute-start.2 = (bf16[256,768]{1,0:T(8,128)(2,1)}, bf16[256,768]{1,0:T(8,128)(2,1)S(1)}, u32[]{:S(2)}, u32[]{:S(2)}) collective-permute-start(bf16[256,768]{1,0:T(8,128)(2,1)} %bitcast.6), channel_id=1, source_target_pairs={{0,1},{1,0},{2,3},{3,2},{4,5},{5,4},{6,7},{7,6},{8,9},{9,8},{10,11... | collective-permute-start | bytes 1179656 | tf_op jit(solution)/shard_map/ppermute | solution.py:1245
  1.2 13.0 %collective-permute-start = (bf16[256,768]{1,0:T(8,128)(2,1)}, bf16[256,768]{1,0:T(8,128)(2,1)S(1)}, u32[]{:S(2)}, u32[]{:S(2)}) collective-permute-start(bf16[256,768]{1,0:T(8,128)(2,1)} %bitcast.11), channel_id=1, source_target_pairs={{0,2},{1,3},{2,0},{3,1},{4,6},{5,7},{6,4},{7,5},{8,10},{9,11},{10,... | collective-permute-start | bytes 1179656 | tf_op jit(solution)/shard_map/ppermute | solution.py:1245
  14.3 1.8 %collective-permute-start.3 = (bf16[256,768]{1,0:T(8,128)(2,1)S(1)}, bf16[256,768]{1,0:T(8,128)(2,1)S(1)}, u32[]{:S(2)}, u32[]{:S(2)}) collective-permute-start(bf16[256,768]{1,0:T(8,128)(2,1)S(1)} %collective-permute-done.refs_1_), channel_id=1, source_target_pairs={{0,1},{1,0},{2,3},{3,2},{4,5},{5,4},{6,7},{7,6},{8,9},{9,8},{10,11... | collective-permute-start | bytes 1179656 | tf_op jit(solution)/shard_map/ppermute | solution.py:1245
  25.7 2.0 %collective-permute-start.4 = (bf16[512,384]{1,0:T(8,128)(2,1)}, bf16[512,384]{1,0:T(8,128)(2,1)S(1)}, u32[]{:S(2)}, u32[]{:S(2)}) collective-permute-start(bf16[512,384]{1,0:T(8,128)(2,1)} %get-tuple-element.112.refs_1_.refs_9_), channel_id=1, source_target_pairs={{0,1},{1,0},{2,3},{3,2},{4,5},{5,4},{6,7},{7,6},{8,9},{9,8},{10,11... | collective-permute-start | bytes 1179656 | tf_op jit(solution)/shard_map/ppermute | solution.py:1245
  45.3 5.8 %collective-permute-start.5 = (bf16[512,768]{1,0:T(8,128)(2,1)}, bf16[512,768]{1,0:T(8,128)(2,1)}, u32[]{:S(2)}, u32[]{:S(2)}) collective-permute-start(bf16[512,768]{1,0:T(8,128)(2,1)} %get-tuple-element.115.refs_2_), channel_id=1, source_target_pairs={{0,1},{1,0},{2,3},{3,2},{4,5},{5,4},{6,7},{7,6},{8,9},{9,8},{10,11... | collective-permute-start | bytes 2359304 | tf_op jit(solution)/shard_map/ppermute | solution.py:1245
  45.5 22.9 %collective-permute-start.6 = (bf16[2,512,384]{2,1,0:T(8,128)(2,1)}, bf16[2,512,384]{2,1,0:T(8,128)(2,1)S(1)}, u32[]{:S(2)}, u32[]{:S(2)}) collective-permute-start(bf16[2,512,384]{2,1,0:T(8,128)(2,1)} %get-tuple-element.129), channel_id=1, source_target_pairs={{0,4},{4,0},{8,12},{12,8},{16,20},{20,16},{24,28},{28,24},{1,5},{5... | collective-permute-start | bytes 2359304 | tf_op jit(solution)/shard_map/ppermute | solution.py:1245
  47.3 2.2 %collective-permute-start.7 = (bf16[2,2,192,384]{3,2,1,0:T(8,128)(2,1)}, bf16[2,2,192,384]{3,2,1,0:T(8,128)(2,1)S(1)}, u32[]{:S(2)}, u32[]{:S(2)}) collective-permute-start(bf16[2,2,192,384]{3,2,1,0:T(8,128)(2,1)} %get-tuple-element.130), channel_id=1, source_target_pairs={{0,1},{1,0},{2,3},{3,2},{4,5},{5,4},{6,7},{7,6},{8,9},{9,8},{10,11... | collective-permute-start | bytes 1769480 | tf_op jit(solution)/shard_map/ppermute | solution.py:1245
  47.4 24.3 %collective-permute-start.9 = (bf16[2,2,2,160,384]{4,3,2,1,0:T(8,128)(2,1)}, bf16[2,2,2,160,384]{4,3,2,1,0:T(8,128)(2,1)S(1)}, u32[]{:S(2)}, u32[]{:S(2)}) collective-permute-start(bf16[2,2,2,160,384]{4,3,2,1,0:T(8,128)(2,1)} %get-tuple-element.131), channel_id=1, source_target_pairs={{0,8},{4,12},{8,0},{12,4},{16,24},{20,28},{24,16},{28,20},{1,9},{5... | collective-permute-start | bytes 2949128 | tf_op jit(solution)/shard_map/ppermute | solution.py:1245
  49.6 22.2 %collective-permute-start.8 = (bf16[2,2,192,384]{3,2,1,0:T(8,128)(2,1)S(1)}, bf16[2,2,192,384]{3,2,1,0:T(8,128)(2,1)S(1)}, u32[]{:S(2)}, u32[]{:S(2)}) collective-permute-start(bf16[2,2,192,384]{3,2,1,0:T(8,128)(2,1)S(1)} %collective-permute-done.7), channel_id=1, source_target_pairs={{0,2},{1,3},{2,0},{3,1},{4,6},{5,7},{6,4},{7,5},{8,10},{9,11},{10,... | collective-permute-start | bytes 1769480 | tf_op jit(solution)/shard_map/ppermute | solution.py:1245
  51.1 20.7 %collective-permute-start.12 = (bf16[2,2,192,384]{3,2,1,0:T(8,128)(2,1)}, bf16[2,2,192,384]{3,2,1,0:T(8,128)(2,1)S(1)}, u32[]{:S(2)}, u32[]{:S(2)}) collective-permute-start(bf16[2,2,192,384]{3,2,1,0:T(8,128)(2,1)} %get-tuple-element.138), channel_id=1, source_target_pairs={{0,1},{1,0},{2,3},{3,2},{4,5},{5,4},{6,7},{7,6},{8,9},{9,8},{10,11... | collective-permute-start | bytes 1769480 | tf_op jit(solution)/shard_map/ppermute | solution.py:1245
  67.9 3.9 %collective-permute-start.10 = (bf16[2,6,48,384]{3,2,1,0:T(8,128)(2,1)}, bf16[2,6,48,384]{3,2,1,0:T(8,128)(2,1)S(1)}, u32[]{:S(2)}, u32[]{:S(2)}) collective-permute-start(bf16[2,6,48,384]{3,2,1,0:T(8,128)(2,1)} %get-tuple-element.132), channel_id=1, source_target_pairs={{0,1},{1,0},{2,3},{3,2},{4,5},{5,4},{6,7},{7,6},{8,9},{9,8},{10,11... | collective-permute-start | bytes 1327112 | tf_op jit(solution)/shard_map/ppermute | solution.py:1245
  68.4 3.3 %collective-permute-start.11 = (bf16[2,6,48,384]{3,2,1,0:T(8,128)(2,1)}, bf16[2,6,48,384]{3,2,1,0:T(8,128)(2,1)S(1)}, u32[]{:S(2)}, u32[]{:S(2)}) collective-permute-start(bf16[2,6,48,384]{3,2,1,0:T(8,128)(2,1)} %get-tuple-element.133), channel_id=1, source_target_pairs={{0,1},{1,0},{2,3},{3,2},{4,5},{5,4},{6,7},{7,6},{8,9},{9,8},{10,11... | collective-permute-start | bytes 1327112 | tf_op jit(solution)/shard_map/ppermute | solution.py:1245
  73.3 9.0 %copy-start.4 = (bf16[1,256,768]{2,1,0:T(8,128)(2,1)S(1)}, bf16[1,256,768]{2,1,0:T(8,128)(2,1)}, u32[]{:S(2)}) copy-start(bf16[1,256,768]{2,1,0:T(8,128)(2,1)} %param.16) | copy-start | bytes 1179652
  73.3 9.0 %copy-start.6 = (bf16[256,768]{1,0:T(8,128)(2,1)S(1)}, bf16[256,768]{1,0:T(8,128)(2,1)}, u32[]{:S(2)}) copy-start(bf16[256,768]{1,0:T(8,128)(2,1)} %copy-done.5) | copy-start | bytes 1179652
  73.3 9.0 %copy-start.9 = (bf16[512,768]{1,0:T(8,128)(2,1)S(1)}, bf16[512,768]{1,0:T(8,128)(2,1)}, u32[]{:S(2)}) copy-start(bf16[512,768]{1,0:T(8,128)(2,1)} %get-tuple-element.121.refs_16_.refs_5_) | copy-start | bytes 2359300
  73.3 9.0 %copy-start.18 = (f32[10752]{0:T(1024)S(1)}, f32[10752]{0:T(1024)}, u32[]{:S(2)}) copy-start(f32[10752]{0:T(1024)} %param.15) | copy-start | bytes 129028
  73.3 9.0 %copy-start.24 = (s32[1,5]{1,0:T(1,128)S(1)}, s32[1,5]{1,0:T(1,128)}, u32[]{:S(2)}) copy-start(s32[1,5]{1,0:T(1,128)} %refs_0_.23) | copy-start | bytes 64
  73.3 9.0 %copy-start.25 = (f32[8,768]{1,0:T(8,128)S(1)}, f32[8,768]{1,0:T(8,128)}, u32[]{:S(2)}) copy-start(f32[8,768]{1,0:T(8,128)} %get-tuple-element.143.refs_12_) | copy-start | bytes 73732
  73.3 9.0 %copy-start.26 = (f32[1,1536]{1,0:T(1,128)S(1)}, f32[1,1536]{1,0:T(1,128)}, u32[]{:S(2)}) copy-start(f32[1,1536]{1,0:T(1,128)} %get-tuple-element.145.refs_14_) | copy-start | bytes 18436
  73.3 9.0 %copy-start.27 = (f32[1,768]{1,0:T(1,128)S(1)}, f32[1,768]{1,0:T(1,128)}, u32[]{:S(2)}) copy-start(f32[1,768]{1,0:T(1,128)} %get-tuple-element.144.refs_13_) | copy-start | bytes 9220
  77.7 26.1 %collective-permute-start.14 = (bf16[1216,384]{1,0:T(8,128)(2,1)}, bf16[1216,384]{1,0:T(8,128)(2,1)S(1)}, u32[]{:S(2)}, u32[]{:S(2)}) collective-permute-start(bf16[1216,384]{1,0:T(8,128)(2,1)} %get-tuple-element.148), channel_id=1, source_target_pairs={{0,2},{1,3},{2,0},{3,1},{4,6},{5,7},{6,4},{7,5},{8,10},{9,11},{10,... | collective-permute-start | bytes 2801672 | tf_op jit(solution)/shard_map/ppermute | solution.py:1245
  79.2 24.5 %collective-permute-start.15 = (bf16[1216,384]{1,0:T(8,128)(2,1)}, bf16[1216,384]{1,0:T(8,128)(2,1)S(1)}, u32[]{:S(2)}, u32[]{:S(2)}) collective-permute-start(bf16[1216,384]{1,0:T(8,128)(2,1)} %get-tuple-element.142), channel_id=1, source_target_pairs={{0,4},{4,0},{8,12},{12,8},{16,20},{20,16},{24,28},{28,24},{1,5},{5... | collective-permute-start | bytes 2801672 | tf_op jit(solution)/shard_map/ppermute | solution.py:1245
  79.7 24.0 %collective-permute-start.13 = (bf16[2,2,160,384]{3,2,1,0:T(8,128)(2,1)}, bf16[2,2,160,384]{3,2,1,0:T(8,128)(2,1)S(1)}, u32[]{:S(2)}, u32[]{:S(2)}) collective-permute-start(bf16[2,2,160,384]{3,2,1,0:T(8,128)(2,1)} %get-tuple-element.147), channel_id=1, source_target_pairs={{0,16},{4,20},{8,24},{12,28},{16,0},{20,4},{24,8},{28,12},{1,17},{... | collective-permute-start | bytes 1474568 | tf_op jit(solution)/shard_map/ppermute | solution.py:1245
  86.8 17.0 %copy-start.3 = (bf16[2,352,384]{2,1,0:T(8,128)(2,1)S(1)}, bf16[2,352,384]{2,1,0:T(8,128)(2,1)}, u32[]{:S(2)}) copy-start(bf16[2,352,384]{2,1,0:T(8,128)(2,1)} %get-tuple-element.171.refs_13_.refs_1_) | copy-start | bytes 1622020
  86.8 17.0 %copy-start.8 = (bf16[2,512,384]{2,1,0:T(8,128)(2,1)S(1)}, bf16[2,512,384]{2,1,0:T(8,128)(2,1)}, u32[]{:S(2)}) copy-start(bf16[2,512,384]{2,1,0:T(8,128)(2,1)} %get-tuple-element.135.refs_3_.refs_4_) | copy-start | bytes 2359300
  86.8 17.0 %copy-start.11 = (bf16[2,512,384]{2,1,0:T(8,128)(2,1)S(1)}, bf16[2,512,384]{2,1,0:T(8,128)(2,1)}, u32[]{:S(2)}) copy-start(bf16[2,512,384]{2,1,0:T(8,128)(2,1)} %copy-done.10) | copy-start | bytes 2359300
  86.8 17.0 %copy-start.14 = (bf16[2,2,192,384]{3,2,1,0:T(8,128)(2,1)S(1)}, bf16[2,2,192,384]{3,2,1,0:T(8,128)(2,1)}, u32[]{:S(2)}) copy-start(bf16[2,2,192,384]{3,2,1,0:T(8,128)(2,1)} %copy-done.13) | copy-start | bytes 1769476
  86.8 17.0 %copy-start.16 = (bf16[2,2,192,384]{3,2,1,0:T(8,128)(2,1)S(1)}, bf16[2,2,192,384]{3,2,1,0:T(8,128)(2,1)}, u32[]{:S(2)}) copy-start(bf16[2,2,192,384]{3,2,1,0:T(8,128)(2,1)} %copy-done.15) | copy-start | bytes 1769476
  86.8 17.0 %copy-start.17 = (bf16[2,128,384]{2,1,0:T(8,128)(2,1)S(1)}, bf16[2,128,384]{2,1,0:T(8,128)(2,1)}, u32[]{:S(2)}) copy-start(bf16[2,128,384]{2,1,0:T(8,128)(2,1)} %get-tuple-element.177.refs_8_.refs_7_) | copy-start | bytes 589828
  95.4 7.1 %collective-permute-start.17 = (f32[16,768]{1,0:T(8,128)S(1)}, f32[16,768]{1,0:T(8,128)S(1)}, u32[]{:S(2)}, u32[]{:S(2)}) collective-permute-start(f32[16,768]{1,0:T(8,128)S(1)} %get-tuple-element.149.refs_9_), channel_id=1, source_target_pairs={{0,4},{4,0},{8,12},{12,8},{16,20},{20,16},{24,28},{28,24},{1,5},{5... | collective-permute-start | bytes 147464 | tf_op jit(solution)/shard_map/ppermute | solution.py:1245
  97.0 5.5 %collective-permute-start.16 = (f32[16,768]{1,0:T(8,128)S(1)}, f32[16,768]{1,0:T(8,128)S(1)}, u32[]{:S(2)}, u32[]{:S(2)}) collective-permute-start(f32[16,768]{1,0:T(8,128)S(1)} %get-tuple-element.149.refs_9_), channel_id=1, source_target_pairs={{0,1},{1,0},{2,3},{3,2},{4,5},{5,4},{6,7},{7,6},{8,9},{9,8},{10,11... | collective-permute-start | bytes 147464 | tf_op jit(solution)/shard_map/ppermute | solution.py:1245
  102.5 1.2 collective-permute-start.18
  103.8 15.2 %copy-start = (bf16[2,2,2,160,384]{4,3,2,1,0:T(8,128)(2,1)S(1)}, bf16[2,2,2,160,384]{4,3,2,1,0:T(8,128)(2,1)}, u32[]{:S(2)}) copy-start(bf16[2,2,2,160,384]{4,3,2,1,0:T(8,128)(2,1)} %get-tuple-element.182.refs_1_.refs_12_) | copy-start | bytes 2949124
  103.8 15.2 %copy-start.2 = (bf16[2,2,2,160,384]{4,3,2,1,0:T(8,128)(2,1)S(1)}, bf16[2,2,2,160,384]{4,3,2,1,0:T(8,128)(2,1)}, u32[]{:S(2)}) copy-start(bf16[2,2,2,160,384]{4,3,2,1,0:T(8,128)(2,1)} %copy-done.1) | copy-start | bytes 2949124
  107.1 11.8 %collective-permute-start.22 = (bf16[768,768]{1,0:T(8,128)(2,1)S(1)}, bf16[768,768]{1,0:T(8,128)(2,1)S(1)}, u32[]{:S(2)}, u32[]{:S(2)}) collective-permute-start(bf16[768,768]{1,0:T(8,128)(2,1)S(1)} %copy-done.34), channel_id=1, source_target_pairs={{0,1},{1,0},{2,3},{3,2},{4,5},{5,4},{6,7},{7,6},{8,9},{9,8},{10,11... | collective-permute-start | bytes 3538952 | tf_op jit(solution)/shard_map/ppermute | solution.py:1245
  107.4 10.3 %collective-permute-start.19 = (bf16[2,224,384]{2,1,0:T(8,128)(2,1)S(1)}, bf16[2,224,384]{2,1,0:T(8,128)(2,1)S(1)}, u32[]{:S(2)}, u32[]{:S(2)}) collective-permute-start(bf16[2,224,384]{2,1,0:T(8,128)(2,1)S(1)} %get-tuple-element.158), channel_id=1, source_target_pairs={{0,8},{4,12},{8,0},{12,4},{16,24},{20,28},{24,16},{28,20},{1,9},{5... | collective-permute-start | bytes 1032200 | tf_op jit(solution)/shard_map/ppermute | solution.py:1245
  108.9 10.0 %collective-permute-start.20 = (bf16[448,384]{1,0:T(8,128)(2,1)S(1)}, bf16[448,384]{1,0:T(8,128)(2,1)S(1)}, u32[]{:S(2)}, u32[]{:S(2)}) collective-permute-start(bf16[448,384]{1,0:T(8,128)(2,1)S(1)} %get-tuple-element.179.refs_9_), channel_id=1, source_target_pairs={{0,2},{1,3},{2,0},{3,1},{4,6},{5,7},{6,4},{7,5},{8,10},{9,11},{10,... | collective-permute-start | bytes 1032200 | tf_op jit(solution)/shard_map/ppermute | solution.py:1245
  109.5 8.2 %collective-permute-start.21 = (bf16[352,384]{1,0:T(8,128)(2,1)S(1)}, bf16[352,384]{1,0:T(8,128)(2,1)S(1)}, u32[]{:S(2)}, u32[]{:S(2)}) collective-permute-start(bf16[352,384]{1,0:T(8,128)(2,1)S(1)} %get-tuple-element.160), channel_id=1, source_target_pairs={{0,4},{4,0},{8,12},{12,8},{16,20},{20,16},{24,28},{28,24},{1,5},{5... | collective-permute-start | bytes 811016 | tf_op jit(solution)/shard_map/ppermute | solution.py:1245
  123.5 12.4 %collective-permute-start.23 = (bf16[416,384]{1,0:T(8,128)(2,1)S(1)}, bf16[416,384]{1,0:T(8,128)(2,1)S(1)}, u32[]{:S(2)}, u32[]{:S(2)}) collective-permute-start(bf16[416,384]{1,0:T(8,128)(2,1)S(1)} %get-tuple-element.170), channel_id=1, source_target_pairs={{0,8},{4,12},{8,0},{12,4},{16,24},{20,28},{24,16},{28,20},{1,9},{5... | collective-permute-start | bytes 958472 | tf_op jit(solution)/shard_map/ppermute | solution.py:1245
  124.0 8.9 %collective-permute-start.24 = (bf16[1,2,160,384]{3,2,1,0:T(8,128)(2,1)S(1)}, bf16[1,2,160,384]{3,2,1,0:T(8,128)(2,1)S(1)}, u32[]{:S(2)}, u32[]{:S(2)}) collective-permute-start(bf16[1,2,160,384]{3,2,1,0:T(8,128)(2,1)S(1)} %get-tuple-element.187), channel_id=1, source_target_pairs={{0,2},{1,3},{2,0},{3,1},{4,6},{5,7},{6,4},{7,5},{8,10},{9,11},{10,... | collective-permute-start | bytes 737288 | tf_op jit(solution)/shard_map/ppermute | solution.py:1245
  124.5 15.8 %collective-permute-start.25 = (bf16[256,768]{1,0:T(8,128)(2,1)S(1)}, bf16[256,768]{1,0:T(8,128)(2,1)S(1)}, u32[]{:S(2)}, u32[]{:S(2)}) collective-permute-start(bf16[256,768]{1,0:T(8,128)(2,1)S(1)} %get-tuple-element.189), channel_id=1, source_target_pairs={{0,2},{1,3},{2,0},{3,1},{4,6},{5,7},{6,4},{7,5},{8,10},{9,11},{10,... | collective-permute-start | bytes 1179656 | tf_op jit(solution)/shard_map/ppermute | solution.py:1245
  126.0 9.9 %copy-start.28 = (s32[96]{0:T(128)S(1)}, s32[96]{0:T(128)}, u32[]{:S(2)}) copy-start(s32[96]{0:T(128)} %constant.2.clone.refs_1_) | copy-start | bytes 1156
  126.0 14.3 %copy-start.7 = (bf16[1,256,768]{2,1,0:T(8,128)(2,1)S(1)}, bf16[1,256,768]{2,1,0:T(8,128)(2,1)}, u32[]{:S(2)}) copy-start(bf16[1,256,768]{2,1,0:T(8,128)(2,1)} %param.9) | copy-start | bytes 1179652
  126.1 17.9 %collective-permute-start.26 = (bf16[224,384]{1,0:T(8,128)(2,1)S(1)}, bf16[224,384]{1,0:T(8,128)(2,1)S(1)}, u32[]{:S(2)}, u32[]{:S(2)}) collective-permute-start(bf16[224,384]{1,0:T(8,128)(2,1)S(1)} %get-tuple-element.197), channel_id=1, source_target_pairs={{0,16},{4,20},{8,24},{12,28},{16,0},{20,4},{24,8},{28,12},{1,17},{... | collective-permute-start | bytes 516104 | tf_op jit(solution)/shard_map/ppermute | solution.py:1245
  128.6 11.8 %copy-start.22 = (f32[256,768]{1,0:T(8,128)S(1)}, f32[256,768]{1,0:T(8,128)}, u32[]{:S(2)}) copy-start(f32[256,768]{1,0:T(8,128)} %get-tuple-element.191.refs_5_) | copy-start | bytes 2359300
  138.3 8.5 %collective-permute-start.28 = (bf16[224,384]{1,0:T(8,128)(2,1)S(1)}, bf16[224,384]{1,0:T(8,128)(2,1)S(1)}, u32[]{:S(2)}, u32[]{:S(2)}) collective-permute-start(bf16[224,384]{1,0:T(8,128)(2,1)S(1)} %get-tuple-element.199), channel_id=1, source_target_pairs={{0,16},{4,20},{8,24},{12,28},{16,0},{20,4},{24,8},{28,12},{1,17},{... | collective-permute-start | bytes 516104 | tf_op jit(solution)/shard_map/ppermute | solution.py:1245
  139.1 4.9 %collective-permute-start.27 = (bf16[160,384]{1,0:T(8,128)(2,1)S(1)}, bf16[160,384]{1,0:T(8,128)(2,1)S(1)}, u32[]{:S(2)}, u32[]{:S(2)}) collective-permute-start(bf16[160,384]{1,0:T(8,128)(2,1)S(1)} %get-tuple-element.198), channel_id=1, source_target_pairs={{0,4},{4,0},{8,12},{12,8},{16,20},{20,16},{24,28},{28,24},{1,5},{5... | collective-permute-start | bytes 368648 | tf_op jit(solution)/shard_map/ppermute | solution.py:1245
  (16 other events, 30.1 us)
